TPU v7x, 32 devices: a whole 2x2x4 slice. The times are simulated.
32 devices in a mesh: py: 4 (over z), pz: 8 (over y, x, core).
Axes of the slice: x: 2, y: 2, z: 4, core: 2. Of those that a mesh axis runs over, the one named last changes fastest.
Arguments:
- conserved: float32 [5, 512, 256, 128], P(None, 'pz', 'py'), may hold values from -2 to 3.5, as said below
- register: float32 [5, 512, 256, 128], P(None, 'pz', 'py'), may hold values from -6 to 6
- stream_blocks: float32 [1, 3, 128, 128], replicated, may hold values from -0.3125 to 0.3125
- wall_matrix: float32 [256, 256], replicated, may hold values from -0.375 to 0.375
- span_blocks: float32 [16, 3, 32, 32], replicated, may hold values from -0.625 to 0.625
- inflow_gain: float32 [5], replicated, may hold values from 0.5 to 2
- source_block: int32 [32, 4096, 1], replicated, may hold values from 0 to 31; in each aligned block of 4096 rows (0 to 4095, 4096 to 8191, ..., all dimensions but the last counted through in order) at most 256 rows name the same one
- source_column: int32 [32, 4096], replicated, may hold values from 0 to 4095
Outputs:
- new_conserved: float32 [5, 512, 256, 128], P(None, 'pz', 'py')
- new_register: float32 [5, 512, 256, 128], P(None, 'pz', 'py')
Inputs may be any that keep to these rules, and one draw needn't show every extreme that they name: Among the 4096 entries of one column block, source_block[b, :, 0], no value appears more than 256 times, and in some column block one value appears exactly 256 times. `conserved`: the first field, the density, lies between 0.5 and 2.
All inputs are finite; a program needn't handle non-finite values.
Results may differ from a plain program's by a relative error of at most 0.0001.
Values sent between devices are 32-bit elements; how exact they have to be, the bound alone decides.
No kernel may reach another device: no remote copies, remote signals or barrier semaphores. Data moves between devices by JAX's collectives and lax.ppermute only.
A program may use at most 192 MiB of HBM per device.

v0:
```python
import jax
import jax.numpy as jnp
from jax import lax
from jax.sharding import PartitionSpec as P

highest = lax.Precision.HIGHEST
section_decay = -5.0 / 9.0
section_gain = 15.0 / 16.0
time_step = 0.1


def padded(cells, sides, width):
    for axis, dim in sides:
        count = lax.axis_size(axis)
        head = lax.slice_in_dim(cells, 0, width, axis=dim)
        tail = lax.slice_in_dim(cells, cells.shape[dim] - width, cells.shape[dim], axis=dim)
        cells = jnp.concatenate(
            [
                lax.ppermute(tail, axis, [(i, (i + 1) % count) for i in range(count)]),
                cells,
                lax.ppermute(head, axis, [((i + 1) % count, i) for i in range(count)]),
            ],
            axis=dim,
        )
    return cells


def flux_set(values, direction):
    speeds = values[1:4] / values[0]
    pressure = 0.4 * (
        values[4] - 0.5 * (values[1] * speeds[0] + values[2] * speeds[1] + values[3] * speeds[2])
    )
    velocity = speeds[direction]
    pieces = [values[1 + direction]]
    for component in range(1, 4):
        moment = values[component] * velocity
        if component - 1 == direction:
            moment = moment + pressure
        pieces.append(moment)
    pieces.append((values[4] + pressure) * velocity)
    return jnp.stack(pieces)


def stream_derivative(values, blocks):
    leading = values.shape[:-1]
    block_count = blocks.shape[0]
    block_width = blocks.shape[2]
    shaped = values.reshape(leading + (block_count, block_width))
    summed = jnp.einsum("kab,...kb->...ka", blocks[:, 1], shaped, precision=highest)
    if block_count > 1:
        lower = jnp.einsum(
            "kab,...kb->...ka", blocks[1:, 0], shaped[..., :-1, :], precision=highest
        )
        upper = jnp.einsum(
            "kab,...kb->...ka", blocks[:-1, 2], shaped[..., 1:, :], precision=highest
        )
        zero_block = jnp.zeros(leading + (1, block_width), jnp.float32)
        summed = (
            summed
            + jnp.concatenate([zero_block, lower], axis=-2)
            + jnp.concatenate([upper, zero_block], axis=-2)
        )
    return summed.reshape(values.shape)


def wall_derivative(values, matrix):
    return jnp.einsum("ab,fzbx->fzax", matrix, values, precision=highest)


def local(
    conserved,
    register,
    stream_blocks,
    wall_matrix,
    span_blocks,
    inflow_gain,
    source_block,
    source_column,
):
    field_count, span_local, wall_local, stream_cells = conserved.shape
    column_count = span_local * wall_local
    recycle_index = 3 * stream_cells // 4
    recycle = conserved[:, :, :, recycle_index].reshape(field_count, column_count)
    myself = lax.axis_index(("py", "pz"))
    own_anchor = lax.dynamic_index_in_dim(source_block[:, :, 0], myself, 0, keepdims=False)
    own_column = lax.dynamic_index_in_dim(source_column, myself, 0, keepdims=False)
    whole_plane = lax.all_gather(recycle, ("py", "pz"), axis=1, tiled=True)
    fetched = jnp.take(whole_plane, own_anchor * column_count + own_column, axis=1)
    inlet_plane = (fetched * inflow_gain[:, None]).reshape(field_count, span_local, wall_local)
    current = conserved.at[:, :, :, 0].set(inlet_plane)
    stream_term = stream_derivative(flux_set(current, 0), stream_blocks)
    by_rows = lax.all_to_all(current, "py", split_axis=1, concat_axis=2, tiled=True)
    wall_term = wall_derivative(flux_set(by_rows, 1), wall_matrix)
    returned = lax.all_to_all(wall_term, "py", split_axis=2, concat_axis=1, tiled=True)
    block_width = span_blocks.shape[2]
    local_blocks = span_local // block_width
    start = lax.axis_index("pz") * local_blocks
    own_blocks = lax.dynamic_slice_in_dim(span_blocks, start, local_blocks, 0)
    flux_span = flux_set(current, 2)
    widened = padded(flux_span, (("pz", 1),), block_width)
    span_term = jnp.zeros(
        (field_count, local_blocks, block_width, wall_local, stream_cells), jnp.float32
    )
    for offset in range(3):
        window = widened[:, offset * block_width : offset * block_width + span_local]
        window = window.reshape(field_count, local_blocks, block_width, wall_local, stream_cells)
        span_term = span_term + jnp.einsum(
            "kab,fkbyx->fkayx", own_blocks[:, offset], window, precision=highest
        )
    side_term = span_term.reshape(current.shape)
    combined = stream_term + returned + side_term
    new_register = section_decay * register - time_step * combined
    new_conserved = current + section_gain * new_register
    return (new_conserved, new_register)


def solution(mesh):
    return jax.shard_map(
        local,
        mesh=mesh,
        in_specs=(
            P(None, "pz", "py", None),
            P(None, "pz", "py", None),
            P(),
            P(),
            P(),
            P(),
            P(),
            P(),
        ),
        out_specs=(P(None, "pz", "py", None), P(None, "pz", "py", None)),
        check_vma=False,
    )
```

profile of v0, /device:TPU:0, one launch (start us, length us, event | category | flops | bytes accessed | tf_op | source)
XLA Modules:
  0.0 1128.1 jit_solution(2301626190191934801)
XLA Ops:
  7.2 4.0 copy.152
  11.3 4.1 copy-done.1
  15.4 6.8 slice.145
  22.2 26.9 %copy.78 = f32[5,64,64,1]{0,2,1,3:T(8,128)} copy(f32[5,64,64,1]{3,2,1,0:T(8,128)} %slice.145) | data formatting | bytes 163840 | tf_op jit(solution)/shard_map/slice | solution.py:83
  52.0 356.3 %all-gather.2.cloned.1.call-done = f32[5,131072]{0,1:T(8,128)} async-done(((f32[5,4096]{0,1:T(8,128)}), f32[5,131072]{0,1:T(8,128)}) %all-gather.2.cloned.1.call-update) | async-done | bytes 2621456 | tf_op jit(solution)/shard_map/all_gather | solution.py:87
  408.3 40.4 %gather_fusion = f32[4096,5]{1,0:T(8,128)S(1)} fusion(f32[5,131072]{0,1:T(8,128)} %all-gather.2.cloned.1.call-done, s32[4096]{0:T(1024)S(1)} %broadcast_clamp_fusion), kind=kCustom, calls=%fused_computation | custom fusion | bytes 180224 | tf_op jit(solution)/shard_map/jit(_take)/gather | solution.py:88
  448.7 31.1 %copy.80 = f32[5,64,64,1]{3,2,1,0:T(8,128)} copy(f32[5,64,64,1]{0,2,1,3:T(8,128)S(1)} %bitcast.106) | data formatting | bytes 163840 | tf_op jit(solution)/shard_map/jit(_take)/gather | solution.py:88
  479.8 9.8 select_multiply_fusion
  489.6 26.4 %scatter.4 = f32[5,64,64,128]{3,2,1,0:T(8,128)} dynamic-update-slice(f32[5,64,64,128]{3,2,1,0:T(8,128)} %copy-done.1, f32[5,64,64,1]{3,2,1,0:T(8,128)} %select_multiply_fusion, s32[]{:T(128)} %constant.66.clone.1, s32[]{:T(128)} %constant.66.clone.1, s32[]{:T(128)} %constant.66.clone.1, s32[]{:T(128)} %constant.66.clone.1) | dynamic-update-slice | bytes 163844 | tf_op jit(solution)/shard_map/scatter | solution.py:90
  516.0 5.1 copy.81
  521.1 232.9 %all_to_all.33 = f32[5,64,64,128]{3,2,0,1:T(8,128)} all-to-all(f32[5,64,64,128]{3,2,0,1:T(8,128)S(1)} %copy.81), channel_id=1, replica_groups=mesh['py'=4,'pz'=8] {'py'}, dimensions={1} | all-to-all | bytes 20971520 | tf_op jit(solution)/shard_map/all_to_all | solution.py:92
  754.0 5.1 copy.82
  759.1 3.9 fusion.28
  763.0 3.2 slice.187
  771.3 3.2 copy.84
  776.4 6.5 copy.85
  783.0 6.5 copy.88
  789.5 3.2 copy.86
  792.7 3.0 copy.87
  795.7 3.2 copy.91
  798.9 2.9 copy.95
  801.8 3.2 copy.93
  805.0 2.9 copy.94
  807.9 4.5 broadcast_divide_fusion
  816.1 2.9 add_dynamic-update-slice_fusion
  822.3 13.6 %convolution_bitcast_fusion = f32[5,16,256,128]{2,3,1,0:T(8,128)} fusion(f32[5,16,256,128]{2,3,1,0:T(8,128)} %multiply_dynamic-update-slice_fusion, f32[256,256]{1,0:T(8,128)S(1)} %copy-done.11), kind=kOutput, calls=%fused_computation.12 | convolution fusion | flops 8053063680 | bytes 21233664 | tf_op jit(solution)/shard_map/ab,fzbx->fzax/dot_general | solution.py:67
  835.9 11.6 %copy.99 = f32[5,16,256,128]{3,1,0,2:T(8,128)} copy(f32[5,16,256,128]{2,3,1,0:T(8,128)} %convolution_bitcast_fusion) | data formatting | bytes 20971520 | tf_op jit(solution)/shard_map/ab,fzbx->fzax/transpose | solution.py:67
  847.5 6.4 all-to-all-start.1
  854.0 4.2 slice_dynamic-update-slice_fusion
  858.1 4.1 slice_divide_fusion
  862.2 3.8 add_dynamic-update-slice_fusion.1
  866.0 3.2 multiply_dynamic-update-slice_fusion.5
  869.2 3.1 constant_dynamic-update-slice_fusion.4
  872.3 2.4 constant_dynamic-update-slice_fusion.3
  874.7 2.7 constant_dynamic-update-slice_fusion.2
  877.4 3.6 constant_dynamic-update-slice_fusion.1
  881.0 10.3 fusion.29
  892.0 3.0 copy_dynamic-update-slice_fusion.4
  899.9 11.7 %fusion.20 = f32[2,5,64,128,32]{3,4,2,1,0:T(8,128)} fusion(f32[5,2,32,64,128]{4,2,3,0,1:T(8,128)S(1)} %copy_dynamic-update-slice_fusion, f32[16,3,32,32]{3,2,1,0:T(8,128)S(1)} %copy-done, s32[]{:T(128)S(6)} %select_n.40, s32[]{:T(128)S(6)} %add.145), kind=kOutput, calls=%fused_computation.63 | convolution fusion | flops 1006632960 | bytes 21004296 | tf_op jit(solution)/shard_map/kab,fkbyx->fkayx/dot_general | solution.py:107
  911.6 93.6 %collective-permute-done.1 = f32[5,32,64,128]{3,2,1,0:T(8,128)} collective-permute-done((f32[5,32,64,128]{3,2,1,0:T(8,128)}, f32[5,32,64,128]{3,2,1,0:T(8,128)}, u32[]{:S(2)}, u32[]{:S(2)}) %collective-permute-start.1) | collective-permute-done | bytes 5242912 | tf_op jit(solution)/shard_map/ppermute | solution.py:21
  1005.2 2.2 collective-permute-done
  1007.4 9.1 pad_maximum_fusion
  1016.5 16.5 %fusion.2 = f32[2,5,64,128,32]{3,4,2,1,0:T(8,128)} fusion(f32[5,2,32,64,128]{4,3,2,1,0:T(8,128)S(1)} %bitcast.92, f32[16,3,32,32]{3,2,1,0:T(8,128)S(1)} %copy-done, s32[]{:T(128)S(6)} %select_n.40), kind=kOutput, calls=%fused_computation.5 | convolution fusion | flops 1006632960 | bytes 21004292 | tf_op jit(solution)/shard_map/kab,fkbyx->fkayx/dot_general | solution.py:107
  1032.9 25.7 %add_bitcast_fusion = f32[5,2,32,64,128]{4,2,3,0,1:T(8,128)} fusion(f32[2,5,64,128,32]{3,4,2,1,0:T(8,128)} %fusion.2, f32[2,5,64,128,32]{3,4,2,1,0:T(8,128)} %fusion.20, f32[16,3,32,32]{3,2,1,0:T(8,128)S(1)} %copy-done, s32[]{:T(128)S(6)} %select_n.40, s32[]{:T(128)S(6)} %add.146, f32[5,2,32,64,128]{4,3,2,1,0:T(8,128)} %bitcast.93), kind=kOutput, calls=%fused_computation.9 | convolution fusion | flops 1011875840 | bytes 41975816 | tf_op jit(solution)/shard_map/kab,fkbyx->fkayx/dot_general | solution.py:107
  1058.6 14.6 %copy.110 = f32[5,2,32,64,128]{4,3,2,1,0:T(8,128)} copy(f32[5,2,32,64,128]{4,2,3,0,1:T(8,128)} %add_bitcast_fusion) | data formatting | bytes 20971520 | tf_op jit(solution)/shard_map/add | solution.py:107
  1073.2 8.5 all-to-all-done.1
  1081.7 11.5 %copy.101 = f32[5,4,16,64,128]{4,3,2,1,0:T(8,128)} copy(f32[5,4,16,64,128]{4,2,0,3,1:T(8,128)} %bitcast.24) | data formatting | bytes 20971520 | tf_op jit(solution)/shard_map/all_to_all | solution.py:94
  1093.2 27.9 %multiply_add_fusion = (f32[5,64,64,128]{3,2,1,0:T(8,128)}, f32[5,64,64,128]{3,2,1,0:T(8,128)}) fusion(f32[5,64,64,128]{3,2,1,0:T(8,128)} %scatter.4, f32[5,64,64,128]{3,2,1,0:T(8,128)} %bitcast.86, f32[5,64,64,128]{3,2,1,0:T(8,128)} %bitcast.87, f32[5,64,64,128]{3,2,1,0:T(8,128)} %get-tuple-element.26, f32[1,3,128,128]{3,2,1,0:T(8,128)} %param.12, ...), kind=kOutput, calls=%fused_computation.7 | convolution fusion | flops 4044881920 | bytes 73465856 | tf_op jit(solution)/shard_map/kab,...kb->...ka/dot_general | solution.py:49
  (61 shorter events, 22.4 us)
Async XLA Ops:
  7.2 892.7 %copy-start = (f32[16,3,32,32]{3,2,1,0:T(8,128)S(1)}, f32[16,3,32,32]{3,2,1,0:T(8,128)}, u32[]{:S(2)}) copy-start(f32[16,3,32,32]{3,2,1,0:T(8,128)} %param.14) | copy-start | bytes 589828
  7.2 401.1 %all-gather.2.cloned.1.call-start = ((), (), s32[]{:S(2)}) async-start(), calls=%async_computation.2 | async-start | bytes 69206016 | tf_op jit(solution)/shard_map/all_gather | solution.py:87
  11.3 4.1 copy-start.1
  448.6 31.1 %copy-start.12 = (f32[5]{0:T(128)S(1)}, f32[5]{0:T(128)}, u32[]{:S(2)}) copy-start(f32[5]{0:T(128)} %param.15) | copy-start | bytes 64
  769.6 4.9 copy-start.4
  812.4 2.0 copy-start.3
  812.5 3.0 copy-start.5
  812.5 3.6 copy-start.6
  818.9 3.3 copy-start.11
  847.5 234.2 %all-to-all-start.1 = ((f32[5,16,256,128]{3,1,0,2:T(8,128)}), f32[5,16,256,128]{3,1,0,2:T(8,128)}, u32[]{:S(2)}, u32[]{:S(2)}) async-start(f32[5,16,256,128]{3,1,0,2:T(8,128)} %copy.99), calls=%async_computation.1 | async-start | bytes 20971520 | tf_op jit(solution)/shard_map/all_to_all | solution.py:94
  853.9 8.3 slice-start
  853.9 8.3 slice-start.1
  858.1 4.1 slice-start.2
  872.3 2.4 copy-start.2
  881.0 14.0 %copy-start.7 = (f32[1,64,64,128]{3,2,1,0:T(8,128)S(1)}, f32[1,64,64,128]{3,2,1,0:T(8,128)}, u32[]{:S(2)}) copy-start(f32[1,64,64,128]{3,2,1,0:T(8,128)} %get-tuple-element.25) | copy-start | bytes 6291460
  891.3 113.9 %collective-permute-start.1 = (f32[5,32,64,128]{3,2,1,0:T(8,128)}, f32[5,32,64,128]{3,2,1,0:T(8,128)}, u32[]{:S(2)}, u32[]{:S(2)}) collective-permute-start(f32[5,32,64,128]{3,2,1,0:T(8,128)} %get-tuple-element.38), channel_id=1, source_target_pairs={{1,0},{2,1},{3,2},{4,3},{5,4},{6,5},{7,6},{0,7},{9,8},{10,9},{11,1... | collective-permute-start | bytes 15728648 | tf_op jit(solution)/shard_map/ppermute | solution.py:21
  891.7 115.6 %collective-permute-start = (f32[5,32,64,128]{3,2,1,0:T(8,128)}, f32[5,32,64,128]{3,2,1,0:T(8,128)}, u32[]{:S(2)}, u32[]{:S(2)}) collective-permute-start(f32[5,32,64,128]{3,2,1,0:T(8,128)} %get-tuple-element.39), channel_id=1, source_target_pairs={{0,1},{1,2},{2,3},{3,4},{4,5},{5,6},{6,7},{7,0},{8,9},{9,10},{10,1... | collective-permute-start | bytes 15728648 | tf_op jit(solution)/shard_map/ppermute | solution.py:19
  892.0 4.2 copy-start.10
  892.0 5.4 copy-start.9
  895.0 3.7 copy-start.8
  898.7 108.7 %slice-start.3 = ((s8[10485760]{0:T(1024)(128)(4,1)}), s8[4194304]{0:T(1024)(128)(4,1)S(1)}, s32[]{:S(2)}) async-start(s8[10485760]{0:T(1024)(128)(4,1)} %bitcast.90), calls=%async_computation.6 | async-start | bytes 8388608
  899.9 107.5 %slice-start.4 = ((s8[10485760]{0:T(1024)(128)(4,1)}), s8[4194304]{0:T(1024)(128)(4,1)S(1)}, s32[]{:S(2)}) async-start(s8[10485760]{0:T(1024)(128)(4,1)} %bitcast.90), calls=%async_computation.7 | async-start | bytes 8388608
  899.9 107.5 %slice-start.5 = ((s8[10485760]{0:T(1024)(128)(4,1)}), s8[2097152]{0:T(1024)(128)(4,1)S(1)}, s32[]{:S(2)}) async-start(s8[10485760]{0:T(1024)(128)(4,1)} %bitcast.90), calls=%async_computation.8 | async-start | bytes 4194304
Sparse Core Ops, SparseCore 0:
  49.3 358.9 all-gather.1
where the time goes:
time: 1130 us
  waiting for transfers between devices  461 us (41%)
  local copies, waits for them, and re-layouts  262 us (23%)
  blocking collectives  233 us (21%)
  matrix products  95.3 us (8%)
  other arithmetic  55.9 us (5%)
  between operations  14.6 us (1%)
    all_gather x1, waiting for transfers between devices, local(): whole_plane = lax.all_gather(recycle, ('py', 'pz'), axis=1, tiled=True)  356 us
    all_to_all x1, blocking collectives, local(): lax.all_to_all(current, 'py', split_axis=1, concat_axis=2, tiled=True)  233 us
    ppermute x1, waiting for transfers between devices, padded(): lax.ppermute(head, axis, [((i + 1) % count, i) for i in range(count)])  93.6 us
    gather x2, local copies, waits for them, and re-layouts, local(): jnp.take(whole_plane, own_anchor * column_count + own_column, axis=1)  71.5 us
    dot_general x3, matrix products, local(): jnp.einsum('kab,fkbyx->fkayx', own_blocks[:, offset], window, precision=h...  53.8 us
    slice x2, local copies, waits for them, and re-layouts, local(): conserved[:, :, :, recycle_index].reshape(field_count, column_count)  33.8 us
    scatter x2, local copies, waits for them, and re-layouts, local(): current = conserved.at[:, :, :, 0].set(inlet_plane)  31.4 us
    dot_general x1, matrix products, stream_derivative(): jnp.einsum('kab,...kb->...ka', blocks[:, 1], shaped, precision=highest)  27.9 us
  transfers between devices with their start and end apart: 4, of which 4 were waited for; matrix products, arithmetic and copies ran while one was open for 11% of the time, Pallas kernels for 0%

commit v1 on v0

v1 whole, which is shorter than its diff:
```python
import functools

import jax
import jax.numpy as jnp
from jax import lax
from jax.experimental import pallas as pl
from jax.experimental.pallas import tpu as pltpu
from jax.sharding import PartitionSpec as P

highest = lax.Precision.HIGHEST
section_decay = -5.0 / 9.0
section_gain = 15.0 / 16.0
time_step = 0.1
vmem_limit = 48 * 1024 * 1024


def shift(values, axis, step):
    count = lax.axis_size(axis)
    return lax.ppermute(values, axis, [(i, (i + step) % count) for i in range(count)])


def flux_pieces(values, direction):
    inverse = 1.0 / values[0]
    speeds = [values[1 + d] * inverse for d in range(3)]
    pressure = 0.4 * (
        values[4] - 0.5 * (values[1] * speeds[0] + values[2] * speeds[1] + values[3] * speeds[2])
    )
    velocity = speeds[direction]
    pieces = [values[1 + direction]]
    for component in range(1, 4):
        moment = values[component] * velocity
        if component - 1 == direction:
            moment = moment + pressure
        pieces.append(moment)
    pieces.append((values[4] + pressure) * velocity)
    return pieces


def matmul(a, b):
    return jnp.dot(a, b, precision=highest, preferred_element_type=jnp.float32)


def wall_kernel(count, fields, place_ref, own_ref, *refs):
    received = refs[: count - 1]
    matrix_ref = refs[count - 1]
    outs = refs[count:]
    rows, cells = own_ref.shape[2:]
    sources = [own_ref] + list(received)
    lines = []
    for source in sources:
        lines.append(
            jnp.concatenate(flux_pieces([source[f, 0] for f in range(fields)], 1), axis=1)
        )
    term = matmul(matrix_ref[...], jnp.concatenate(lines, axis=0))
    for s, out in enumerate(outs):
        for f in range(fields):
            out[f, 0] = term[s * rows : (s + 1) * rows, f * cells : (f + 1) * cells]


def wall_part(place, conserved, received, matrix, offset, part):
    fields, span, rows, cells = conserved.shape
    count = len(received) + 1
    group = span // count
    block = (fields, 1, rows, cells)
    piece = pl.BlockSpec(block, lambda i, place: (0, i, 0, 0))
    return pl.pallas_call(
        functools.partial(wall_kernel, count, fields),
        out_shape=[jax.ShapeDtypeStruct((fields, part, rows, cells), jnp.float32)] * count,
        grid_spec=pltpu.PrefetchScalarGridSpec(
            num_scalar_prefetch=1,
            grid=(part,),
            in_specs=[pl.BlockSpec(block, lambda i, place: (0, place[0] * group + offset + i, 0, 0))]
            + [piece] * (count - 1)
            + [pl.BlockSpec(matrix.shape, lambda i, place: (0, 0))],
            out_specs=[piece] * count,
        ),
        compiler_params=pltpu.CompilerParams(vmem_limit_bytes=vmem_limit),
        cost_estimate=pl.CostEstimate(
            flops=12 * part * fields * cells * matrix.shape[0] ** 2,
            bytes_accessed=8 * count * fields * part * rows * cells,
            transcendentals=0,
        ),
        name="wall_part",
    )(place, conserved, *received, matrix)


def local_kernel(
    halo,
    cons_ref,
    before_ref,
    after_ref,
    reg_ref,
    inlet_ref,
    edge_ref,
    band_ref,
    stream_ref,
    current_ref,
    partial_ref,
    span_flux,
    stream_flux,
    span_out,
):
    fields, span, tile, cells = cons_ref.shape
    wide = span + 2 * halo
    lane = lax.broadcasted_iota(jnp.int32, (tile, cells), 1)
    for z in range(wide):
        if z < halo:
            source, at = before_ref, z
        elif z < halo + span:
            source, at = cons_ref, z - halo
        else:
            source, at = after_ref, z - halo - span
        values = [
            jnp.where(lane == 0, inlet_ref[f, :, z : z + 1], source[f, at]) for f in range(fields)
        ]
        for f, piece in enumerate(flux_pieces(values, 2)):
            for t in range(cells // 128):
                span_flux[t, pl.ds((f * wide + z) * tile, tile), :] = piece[:, t * 128 : t * 128 + 128]
        if source is cons_ref:
            for f, piece in enumerate(flux_pieces(values, 0)):
                stream_flux[pl.ds((f * span + at) * tile, tile), :] = piece
                current_ref[f, at] = values[f]
    band = band_ref[...]
    for f in range(fields):
        for y in range(tile):
            for t in range(cells // 128):
                lines = span_flux[t, pl.ds(f * wide * tile + y, wide, stride=tile), :]
                span_out[t, pl.ds(f * span * tile + y, span, stride=tile), :] = matmul(band, lines)
    weights = stream_ref[...]
    for f in range(fields):
        rows = pl.ds(f * span * tile, span * tile)
        beside = jnp.concatenate([span_out[t, rows, :] for t in range(cells // 128)], axis=1)
        total = matmul(stream_flux[rows, :], weights) + beside
        total = total.reshape(span, tile, cells)
        for z in range(span):
            term = total[z] + jnp.where(lane == 0, edge_ref[f, :, z : z + 1], 0.0)
            partial_ref[f, z] = section_decay * reg_ref[f, z] - time_step * term


def local_part(conserved, before, after, register, inlet, edge, band, weights):
    fields, span, rows, cells = conserved.shape
    halo = before.shape[1]
    wide = span + 2 * halo
    tile = 8
    main = pl.BlockSpec((fields, span, tile, cells), lambda i: (0, 0, i, 0))
    side = pl.BlockSpec((fields, halo, tile, cells), lambda i: (0, 0, i, 0))
    whole = lambda a: pl.BlockSpec(a.shape, lambda i: (0, 0))
    column = lambda a: pl.BlockSpec((fields, tile, a.shape[2]), lambda i: (0, i, 0))
    shape = jax.ShapeDtypeStruct(conserved.shape, jnp.float32)
    return pl.pallas_call(
        functools.partial(local_kernel, halo),
        out_shape=[shape, shape],
        grid=(rows // tile,),
        in_specs=[main, side, side, main, column(inlet), column(edge), whole(band), whole(weights)],
        out_specs=[main, main],
        scratch_shapes=[
            pltpu.VMEM((cells // 128, fields * wide * tile, 128), jnp.float32),
            pltpu.VMEM((fields * span * tile, cells), jnp.float32),
            pltpu.VMEM((cells // 128, fields * span * tile, 128), jnp.float32),
        ],
        compiler_params=pltpu.CompilerParams(vmem_limit_bytes=vmem_limit),
        cost_estimate=pl.CostEstimate(
            flops=12 * conserved.size * (cells + wide),
            bytes_accessed=20 * conserved.size,
            transcendentals=0,
        ),
        name="local_part",
    )(conserved, before, after, register, inlet, edge, band, weights)


def close_kernel(place_ref, current_ref, partial_ref, term_ref, cons_out, reg_out):
    lane = lax.broadcasted_iota(jnp.int32, term_ref.shape, 3)
    new = partial_ref[...] - time_step * jnp.where(lane == 0, 0.0, term_ref[...])
    reg_out[...] = new
    cons_out[...] = current_ref[...] + section_gain * new


def close_part(place, current, partial, term, group, offset):
    fields, part, rows, cells = term.shape
    block = (fields, 1, rows, cells)
    there = pl.BlockSpec(block, lambda i, place: (0, place[0] * group + offset + i, 0, 0))
    shape = jax.ShapeDtypeStruct(current.shape, jnp.float32)
    return pl.pallas_call(
        close_kernel,
        out_shape=[shape, shape],
        grid_spec=pltpu.PrefetchScalarGridSpec(
            num_scalar_prefetch=1,
            grid=(part,),
            in_specs=[there, there, pl.BlockSpec(block, lambda i, place: (0, i, 0, 0))],
            out_specs=[there, there],
        ),
        input_output_aliases={1: 0, 2: 1},
        compiler_params=pltpu.CompilerParams(vmem_limit_bytes=vmem_limit),
        cost_estimate=pl.CostEstimate(
            flops=4 * term.size, bytes_accessed=20 * term.size, transcendentals=0
        ),
        name="close_part",
    )(place, current, partial, term)


def stream_weights(blocks):
    count, _, width, _ = blocks.shape
    size = count * width
    full = jnp.zeros((size, size), jnp.float32)
    for k in range(count):
        for j in range(3):
            if 0 <= k + j - 1 < count:
                full = lax.dynamic_update_slice(full, blocks[k, j], (k * width, (k + j - 1) * width))
    return full.T


def span_band(blocks):
    count, _, width, _ = blocks.shape
    full = jnp.zeros((count * width, (count + 2) * width), jnp.float32)
    for k in range(count):
        for j in range(3):
            full = lax.dynamic_update_slice(full, blocks[k, j], (k * width, (k + j) * width))
    return full


def local(
    conserved,
    register,
    stream_blocks,
    wall_matrix,
    span_blocks,
    inflow_gain,
    source_block,
    source_column,
):
    fields, span, rows, cells = conserved.shape
    columns = span * rows
    count = lax.axis_size("py")
    across = lax.axis_size("pz")
    row = lax.axis_index("py")
    group = span // count
    parts = min(4, group)
    part = group // parts
    width = span_blocks.shape[2]
    place = lambda s: jnp.reshape((row + s) % count, (1,)).astype(jnp.int32)

    def outgoing(source, c):
        sent = []
        for s in range(1, count):
            start = ((row + s) % count) * group + c * part
            piece = lax.dynamic_slice_in_dim(source, start, part, 1)
            sent.append(shift(piece, "py", s))
        return sent

    received = [outgoing(conserved, 0)]

    recycle = conserved[:, :, :, 3 * cells // 4].reshape(-1, 128)
    recycle, later = lax.optimization_barrier((recycle, conserved))
    along = [recycle] + [shift(recycle, "py", s) for s in range(1, count)]
    for c in range(1, parts):
        received.append(outgoing(later, c))
    after = shift(later[:, :width], "pz", -1)
    before = shift(later[:, span - width :], "pz", 1)

    stacked = jnp.stack(along)
    whole_plane = lax.all_gather(stacked, "pz", axis=0)
    whole_plane = whole_plane.reshape(across, count, fields, columns)
    whole_plane = jnp.transpose(whole_plane, (2, 0, 1, 3)).reshape(fields, -1)
    myself = lax.axis_index(("py", "pz"))
    own_block = lax.dynamic_index_in_dim(source_block[:, :, 0], myself, 0, keepdims=False)
    own_column = lax.dynamic_index_in_dim(source_column, myself, 0, keepdims=False)
    slot = (own_block % across) * count + (row - own_block // across) % count
    fetched = jnp.take(whole_plane, slot * columns + own_column, axis=1)
    inlet = (fetched * inflow_gain[:, None]).reshape(fields, span, rows)

    inlet_after = shift(inlet[:, :width], "pz", -1)
    inlet_before = shift(inlet[:, span - width :], "pz", 1)
    lines = jnp.stack([inlet] + [shift(inlet, "py", s) for s in range(1, count)])
    order = (row - jnp.arange(count)) % count
    squares = wall_matrix.reshape(count, rows, count, rows)
    squares = jnp.take(jnp.take(squares, order, axis=0), order, axis=2)
    matrix = squares.reshape(wall_matrix.shape)
    line_flux = jnp.stack(flux_pieces([lines[:, f] for f in range(fields)], 1))
    edge = jnp.einsum("asb,fszb->faz", squares[0], line_flux, precision=highest)
    inlet_wide = jnp.concatenate([inlet_before, inlet, inlet_after], axis=1).swapaxes(1, 2)

    local_blocks = span // width
    own_blocks = lax.dynamic_slice_in_dim(
        span_blocks, lax.axis_index("pz") * local_blocks, local_blocks, 0
    )
    current, partial = local_part(
        conserved,
        before,
        after,
        register,
        inlet_wide,
        edge,
        span_band(own_blocks),
        stream_weights(stream_blocks),
    )

    returned = []
    for c in range(parts):
        pieces = wall_part(place(0), conserved, received[c], matrix, c * part, part)
        returned.append([pieces[0]] + [shift(pieces[s], "py", -s) for s in range(1, count)])
    for c in range(parts):
        for s in range(count):
            current, partial = close_part(
                place(s), current, partial, returned[c][s], group, c * part
            )
    return (current, partial)


def solution(mesh):
    return jax.shard_map(
        local,
        mesh=mesh,
        in_specs=(
            P(None, "pz", "py", None),
            P(None, "pz", "py", None),
            P(),
            P(),
            P(),
            P(),
            P(),
            P(),
        ),
        out_specs=(P(None, "pz", "py", None), P(None, "pz", "py", None)),
        check_vma=False,
    )
```

time: 1130 us -> 633 us (0.56)
  waiting for transfers between devices: 461 us -> 122 us
  blocking collectives: 233 us -> 0 us
  starting transfers between devices: 7.15 us -> 208 us
  Pallas kernels: 0 us -> 112 us
  local copies, waits for them, and re-layouts: 262 us -> 164 us
  matrix products: 95.3 us -> 1.46 us
  other arithmetic: 55.9 us -> 8.03 us
    all_gather x1, waiting for transfers between devices: 356 us -> 0.01 us  [local(): whole_plane = lax.all_gather(stacked, 'pz', axis=0)]
    all_to_all x1 -> x0, blocking collectives: 233 us -> none  [local(): lax.all_to_all(current, 'py', split_axis=1, concat_axis=2, tiled=True)]
    ppermute x2 -> x34, starting transfers between devices: 0.66 us -> 208 us  [shift(): lax.ppermute(values, axis, [(i, (i + step) % count) for i in range(count)])]
    pallas_call x0 -> x21, Pallas kernels: none -> 112 us  [the longest x16 57.2 us: close_part(): pl.pallas_call(close_kernel, out_shape=[shape, shape], grid_spec=pltpu.Pr...]
    dot_general x5 -> x1, matrix products: 95.3 us -> 1.46 us  [local(): edge = jnp.einsum('asb,fszb->faz', squares[0], line_flux, precision=highest)]
    slice x13 -> x4, local copies, waits for them, and re-layouts: 80.5 us -> 21.5 us  [the longest x1 10.4 us: local(): after = shift(later[:, :width], 'pz', -1)]
    scatter x2 -> x0, local copies, waits for them, and re-layouts: 31.4 us -> none  [local(): current = conserved.at[:, :, :, 0].set(inlet_plane)]
    ppermute x2 -> x34, waiting for transfers between devices: 95.8 us -> 122 us  [shift(): lax.ppermute(values, axis, [(i, (i + step) % count) for i in range(count)])]
  transfers between devices with their start and end apart: 4 -> 35, of which waited for: 4 -> 9; matrix products, arithmetic and copies ran while one was open for 11% -> 23% of each run, Pallas kernels for 0% -> 17%
where the time goes in v1:
time: 633 us; the launch traced here: 630 us
  starting transfers between devices  208 us (33%)
  local copies, waits for them, and re-layouts  164 us (26%)
  waiting for transfers between devices  122 us (19%)
  Pallas kernels  112 us (18%)
  between operations  14.4 us (2%)
  other arithmetic  8.03 us (1%)
    ppermute x34, starting transfers between devices, shift(): lax.ppermute(values, axis, [(i, (i + step) % count) for i in range(count)])  208 us
    ppermute x34, waiting for transfers between devices, shift(): lax.ppermute(values, axis, [(i, (i + step) % count) for i in range(count)])  122 us
    gather x3, local copies, waits for them, and re-layouts, local(): fetched = jnp.take(whole_plane, slot * columns + own_column, axis=1)  65.4 us
    pallas_call x16, Pallas kernels, close_part(): pl.pallas_call(close_kernel, out_shape=[shape, shape], grid_spec=pltpu.Pr...  57.2 us
    pallas_call x1, Pallas kernels, local_part(): pl.pallas_call(functools.partial(local_kernel, halo), out_shape=[shape, s...  36.3 us
    transpose x1, local copies, waits for them, and re-layouts, local(): whole_plane = jnp.transpose(whole_plane, (2, 0, 1, 3)).reshape(fields, -1)  31 us
    pallas_call x4, Pallas kernels, wall_part(): pl.pallas_call(functools.partial(wall_kernel, count, fields), out_shape=[...  19 us
    unnamed x58, local copies, waits for them, and re-layouts  17.6 us
  transfers between devices with their start and end apart: 35, of which 9 were waited for; matrix products, arithmetic and copies ran while one was open for 23% of the time, Pallas kernels for 17%

profile of v1, /device:TPU:0, one launch (start us, length us, event | category | flops | bytes accessed | tf_op | source)
XLA Modules:
  0.0 630.4 jit_solution(60439828400665111)
XLA Ops:
  7.2 9.5 %slice_reduce_fusion = f32[5,64,64]{2,1,0:T(8,128)S(1)} fusion(f32[5,64,64,128]{3,2,1,0:T(8,128)} %own_ref.7), kind=kLoop, calls=%fused_computation.3 | loop fusion | bytes 163840 | tf_op jit(solution)/shard_map/slice | solution.py:252
  16.8 3.1 collective-permute-start.2
  24.9 3.0 collective-permute-done.3
  28.9 10.4 %fusion.31 = (f32[5,32,64,128]{3,2,1,0:T(8,128)}, f32[5,32,64,128]{3,2,1,0:T(8,128)}) fusion(f32[5,64,64,128]{3,2,1,0:T(8,128)} %own_ref.7), kind=kLoop, calls=%fused_computation.105 | loop fusion | bytes 20971520 | tf_op jit(solution)/shard_map/slice | solution.py:257
  51.0 5.3 constant_dynamic-slice_fusion
  56.4 7.9 %collective-permute-done.10.refs_0_ = f32[5,4,64,128]{3,2,1,0:T(8,128)S(1)} collective-permute-done((f32[5,4,64,128]{3,2,1,0:T(8,128)S(1)}, f32[5,4,64,128]{3,2,1,0:T(8,128)S(1)}, u32[]{:S(2)}, u32[]{:S(2)}) %collective-permute-start.10) | collective-permute-done | bytes 655392 | tf_op jit(solution)/shard_map/ppermute | solution.py:19
  64.3 23.8 %collective-permute-start.16 = (f32[5,4,64,128]{3,2,1,0:T(8,128)}, f32[5,4,64,128]{3,2,1,0:T(8,128)S(1)}, u32[]{:S(2)}, u32[]{:S(2)}) collective-permute-start(f32[5,4,64,128]{3,2,1,0:T(8,128)} %get-tuple-element.114), channel_id=1, source_target_pairs={{0,8},{8,16},{16,24},{24,0},{1,9},{9,17},{17,25},{25,1},{2,10},{10... | collective-permute-start | bytes 1966088 | tf_op jit(solution)/shard_map/ppermute | solution.py:19
  103.0 25.0 %collective-permute-start.18 = (f32[5,4,64,128]{3,2,1,0:T(8,128)}, f32[5,4,64,128]{3,2,1,0:T(8,128)S(1)}, u32[]{:S(2)}, u32[]{:S(2)}) collective-permute-start(f32[5,4,64,128]{3,2,1,0:T(8,128)} %get-tuple-element.112), channel_id=1, source_target_pairs={{0,24},{8,0},{16,8},{24,16},{1,25},{9,1},{17,9},{25,17},{2,26},{10... | collective-permute-start | bytes 1966088 | tf_op jit(solution)/shard_map/ppermute | solution.py:19
  129.0 17.4 %collective-permute-start.22 = (f32[5,4,64,128]{3,2,1,0:T(8,128)}, f32[5,4,64,128]{3,2,1,0:T(8,128)S(1)}, u32[]{:S(2)}, u32[]{:S(2)}) collective-permute-start(f32[5,4,64,128]{3,2,1,0:T(8,128)} %get-tuple-element.111), channel_id=1, source_target_pairs={{0,8},{8,16},{16,24},{24,0},{1,9},{9,17},{17,25},{25,1},{2,10},{10... | collective-permute-start | bytes 1966088 | tf_op jit(solution)/shard_map/ppermute | solution.py:19
  147.5 6.1 collective-permute-done.17.refs_1_
  154.4 13.1 %collective-permute-done.18.refs_2_ = f32[5,4,64,128]{3,2,1,0:T(8,128)S(1)} collective-permute-done((f32[5,4,64,128]{3,2,1,0:T(8,128)}, f32[5,4,64,128]{3,2,1,0:T(8,128)S(1)}, u32[]{:S(2)}, u32[]{:S(2)}) %collective-permute-start.18) | collective-permute-done | bytes 655392 | tf_op jit(solution)/shard_map/ppermute | solution.py:19
  168.3 17.6 %collective-permute-start.24 = (f32[5,4,64,128]{3,2,1,0:T(8,128)}, f32[5,4,64,128]{3,2,1,0:T(8,128)}, u32[]{:S(2)}, u32[]{:S(2)}) collective-permute-start(f32[5,4,64,128]{3,2,1,0:T(8,128)} %get-tuple-element.109), channel_id=1, source_target_pairs={{0,24},{8,0},{16,8},{24,16},{1,25},{9,1},{17,9},{25,17},{2,26},{10... | collective-permute-start | bytes 1966088 | tf_op jit(solution)/shard_map/ppermute | solution.py:19
  187.4 16.0 %collective-permute-start.28 = (f32[5,4,64,128]{3,2,1,0:T(8,128)}, f32[5,4,64,128]{3,2,1,0:T(8,128)}, u32[]{:S(2)}, u32[]{:S(2)}) collective-permute-start(f32[5,4,64,128]{3,2,1,0:T(8,128)} %get-tuple-element.108), channel_id=1, source_target_pairs={{0,8},{8,16},{16,24},{24,0},{1,9},{9,17},{17,25},{25,1},{2,10},{10... | collective-permute-start | bytes 1966088 | tf_op jit(solution)/shard_map/ppermute | solution.py:19
  209.2 4.7 wall_part.4
  216.5 4.5 wall_part.5
  225.4 2.9 collective-permute-start.30
  228.4 4.9 wall_part.6
  235.8 4.4 reshape.478
  240.2 31.0 %copy.85 = f32[5,8,4,4096]{0,3,2,1:T(8,128)} copy(f32[5,8,4,4096]{3,0,2,1:T(8,128)} %bitcast.127) | data formatting | bytes 5242880 | tf_op jit(solution)/shard_map/transpose | solution.py:263
  271.2 59.4 %gather_fusion = f32[4096,5]{1,0:T(8,128)} fusion(f32[5,131072]{0,1:T(8,128)} %bitcast.9, s32[4096]{0:T(1024)S(1)} %copy-done.26), kind=kCustom, calls=%fused_computation | custom fusion | bytes 180224 | tf_op jit(solution)/shard_map/jit(_take)/gather | solution.py:268
  330.6 3.3 copy.87
  333.9 17.7 %collective-permute-start.13 = (f32[5,4,64,128]{3,2,1,0:T(8,128)}, f32[5,4,64,128]{3,2,1,0:T(8,128)S(1)}, u32[]{:S(2)}, u32[]{:S(2)}) collective-permute-start(f32[5,4,64,128]{3,2,1,0:T(8,128)} %copy-done.22), channel_id=1, source_target_pairs={{0,24},{8,0},{16,8},{24,16},{1,25},{9,1},{17,9},{25,17},{2,26},{10... | collective-permute-start | bytes 1966088 | tf_op jit(solution)/shard_map/ppermute | solution.py:19
  358.0 4.9 wall_part.7
  368.1 3.0 collective-permute-start.8
  372.2 5.1 collective-permute-done.7
  377.3 12.8 %collective-permute-start.14 = (f32[5,4,64,128]{3,2,1,0:T(8,128)}, f32[5,4,64,128]{3,2,1,0:T(8,128)S(1)}, u32[]{:S(2)}, u32[]{:S(2)}) collective-permute-start(f32[5,4,64,128]{3,2,1,0:T(8,128)} %copy-done.21), channel_id=1, source_target_pairs={{0,16},{8,24},{16,0},{24,8},{1,17},{9,25},{17,1},{25,9},{2,18},{10... | collective-permute-start | bytes 1966088 | tf_op jit(solution)/shard_map/ppermute | solution.py:19
  395.9 53.2 %collective-permute-done.14.term_ref = f32[5,4,64,128]{3,2,1,0:T(8,128)S(1)} collective-permute-done((f32[5,4,64,128]{3,2,1,0:T(8,128)}, f32[5,4,64,128]{3,2,1,0:T(8,128)S(1)}, u32[]{:S(2)}, u32[]{:S(2)}) %collective-permute-start.14) | collective-permute-done | bytes 655392 | tf_op jit(solution)/shard_map/ppermute | solution.py:19
  449.1 3.8 collective-permute-start.25
  454.5 32.5 %collective-permute-done.20.term_ref = f32[5,4,64,128]{3,2,1,0:T(8,128)S(1)} collective-permute-done((f32[5,4,64,128]{3,2,1,0:T(8,128)}, f32[5,4,64,128]{3,2,1,0:T(8,128)S(1)}, u32[]{:S(2)}, u32[]{:S(2)}) %collective-permute-start.20) | collective-permute-done | bytes 655392 | tf_op jit(solution)/shard_map/ppermute | solution.py:19
  487.1 24.1 %collective-permute-start.27 = (f32[5,4,64,128]{3,2,1,0:T(8,128)}, f32[5,4,64,128]{3,2,1,0:T(8,128)S(1)}, u32[]{:S(2)}, u32[]{:S(2)}) collective-permute-start(f32[5,4,64,128]{3,2,1,0:T(8,128)} %copy-done.11), channel_id=1, source_target_pairs={{0,8},{8,16},{16,24},{24,0},{1,9},{9,17},{17,25},{25,1},{2,10},{10... | collective-permute-start | bytes 1966088 | tf_op jit(solution)/shard_map/ppermute | solution.py:19
  511.2 17.2 %collective-permute-start.32 = (f32[5,4,64,128]{3,2,1,0:T(8,128)}, f32[5,4,64,128]{3,2,1,0:T(8,128)S(1)}, u32[]{:S(2)}, u32[]{:S(2)}) collective-permute-start(f32[5,4,64,128]{3,2,1,0:T(8,128)} %copy-done.14), channel_id=1, source_target_pairs={{0,16},{8,24},{16,0},{24,8},{1,17},{9,25},{17,1},{25,9},{2,18},{10... | collective-permute-start | bytes 1966088 | tf_op jit(solution)/shard_map/ppermute | solution.py:19
  530.0 36.3 %local_part.1 = (f32[5,64,64,128]{3,2,1,0:T(8,128)}, f32[5,64,64,128]{3,2,1,0:T(8,128)}) custom-call(f32[5,64,64,128]{3,2,1,0:T(8,128)} %own_ref.7, f32[5,32,64,128]{3,2,1,0:T(8,128)} %collective-permute-done.before_ref, f32[5,32,64,128]{3,2,1,0:T(8,128)} %collective-permute-done.1.after_ref, f32[5,64,64,128]{3,2,1,0:T(8,128)} %reg_ref.1, ...), custom_call_target="tpu_custom_call" | custom-call | flops 8053063680 | bytes 52428800 | tf_op jit(solution)/shard_map/local_part/pallas_call | solution.py:150
  566.3 3.6 close_part.16
  569.9 3.6 close_part.17
  573.5 3.6 close_part.18
  577.0 3.6 close_part.19
  580.6 3.6 close_part.20
  584.2 3.6 close_part.21
  587.8 3.6 close_part.22
  591.3 3.6 close_part.23
  594.9 3.6 close_part.24
  598.5 3.6 close_part.25
  602.1 3.6 close_part.26
  605.6 3.6 close_part.27
  609.2 3.6 close_part.28
  612.8 3.6 close_part.29
  616.4 3.6 close_part.30
  620.0 3.6 close_part.31
  (152 shorter events, 74.8 us)
Async XLA Ops:
  7.2 228.6 %all-gather.3.cloned.1.call-start = ((), (), s32[]{:S(2)}) async-start(), calls=%async_computation | async-start | bytes 2949120 | tf_op jit(solution)/shard_map/all_gather | solution.py:261
  16.8 8.1 %collective-permute-start.2 = (f32[160,128]{1,0:T(8,128)S(1)}, f32[160,128]{1,0:T(8,128)S(1)}, u32[]{:S(2)}, u32[]{:S(2)}) collective-permute-start(f32[160,128]{1,0:T(8,128)S(1)} %reshape_squeeze.3), channel_id=1, source_target_pairs={{0,8},{8,16},{16,24},{24,0},{1,9},{9,17},{17,25},{25,1},{2,10},{10... | collective-permute-start | bytes 245768 | tf_op jit(solution)/shard_map/ppermute | solution.py:19
  19.9 8.1 %collective-permute-start.3 = (f32[160,128]{1,0:T(8,128)S(1)}, f32[160,128]{1,0:T(8,128)S(1)}, u32[]{:S(2)}, u32[]{:S(2)}) collective-permute-start(f32[160,128]{1,0:T(8,128)S(1)} %reshape_squeeze.3), channel_id=1, source_target_pairs={{0,16},{8,24},{16,0},{24,8},{1,17},{9,25},{17,1},{25,9},{2,18},{10... | collective-permute-start | bytes 245768 | tf_op jit(solution)/shard_map/ppermute | solution.py:19
  22.4 5.7 collective-permute-start.4
  39.3 49.0 %copy-start.25 = (f32[256,256]{1,0:T(8,128)S(1)}, f32[256,256]{1,0:T(8,128)}, u32[]{:S(2)}) copy-start(f32[256,256]{1,0:T(8,128)} %param.11) | copy-start | bytes 786436
  39.3 472.0 %collective-permute-start = (f32[5,32,64,128]{3,2,1,0:T(8,128)}, f32[5,32,64,128]{3,2,1,0:T(8,128)}, u32[]{:S(2)}, u32[]{:S(2)}) collective-permute-start(f32[5,32,64,128]{3,2,1,0:T(8,128)} %get-tuple-element.119), channel_id=1, source_target_pairs={{0,1},{1,2},{2,3},{3,4},{4,5},{5,6},{6,7},{7,0},{8,9},{9,10},{10,1... | collective-permute-start | bytes 15728648 | tf_op jit(solution)/shard_map/ppermute | solution.py:19
  39.3 489.2 %collective-permute-start.1 = (f32[5,32,64,128]{3,2,1,0:T(8,128)}, f32[5,32,64,128]{3,2,1,0:T(8,128)}, u32[]{:S(2)}, u32[]{:S(2)}) collective-permute-start(f32[5,32,64,128]{3,2,1,0:T(8,128)} %get-tuple-element.118), channel_id=1, source_target_pairs={{0,7},{1,0},{2,1},{3,2},{4,3},{5,4},{6,5},{7,6},{8,15},{9,8},{10,9... | collective-permute-start | bytes 15728648 | tf_op jit(solution)/shard_map/ppermute | solution.py:19
  44.7 19.6 %collective-permute-start.10 = (f32[5,4,64,128]{3,2,1,0:T(8,128)S(1)}, f32[5,4,64,128]{3,2,1,0:T(8,128)S(1)}, u32[]{:S(2)}, u32[]{:S(2)}) collective-permute-start(f32[5,4,64,128]{3,2,1,0:T(8,128)S(1)} %get-tuple-element.117), channel_id=1, source_target_pairs={{0,8},{8,16},{16,24},{24,0},{1,9},{9,17},{17,25},{25,1},{2,10},{10... | collective-permute-start | bytes 1966088 | tf_op jit(solution)/shard_map/ppermute | solution.py:19
  46.7 53.9 %collective-permute-start.11 = (f32[5,4,64,128]{3,2,1,0:T(8,128)}, f32[5,4,64,128]{3,2,1,0:T(8,128)S(1)}, u32[]{:S(2)}, u32[]{:S(2)}) collective-permute-start(f32[5,4,64,128]{3,2,1,0:T(8,128)} %get-tuple-element.116), channel_id=1, source_target_pairs={{0,16},{8,24},{16,0},{24,8},{1,17},{9,25},{17,1},{25,9},{2,18},{10... | collective-permute-start | bytes 1966088 | tf_op jit(solution)/shard_map/ppermute | solution.py:19
  48.6 54.4 %collective-permute-start.12 = (f32[5,4,64,128]{3,2,1,0:T(8,128)}, f32[5,4,64,128]{3,2,1,0:T(8,128)S(1)}, u32[]{:S(2)}, u32[]{:S(2)}) collective-permute-start(f32[5,4,64,128]{3,2,1,0:T(8,128)} %get-tuple-element.115), channel_id=1, source_target_pairs={{0,24},{8,0},{16,8},{24,16},{1,25},{9,1},{17,9},{25,17},{2,26},{10... | collective-permute-start | bytes 1966088 | tf_op jit(solution)/shard_map/ppermute | solution.py:19
  64.3 64.7 %collective-permute-start.16 = (f32[5,4,64,128]{3,2,1,0:T(8,128)}, f32[5,4,64,128]{3,2,1,0:T(8,128)S(1)}, u32[]{:S(2)}, u32[]{:S(2)}) collective-permute-start(f32[5,4,64,128]{3,2,1,0:T(8,128)} %get-tuple-element.114), channel_id=1, source_target_pairs={{0,8},{8,16},{16,24},{24,0},{1,9},{9,17},{17,25},{25,1},{2,10},{10... | collective-permute-start | bytes 1966088 | tf_op jit(solution)/shard_map/ppermute | solution.py:19
  95.5 33.5 %copy-start.23 = (f32[4,4,64,64]{3,2,1,0:T(8,128)}, f32[4,4,64,64]{3,2,1,0:T(8,128)S(1)}, u32[]{:S(2)}) copy-start(f32[4,4,64,64]{3,2,1,0:T(8,128)S(1)} %gather_fusion.2) | copy-start | bytes 786436
  100.6 53.0 %collective-permute-start.17 = (f32[5,4,64,128]{3,2,1,0:T(8,128)}, f32[5,4,64,128]{3,2,1,0:T(8,128)S(1)}, u32[]{:S(2)}, u32[]{:S(2)}) collective-permute-start(f32[5,4,64,128]{3,2,1,0:T(8,128)} %get-tuple-element.113), channel_id=1, source_target_pairs={{0,16},{8,24},{16,0},{24,8},{1,17},{9,25},{17,1},{25,9},{2,18},{10... | collective-permute-start | bytes 1966088 | tf_op jit(solution)/shard_map/ppermute | solution.py:19
  103.0 64.5 %collective-permute-start.18 = (f32[5,4,64,128]{3,2,1,0:T(8,128)}, f32[5,4,64,128]{3,2,1,0:T(8,128)S(1)}, u32[]{:S(2)}, u32[]{:S(2)}) collective-permute-start(f32[5,4,64,128]{3,2,1,0:T(8,128)} %get-tuple-element.112), channel_id=1, source_target_pairs={{0,24},{8,0},{16,8},{24,16},{1,25},{9,1},{17,9},{25,17},{2,26},{10... | collective-permute-start | bytes 1966088 | tf_op jit(solution)/shard_map/ppermute | solution.py:19
  129.0 57.5 %collective-permute-start.22 = (f32[5,4,64,128]{3,2,1,0:T(8,128)}, f32[5,4,64,128]{3,2,1,0:T(8,128)S(1)}, u32[]{:S(2)}, u32[]{:S(2)}) collective-permute-start(f32[5,4,64,128]{3,2,1,0:T(8,128)} %get-tuple-element.111), channel_id=1, source_target_pairs={{0,8},{8,16},{16,24},{24,0},{1,9},{9,17},{17,25},{25,1},{2,10},{10... | collective-permute-start | bytes 1966088 | tf_op jit(solution)/shard_map/ppermute | solution.py:19
  154.4 69.2 %collective-permute-start.23 = (f32[5,4,64,128]{3,2,1,0:T(8,128)}, f32[5,4,64,128]{3,2,1,0:T(8,128)}, u32[]{:S(2)}, u32[]{:S(2)}) collective-permute-start(f32[5,4,64,128]{3,2,1,0:T(8,128)} %get-tuple-element.110), channel_id=1, source_target_pairs={{0,16},{8,24},{16,0},{24,8},{1,17},{9,25},{17,1},{25,9},{2,18},{10... | collective-permute-start | bytes 1966088 | tf_op jit(solution)/shard_map/ppermute | solution.py:19
  168.3 57.1 %collective-permute-start.24 = (f32[5,4,64,128]{3,2,1,0:T(8,128)}, f32[5,4,64,128]{3,2,1,0:T(8,128)}, u32[]{:S(2)}, u32[]{:S(2)}) collective-permute-start(f32[5,4,64,128]{3,2,1,0:T(8,128)} %get-tuple-element.109), channel_id=1, source_target_pairs={{0,24},{8,0},{16,8},{24,16},{1,25},{9,1},{17,9},{25,17},{2,26},{10... | collective-permute-start | bytes 1966088 | tf_op jit(solution)/shard_map/ppermute | solution.py:19
  186.6 0.9 copy-start
  187.4 146.4 %collective-permute-start.28 = (f32[5,4,64,128]{3,2,1,0:T(8,128)}, f32[5,4,64,128]{3,2,1,0:T(8,128)}, u32[]{:S(2)}, u32[]{:S(2)}) collective-permute-start(f32[5,4,64,128]{3,2,1,0:T(8,128)} %get-tuple-element.108), channel_id=1, source_target_pairs={{0,8},{8,16},{16,24},{24,0},{1,9},{9,17},{17,25},{25,1},{2,10},{10... | collective-permute-start | bytes 1966088 | tf_op jit(solution)/shard_map/ppermute | solution.py:19
  209.2 7.3 %copy-start.3 = (f32[5,4,64,128]{3,2,1,0:T(8,128)S(1)}, f32[5,4,64,128]{3,2,1,0:T(8,128)}, u32[]{:S(2)}) copy-start(f32[5,4,64,128]{3,2,1,0:T(8,128)} %copy-done.2) | copy-start | bytes 1966084
  209.2 7.3 %copy-start.5 = (f32[5,4,64,128]{3,2,1,0:T(8,128)S(1)}, f32[5,4,64,128]{3,2,1,0:T(8,128)}, u32[]{:S(2)}) copy-start(f32[5,4,64,128]{3,2,1,0:T(8,128)} %copy-done.4) | copy-start | bytes 1966084
  209.2 19.1 %copy-start.1 = (f32[5,4,64,128]{3,2,1,0:T(8,128)S(1)}, f32[5,4,64,128]{3,2,1,0:T(8,128)}, u32[]{:S(2)}) copy-start(f32[5,4,64,128]{3,2,1,0:T(8,128)} %copy-done) | copy-start | bytes 1966084
  213.9 0.9 copy-start.20
  214.8 0.9 copy-start.21
  223.6 129.8 %collective-permute-start.29 = (f32[5,4,64,128]{3,2,1,0:T(8,128)}, f32[5,4,64,128]{3,2,1,0:T(8,128)S(1)}, u32[]{:S(2)}, u32[]{:S(2)}) collective-permute-start(f32[5,4,64,128]{3,2,1,0:T(8,128)} %get-tuple-element.107), channel_id=1, source_target_pairs={{0,16},{8,24},{16,0},{24,8},{1,17},{9,25},{17,1},{25,9},{2,18},{10... | collective-permute-start | bytes 1966088 | tf_op jit(solution)/shard_map/ppermute | solution.py:19
  225.4 128.8 %collective-permute-start.30 = (f32[5,4,64,128]{3,2,1,0:T(8,128)}, f32[5,4,64,128]{3,2,1,0:T(8,128)}, u32[]{:S(2)}, u32[]{:S(2)}) collective-permute-start(f32[5,4,64,128]{3,2,1,0:T(8,128)} %get-tuple-element.106), channel_id=1, source_target_pairs={{0,24},{8,0},{16,8},{24,16},{1,25},{9,1},{17,9},{25,17},{2,26},{10... | collective-permute-start | bytes 1966088 | tf_op jit(solution)/shard_map/ppermute | solution.py:19
  240.2 31.0 %copy-start.26 = (s32[4096]{0:T(1024)S(1)}, s32[4096]{0:T(1024)}, u32[]{:S(2)}) copy-start(s32[4096]{0:T(1024)} %broadcast_clamp_fusion) | copy-start | bytes 49156
  240.2 111.4 %copy-start.27 = (f32[5]{0:T(128)S(1)}, f32[5]{0:T(128)}, u32[]{:S(2)}) copy-start(f32[5]{0:T(128)} %param.13) | copy-start | bytes 64
  333.9 34.2 %collective-permute-start.13 = (f32[5,4,64,128]{3,2,1,0:T(8,128)}, f32[5,4,64,128]{3,2,1,0:T(8,128)S(1)}, u32[]{:S(2)}, u32[]{:S(2)}) collective-permute-start(f32[5,4,64,128]{3,2,1,0:T(8,128)} %copy-done.22), channel_id=1, source_target_pairs={{0,24},{8,0},{16,8},{24,16},{1,25},{9,1},{17,9},{25,17},{2,26},{10... | collective-permute-start | bytes 1966088 | tf_op jit(solution)/shard_map/ppermute | solution.py:19
  352.6 1.7 copy-start.24
  354.2 13.9 %collective-permute-start.5 = (f32[5,32,64]{1,2,0:T(8,128)}, f32[5,32,64]{1,2,0:T(8,128)}, u32[]{:S(2)}, u32[]{:S(2)}) collective-permute-start(f32[5,32,64]{1,2,0:T(8,128)} %get-tuple-element.126), channel_id=1, source_target_pairs={{0,1},{1,2},{2,3},{3,4},{4,5},{5,6},{6,7},{7,0},{8,9},{9,10},{10,1... | collective-permute-start | bytes 122888 | tf_op jit(solution)/shard_map/ppermute | solution.py:19
  354.2 16.9 %collective-permute-start.6 = (f32[5,32,64]{1,2,0:T(8,128)}, f32[5,32,64]{1,2,0:T(8,128)}, u32[]{:S(2)}, u32[]{:S(2)}) collective-permute-start(f32[5,32,64]{1,2,0:T(8,128)} %get-tuple-element.127), channel_id=1, source_target_pairs={{0,7},{1,0},{2,1},{3,2},{4,3},{5,4},{6,5},{7,6},{8,15},{9,8},{10,9... | collective-permute-start | bytes 122888 | tf_op jit(solution)/shard_map/ppermute | solution.py:19
  356.9 1.1 copy-start.7
  364.5 0.9 copy-start.15
  368.0 9.2 %collective-permute-start.7 = (f32[5,64,64]{1,2,0:T(8,128)}, f32[5,64,64]{1,2,0:T(8,128)S(1)}, u32[]{:S(2)}, u32[]{:S(2)}) collective-permute-start(f32[5,64,64]{1,2,0:T(8,128)} %copy-done.24), channel_id=1, source_target_pairs={{0,8},{8,16},{16,24},{24,0},{1,9},{9,17},{17,25},{25,1},{2,10},{10... | collective-permute-start | bytes 245768 | tf_op jit(solution)/shard_map/ppermute | solution.py:19
  368.1 22.0 %collective-permute-start.8 = (f32[5,64,64]{1,2,0:T(8,128)}, f32[5,64,64]{1,2,0:T(8,128)S(1)}, u32[]{:S(2)}, u32[]{:S(2)}) collective-permute-start(f32[5,64,64]{1,2,0:T(8,128)} %copy-done.24), channel_id=1, source_target_pairs={{0,16},{8,24},{16,0},{24,8},{1,17},{9,25},{17,1},{25,9},{2,18},{10... | collective-permute-start | bytes 245768 | tf_op jit(solution)/shard_map/ppermute | solution.py:19
  371.2 20.6 %collective-permute-start.9 = (f32[5,64,64]{1,2,0:T(8,128)}, f32[5,64,64]{1,2,0:T(8,128)S(1)}, u32[]{:S(2)}, u32[]{:S(2)}) collective-permute-start(f32[5,64,64]{1,2,0:T(8,128)} %copy-done.24), channel_id=1, source_target_pairs={{0,24},{8,0},{16,8},{24,16},{1,25},{9,1},{17,9},{25,17},{2,26},{10... | collective-permute-start | bytes 245768 | tf_op jit(solution)/shard_map/ppermute | solution.py:19
  377.3 71.8 %collective-permute-start.14 = (f32[5,4,64,128]{3,2,1,0:T(8,128)}, f32[5,4,64,128]{3,2,1,0:T(8,128)S(1)}, u32[]{:S(2)}, u32[]{:S(2)}) collective-permute-start(f32[5,4,64,128]{3,2,1,0:T(8,128)} %copy-done.21), channel_id=1, source_target_pairs={{0,16},{8,24},{16,0},{24,8},{1,17},{9,25},{17,1},{25,9},{2,18},{10... | collective-permute-start | bytes 1966088 | tf_op jit(solution)/shard_map/ppermute | solution.py:19
  390.1 59.0 %collective-permute-start.15 = (f32[5,4,64,128]{3,2,1,0:T(8,128)}, f32[5,4,64,128]{3,2,1,0:T(8,128)S(1)}, u32[]{:S(2)}, u32[]{:S(2)}) collective-permute-start(f32[5,4,64,128]{3,2,1,0:T(8,128)} %copy-done.20), channel_id=1, source_target_pairs={{0,8},{8,16},{16,24},{24,0},{1,9},{9,17},{17,25},{25,1},{2,10},{10... | collective-permute-start | bytes 1966088 | tf_op jit(solution)/shard_map/ppermute | solution.py:19
  391.8 57.3 %collective-permute-start.19 = (f32[5,4,64,128]{3,2,1,0:T(8,128)}, f32[5,4,64,128]{3,2,1,0:T(8,128)S(1)}, u32[]{:S(2)}, u32[]{:S(2)}) collective-permute-start(f32[5,4,64,128]{3,2,1,0:T(8,128)} %copy-done.19), channel_id=1, source_target_pairs={{0,24},{8,0},{16,8},{24,16},{1,25},{9,1},{17,9},{25,17},{2,26},{10... | collective-permute-start | bytes 1966088 | tf_op jit(solution)/shard_map/ppermute | solution.py:19
  449.1 38.0 %collective-permute-start.20 = (f32[5,4,64,128]{3,2,1,0:T(8,128)}, f32[5,4,64,128]{3,2,1,0:T(8,128)S(1)}, u32[]{:S(2)}, u32[]{:S(2)}) collective-permute-start(f32[5,4,64,128]{3,2,1,0:T(8,128)} %copy-done.17), channel_id=1, source_target_pairs={{0,16},{8,24},{16,0},{24,8},{1,17},{9,25},{17,1},{25,9},{2,18},{10... | collective-permute-start | bytes 1966088 | tf_op jit(solution)/shard_map/ppermute | solution.py:19
  449.1 38.0 %collective-permute-start.21 = (f32[5,4,64,128]{3,2,1,0:T(8,128)}, f32[5,4,64,128]{3,2,1,0:T(8,128)S(1)}, u32[]{:S(2)}, u32[]{:S(2)}) collective-permute-start(f32[5,4,64,128]{3,2,1,0:T(8,128)} %copy-done.16), channel_id=1, source_target_pairs={{0,8},{8,16},{16,24},{24,0},{1,9},{9,17},{17,25},{25,1},{2,10},{10... | collective-permute-start | bytes 1966088 | tf_op jit(solution)/shard_map/ppermute | solution.py:19
  449.1 62.1 %collective-permute-start.25 = (f32[5,4,64,128]{3,2,1,0:T(8,128)}, f32[5,4,64,128]{3,2,1,0:T(8,128)S(1)}, u32[]{:S(2)}, u32[]{:S(2)}) collective-permute-start(f32[5,4,64,128]{3,2,1,0:T(8,128)} %copy-done.18), channel_id=1, source_target_pairs={{0,24},{8,0},{16,8},{24,16},{1,25},{9,1},{17,9},{25,17},{2,26},{10... | collective-permute-start | bytes 1966088 | tf_op jit(solution)/shard_map/ppermute | solution.py:19
  487.1 115.0 %collective-permute-start.26 = (f32[5,4,64,128]{3,2,1,0:T(8,128)}, f32[5,4,64,128]{3,2,1,0:T(8,128)S(1)}, u32[]{:S(2)}, u32[]{:S(2)}) collective-permute-start(f32[5,4,64,128]{3,2,1,0:T(8,128)} %copy-done.13), channel_id=1, source_target_pairs={{0,16},{8,24},{16,0},{24,8},{1,17},{9,25},{17,1},{25,9},{2,18},{10... | collective-permute-start | bytes 1966088 | tf_op jit(solution)/shard_map/ppermute | solution.py:19
  487.1 118.6 %collective-permute-start.27 = (f32[5,4,64,128]{3,2,1,0:T(8,128)}, f32[5,4,64,128]{3,2,1,0:T(8,128)S(1)}, u32[]{:S(2)}, u32[]{:S(2)}) collective-permute-start(f32[5,4,64,128]{3,2,1,0:T(8,128)} %copy-done.11), channel_id=1, source_target_pairs={{0,8},{8,16},{16,24},{24,0},{1,9},{9,17},{17,25},{25,1},{2,10},{10... | collective-permute-start | bytes 1966088 | tf_op jit(solution)/shard_map/ppermute | solution.py:19
  511.2 101.6 %collective-permute-start.31 = (f32[5,4,64,128]{3,2,1,0:T(8,128)}, f32[5,4,64,128]{3,2,1,0:T(8,128)S(1)}, u32[]{:S(2)}, u32[]{:S(2)}) collective-permute-start(f32[5,4,64,128]{3,2,1,0:T(8,128)} %copy-done.15), channel_id=1, source_target_pairs={{0,24},{8,0},{16,8},{24,16},{1,25},{9,1},{17,9},{25,17},{2,26},{10... | collective-permute-start | bytes 1966088 | tf_op jit(solution)/shard_map/ppermute | solution.py:19
  511.2 105.2 %collective-permute-start.32 = (f32[5,4,64,128]{3,2,1,0:T(8,128)}, f32[5,4,64,128]{3,2,1,0:T(8,128)S(1)}, u32[]{:S(2)}, u32[]{:S(2)}) collective-permute-start(f32[5,4,64,128]{3,2,1,0:T(8,128)} %copy-done.14), channel_id=1, source_target_pairs={{0,16},{8,24},{16,0},{24,8},{1,17},{9,25},{17,1},{25,9},{2,18},{10... | collective-permute-start | bytes 1966088 | tf_op jit(solution)/shard_map/ppermute | solution.py:19
  528.4 91.5 %collective-permute-start.33 = (f32[5,4,64,128]{3,2,1,0:T(8,128)}, f32[5,4,64,128]{3,2,1,0:T(8,128)S(1)}, u32[]{:S(2)}, u32[]{:S(2)}) collective-permute-start(f32[5,4,64,128]{3,2,1,0:T(8,128)} %copy-done.12), channel_id=1, source_target_pairs={{0,8},{8,16},{16,24},{24,0},{1,9},{9,17},{17,25},{25,1},{2,10},{10... | collective-permute-start | bytes 1966088 | tf_op jit(solution)/shard_map/ppermute | solution.py:19
  (15 other events, 12.3 us)
Sparse Core Ops, SparseCore 0:
  29.0 38.8 all-gather.2

commit v2 on v1

--- a/solution.py
+++ b/solution.py
@@ -1,4 +1,5 @@
 import functools
+import math
 
 import jax
 import jax.numpy as jnp
@@ -17,6 +18,16 @@
 def shift(values, axis, step):
     count = lax.axis_size(axis)
     return lax.ppermute(values, axis, [(i, (i + step) % count) for i in range(count)])
+
+
+def after(values, *earlier):
+    return lax.optimization_barrier((values, earlier))[0]
+
+
+def order_of_steps(count):
+    pairs = [(s, count - s) for s in range(1, (count + 1) // 2)]
+    middle = [count // 2] if count % 2 == 0 and count > 1 else []
+    return [s for pair in pairs for s in pair] + middle
 
 
 def flux_pieces(values, direction):
@@ -82,6 +93,62 @@
         ),
         name="wall_part",
     )(place, conserved, *received, matrix)
+
+
+def inlet_kernel(table_ref, slot_ref, column_ref, gain_ref, out_ref, split):
+    slots, fields, lines, lanes = table_ref.shape
+    height = slots * lines
+
+    @pl.when(pl.program_id(0) == 0)
+    def _():
+        for f in range(fields):
+            rest = table_ref[:, f].reshape(height, lanes)
+            for k in range(3):
+                piece = rest.astype(jnp.bfloat16)
+                split[k * fields + f] = piece.T
+                rest = rest - piece.astype(jnp.float32)
+
+    width = slot_ref.shape[1]
+    column = column_ref[...]
+    line = slot_ref[...] * lines + column // lanes
+    choice = jnp.where(
+        lax.broadcasted_iota(jnp.int32, (height, width), 0) == line, 1.0, 0.0
+    ).astype(jnp.bfloat16)
+    lane = lax.broadcasted_iota(jnp.int32, (lanes, width), 0) == column % lanes
+    for f in range(fields):
+        total = jnp.zeros((lanes, width), jnp.float32)
+        for k in (2, 1, 0):
+            total += jnp.dot(split[k * fields + f], choice, preferred_element_type=jnp.float32)
+        picked = jnp.sum(jnp.where(lane, total, 0.0), axis=0, keepdims=True)
+        out_ref[f : f + 1, :] = picked * gain_ref[f]
+
+
+def inlet_part(table, slot, column, gain):
+    slots, fields, lines, lanes = table.shape
+    height = slots * lines
+    columns = column.shape[1]
+    width = math.gcd(columns, 512)
+    row = pl.BlockSpec((1, width), lambda i: (0, i))
+    return pl.pallas_call(
+        inlet_kernel,
+        out_shape=jax.ShapeDtypeStruct((fields, columns), jnp.float32),
+        grid=(columns // width,),
+        in_specs=[
+            pl.BlockSpec(table.shape, lambda i: (0, 0, 0, 0)),
+            row,
+            row,
+            pl.BlockSpec(memory_space=pltpu.SMEM),
+        ],
+        out_specs=pl.BlockSpec((fields, width), lambda i: (0, i)),
+        scratch_shapes=[pltpu.VMEM((3 * fields, lanes, height), jnp.bfloat16)],
+        compiler_params=pltpu.CompilerParams(vmem_limit_bytes=vmem_limit),
+        cost_estimate=pl.CostEstimate(
+            flops=6 * fields * lanes * height * columns,
+            bytes_accessed=4 * table.size,
+            transcendentals=0,
+        ),
+        name="inlet_part",
+    )(table, slot, column, gain)
 
 
 def local_kernel(
@@ -177,15 +244,18 @@
 
 def close_part(place, current, partial, term, group, offset):
     fields, part, rows, cells = term.shape
-    block = (fields, 1, rows, cells)
-    there = pl.BlockSpec(block, lambda i, place: (0, place[0] * group + offset + i, 0, 0))
+    step = math.gcd(part, 4)
+    block = (fields, step, rows, cells)
+    there = pl.BlockSpec(
+        block, lambda i, place: (0, (place[0] * group + offset) // step + i, 0, 0)
+    )
     shape = jax.ShapeDtypeStruct(current.shape, jnp.float32)
     return pl.pallas_call(
         close_kernel,
         out_shape=[shape, shape],
         grid_spec=pltpu.PrefetchScalarGridSpec(
             num_scalar_prefetch=1,
-            grid=(part,),
+            grid=(part // step,),
             in_specs=[there, there, pl.BlockSpec(block, lambda i, place: (0, i, 0, 0))],
             out_specs=[there, there],
         ),
@@ -234,74 +304,102 @@
     across = lax.axis_size("pz")
     row = lax.axis_index("py")
     group = span // count
-    parts = min(4, group)
+    parts = min(2, group)
     part = group // parts
     width = span_blocks.shape[2]
+    steps = order_of_steps(count)
     place = lambda s: jnp.reshape((row + s) % count, (1,)).astype(jnp.int32)
 
-    def outgoing(source, c):
-        sent = []
-        for s in range(1, count):
-            start = ((row + s) % count) * group + c * part
-            piece = lax.dynamic_slice_in_dim(source, start, part, 1)
-            sent.append(shift(piece, "py", s))
-        return sent
-
-    received = [outgoing(conserved, 0)]
-
-    recycle = conserved[:, :, :, 3 * cells // 4].reshape(-1, 128)
-    recycle, later = lax.optimization_barrier((recycle, conserved))
-    along = [recycle] + [shift(recycle, "py", s) for s in range(1, count)]
-    for c in range(1, parts):
-        received.append(outgoing(later, c))
-    after = shift(later[:, :width], "pz", -1)
-    before = shift(later[:, span - width :], "pz", 1)
-
-    stacked = jnp.stack(along)
-    whole_plane = lax.all_gather(stacked, "pz", axis=0)
-    whole_plane = whole_plane.reshape(across, count, fields, columns)
-    whole_plane = jnp.transpose(whole_plane, (2, 0, 1, 3)).reshape(fields, -1)
+    def outgoing(source, c, s):
+        start = ((row - s) % count) * group + c * part
+        return lax.dynamic_slice_in_dim(source, start, part, 1)
+
+    first = {s: outgoing(conserved, 0, s) for s in steps}
+    early, late = steps[:2], steps[2:]
+    received = [{s: shift(first[s], "py", -s) for s in early}, {}]
+
+    behind = after(conserved, *[first[s] for s in early])
+    recycle = behind[:, :, :, 3 * cells // 4].reshape(-1, 128)
+    along = [recycle] + [shift(recycle, "py", -s) for s in range(1, count)]
+    rest = after(conserved, recycle)
+    second = {s: outgoing(rest, parts - 1, s) for s in steps}
+    head, tail = after((rest[:, :width], rest[:, span - width :]), *along)
+    for s in late:
+        received[0][s] = shift(after(first[s], received[0][early[0]]), "py", -s)
+    waits = [received[0][s] for s in steps[1:]]
+    for s, wait in zip(steps, waits + [waits[-1]] * count):
+        received[1][s] = shift(after(second[s], wait), "py", -s)
+    halo_after = shift(head, "pz", -1)
+    halo_before = shift(tail, "pz", 1)
+
+    table = lax.all_gather(jnp.stack(along), "pz", axis=0).reshape(across * count, fields, -1, 128)
     myself = lax.axis_index(("py", "pz"))
-    own_block = lax.dynamic_index_in_dim(source_block[:, :, 0], myself, 0, keepdims=False)
-    own_column = lax.dynamic_index_in_dim(source_column, myself, 0, keepdims=False)
-    slot = (own_block % across) * count + (row - own_block // across) % count
-    fetched = jnp.take(whole_plane, slot * columns + own_column, axis=1)
-    inlet = (fetched * inflow_gain[:, None]).reshape(fields, span, rows)
+    own_block = lax.dynamic_slice_in_dim(source_block[:, :, 0], myself, 1, 0)
+    own_column = lax.dynamic_slice_in_dim(source_column, myself, 1, 0)
+    slot = (own_block % across) * count + (own_block // across - row) % count
+
+    twice = jnp.concatenate([wall_matrix, wall_matrix], axis=0)
+    twice = lax.dynamic_slice_in_dim(twice, row * rows, count * rows, 0)
+    twice = jnp.concatenate([twice, twice], axis=1)
+    matrix = lax.dynamic_slice_in_dim(twice, row * rows, count * rows, 1)
+
+    returned = [{}, {}]
+    pieces = wall_part(
+        place(0), conserved, [received[0][s] for s in range(1, count)], matrix, 0, part
+    )
+    returned[0][0] = pieces[0]
+    waits = [received[1][s] for s in steps]
+    for s, wait in zip(steps, waits[:-1] + [waits[-2]] * count):
+        returned[0][s] = shift(after(pieces[s], wait), "py", s)
+
+    inlet = inlet_part(table, slot, own_column, inflow_gain).reshape(fields, span, rows)
 
     inlet_after = shift(inlet[:, :width], "pz", -1)
     inlet_before = shift(inlet[:, span - width :], "pz", 1)
-    lines = jnp.stack([inlet] + [shift(inlet, "py", s) for s in range(1, count)])
-    order = (row - jnp.arange(count)) % count
-    squares = wall_matrix.reshape(count, rows, count, rows)
-    squares = jnp.take(jnp.take(squares, order, axis=0), order, axis=2)
-    matrix = squares.reshape(wall_matrix.shape)
+    flat = inlet.reshape(-1, 128)
+    lines = lax.all_to_all(
+        jnp.broadcast_to(flat, (count,) + flat.shape), "py", split_axis=0, concat_axis=0
+    )
+    lines = lines.reshape(count, fields, span, rows)
     line_flux = jnp.stack(flux_pieces([lines[:, f] for f in range(fields)], 1))
-    edge = jnp.einsum("asb,fszb->faz", squares[0], line_flux, precision=highest)
+    own_rows = lax.dynamic_slice_in_dim(wall_matrix, row * rows, rows, 0)
+    edge = jnp.einsum(
+        "asb,fszb->faz", own_rows.reshape(rows, count, rows), line_flux, precision=highest
+    )
     inlet_wide = jnp.concatenate([inlet_before, inlet, inlet_after], axis=1).swapaxes(1, 2)
 
     local_blocks = span // width
     own_blocks = lax.dynamic_slice_in_dim(
         span_blocks, lax.axis_index("pz") * local_blocks, local_blocks, 0
     )
+
+    pieces = wall_part(
+        place(0),
+        conserved,
+        [received[1][s] for s in range(1, count)],
+        matrix,
+        (parts - 1) * part,
+        part,
+    )
+    returned[1][0] = pieces[0]
+    waits = [returned[0][s] for s in steps]
+    for s, wait in zip(steps, waits[:-1] + [waits[-2]] * count):
+        returned[1][s] = shift(after(pieces[s], wait), "py", s)
+
     current, partial = local_part(
         conserved,
-        before,
-        after,
+        halo_before,
+        halo_after,
         register,
         inlet_wide,
         edge,
         span_band(own_blocks),
         stream_weights(stream_blocks),
     )
-
-    returned = []
     for c in range(parts):
-        pieces = wall_part(place(0), conserved, received[c], matrix, c * part, part)
-        returned.append([pieces[0]] + [shift(pieces[s], "py", -s) for s in range(1, count)])
-    for c in range(parts):
-        for s in range(count):
+        for s in [0] + steps:
             current, partial = close_part(
-                place(s), current, partial, returned[c][s], group, c * part
+                place(-s), current, partial, returned[c][s], group, c * part
             )
     return (current, partial)
 

time: 633 us -> 518 us (0.82)
  waiting for transfers between devices: 122 us -> 245 us
  local copies, waits for them, and re-layouts: 164 us -> 42.2 us
  starting transfers between devices: 208 us -> 111 us
  Pallas kernels: 112 us -> 101 us
    ppermute x34 -> x19, waiting for transfers between devices: 122 us -> 245 us  [shift(): lax.ppermute(values, axis, [(i, (i + step) % count) for i in range(count)])]
    ppermute x34 -> x19, starting transfers between devices: 208 us -> 107 us  [shift(): lax.ppermute(values, axis, [(i, (i + step) % count) for i in range(count)])]
    gather x7 -> x0, local copies, waits for them, and re-layouts: 71.7 us -> none  [the longest x3 65.4 us: local(): fetched = jnp.take(whole_plane, slot * columns + own_column, axis=1)]
    pallas_call x16 -> x8, Pallas kernels: 57.2 us -> 24.9 us  [close_part(): pl.pallas_call(close_kernel, out_shape=[shape, shape], grid_spec=pltpu.Pr...]
    transpose x1 -> x0, local copies, waits for them, and re-layouts: 31 us -> none  [local(): whole_plane = jnp.transpose(whole_plane, (2, 0, 1, 3)).reshape(fields, -1)]
    pallas_call x0 -> x1, Pallas kernels: none -> 20 us  [inlet_part(): pl.pallas_call(inlet_kernel, out_shape=jax.ShapeDtypeStruct((fields, colu...]
    unnamed x58 -> x20, local copies, waits for them, and re-layouts: 17.6 us -> 6.22 us
    pallas_call x4 -> x2, Pallas kernels: 19 us -> 19.9 us  [wall_part(): pl.pallas_call(functools.partial(wall_kernel, count, fields), out_shape=[...]
  transfers between devices with their start and end apart: 35 -> 21, of which waited for: 9 -> 9; matrix products, arithmetic and copies ran while one was open for 23% -> 5% of each run, Pallas kernels for 17% -> 19%
where the time goes in v2:
time: 518 us; the launch traced here: 517 us
  waiting for transfers between devices  245 us (47%)
  starting transfers between devices  111 us (21%)
  Pallas kernels  101 us (19%)
  local copies, waits for them, and re-layouts  42.2 us (8%)
  between operations  14.4 us (3%)
    ppermute x19, waiting for transfers between devices, shift(): lax.ppermute(values, axis, [(i, (i + step) % count) for i in range(count)])  245 us
    ppermute x19, starting transfers between devices, shift(): lax.ppermute(values, axis, [(i, (i + step) % count) for i in range(count)])  107 us
    pallas_call x1, Pallas kernels, local_part(): pl.pallas_call(functools.partial(local_kernel, halo), out_shape=[shape, s...  36.3 us
    pallas_call x8, Pallas kernels, close_part(): pl.pallas_call(close_kernel, out_shape=[shape, shape], grid_spec=pltpu.Pr...  24.9 us
    pallas_call x1, Pallas kernels, inlet_part(): pl.pallas_call(inlet_kernel, out_shape=jax.ShapeDtypeStruct((fields, colu...  20 us
    pallas_call x2, Pallas kernels, wall_part(): pl.pallas_call(functools.partial(wall_kernel, count, fields), out_shape=[...  19.9 us
  transfers between devices with their start and end apart: 21, of which 9 were waited for; matrix products, arithmetic and copies ran while one was open for 5% of the time, Pallas kernels for 19%

profile of v2, /device:TPU:0, one launch (start us, length us, event | category | flops | bytes accessed | tf_op | source)
XLA Modules:
  0.0 517.1 jit_solution(139767161587757843)
XLA Ops:
  7.3 3.5 constant_dynamic-slice_fusion.3
  10.8 9.5 %slice_reduce_fusion = f32[5,64,64]{2,1,0:T(8,128)S(1)} fusion(f32[5,64,64,128]{3,2,1,0:T(8,128)} %own_ref.3), kind=kLoop, calls=%fused_computation | loop fusion | bytes 163840 | tf_op jit(solution)/shard_map/slice | solution.py:322
  20.4 5.1 collective-permute-start
  25.5 1.0 collective-permute-start.2
  26.6 1.7 collective-permute-done
  28.3 4.7 collective-permute-done.1
  33.8 2.2 collective-permute-start.7
  36.0 29.8 %collective-permute-done.7.refs_0_ = f32[5,8,64,128]{3,2,1,0:T(8,128)S(1)} collective-permute-done((f32[5,8,64,128]{3,2,1,0:T(8,128)}, f32[5,8,64,128]{3,2,1,0:T(8,128)S(1)}, u32[]{:S(2)}, u32[]{:S(2)}) %collective-permute-start.7) | collective-permute-done | bytes 1310752 | tf_op jit(solution)/shard_map/ppermute | solution.py:20
  65.8 1.1 copy-done.8
  66.8 2.1 collective-permute-start.8
  68.9 10.3 %fusion.19 = (f32[5,32,64,128]{3,2,1,0:T(8,128)}, f32[5,32,64,128]{3,2,1,0:T(8,128)}) fusion(f32[5,64,64,128]{3,2,1,0:T(8,128)} %own_ref.3), kind=kLoop, calls=%fused_computation.59 | loop fusion | bytes 20971520 | tf_op jit(solution)/shard_map/slice | solution.py:326
  79.3 2.6 collective-permute-start.4
  81.9 4.3 constant_dynamic-slice_fusion
  86.2 9.4 %collective-permute-done.9.refs_2_ = f32[5,8,64,128]{3,2,1,0:T(8,128)} collective-permute-done((f32[5,8,64,128]{3,2,1,0:T(8,128)S(1)}, f32[5,8,64,128]{3,2,1,0:T(8,128)}, u32[]{:S(2)}, u32[]{:S(2)}) %collective-permute-start.9) | collective-permute-done | bytes 1310752 | tf_op jit(solution)/shard_map/ppermute | solution.py:20
  95.6 54.1 %collective-permute-done.8.refs_1_ = f32[5,8,64,128]{3,2,1,0:T(8,128)} collective-permute-done((f32[5,8,64,128]{3,2,1,0:T(8,128)S(1)}, f32[5,8,64,128]{3,2,1,0:T(8,128)}, u32[]{:S(2)}, u32[]{:S(2)}) %collective-permute-start.8) | collective-permute-done | bytes 1310752 | tf_op jit(solution)/shard_map/ppermute | solution.py:20
  149.7 26.4 %collective-permute-start.12 = (f32[5,8,64,128]{3,2,1,0:T(8,128)}, f32[5,8,64,128]{3,2,1,0:T(8,128)}, u32[]{:S(2)}, u32[]{:S(2)}) collective-permute-start(f32[5,8,64,128]{3,2,1,0:T(8,128)} %get-tuple-element.56), channel_id=1, source_target_pairs={{0,8},{8,16},{16,24},{24,0},{1,9},{9,17},{17,25},{25,1},{2,10},{10... | collective-permute-start | bytes 3932168 | tf_op jit(solution)/shard_map/ppermute | solution.py:20
  177.0 0.8 dynamic-slice_bitcast_fusion
  177.8 0.9 dynamic_update_slice.19
  178.8 0.9 dynamic_update_slice.20
  182.5 1.1 fusion.14
  183.6 10.3 %wall_part.2 = (f32[5,8,64,128]{3,2,1,0:T(8,128)S(1)}, f32[5,8,64,128]{3,2,1,0:T(8,128)}, f32[5,8,64,128]{3,2,1,0:T(8,128)}, f32[5,8,64,128]{3,2,1,0:T(8,128)}) custom-call(s32[1]{0:T(128)} %bitcast.3.place_ref, f32[5,64,64,128]{3,2,1,0:T(8,128)} %own_ref.3, f32[5,8,64,128]{3,2,1,0:T(8,128)} %copy-done.8, f32[5,8,64,128]{3,2,1,0:T(8,128)} %collective-permute-done.8.refs_1_, ...), custom_call_target="tpu_custom_call" | custom-call | flops 4026531840 | bytes 10485760 | tf_op jit(solution)/shard_map/wall_part/pallas_call | solution.py:77
  193.9 3.6 collective-permute-start.15
  197.5 11.6 %collective-permute-done.12.refs_2_ = f32[5,8,64,128]{3,2,1,0:T(8,128)} collective-permute-done((f32[5,8,64,128]{3,2,1,0:T(8,128)}, f32[5,8,64,128]{3,2,1,0:T(8,128)}, u32[]{:S(2)}, u32[]{:S(2)}) %collective-permute-start.12) | collective-permute-done | bytes 1310752 | tf_op jit(solution)/shard_map/ppermute | solution.py:20
  209.1 2.0 collective-permute-start.13
  211.0 1.7 copy-done.2
  212.8 20.0 %inlet_part.1 = f32[5,4096]{1,0:T(8,128)S(1)} custom-call(f32[32,5,32,128]{3,2,1,0:T(8,128)S(1)} %bitcast.110, s32[1,4096]{1,0:T(1,128)S(1)} %get-tuple-element.98.slot_ref, s32[1,4096]{1,0:T(1,128)S(1)} %get-tuple-element.99.column_ref, f32[5]{0:T(128)S(1)} %copy-done.5), custom_call_target="tpu_custom_call" | custom-call | flops 16106127360 | bytes 2621440 | tf_op jit(solution)/shard_map/inlet_part/pallas_call | solution.py:132
  233.6 4.1 all-to-all-start
  238.0 55.4 %collective-permute-done.15.refs_1_ = f32[5,8,64,128]{3,2,1,0:T(8,128)} collective-permute-done((f32[5,8,64,128]{3,2,1,0:T(8,128)}, f32[5,8,64,128]{3,2,1,0:T(8,128)}, u32[]{:S(2)}, u32[]{:S(2)}) %collective-permute-start.15) | collective-permute-done | bytes 1310752 | tf_op jit(solution)/shard_map/ppermute | solution.py:20
  293.4 1.9 collective-permute-start.6
  295.3 9.7 %wall_part.3 = (f32[5,8,64,128]{3,2,1,0:T(8,128)S(1)}, f32[5,8,64,128]{3,2,1,0:T(8,128)}, f32[5,8,64,128]{3,2,1,0:T(8,128)S(1)}, f32[5,8,64,128]{3,2,1,0:T(8,128)S(1)}) custom-call(s32[1]{0:T(128)} %bitcast.3.place_ref, f32[5,64,64,128]{3,2,1,0:T(8,128)} %own_ref.3, f32[5,8,64,128]{3,2,1,0:T(8,128)} %collective-permute-done.10.refs_0_, ...), custom_call_target="tpu_custom_call" | custom-call | flops 4026531840 | bytes 10485760 | tf_op jit(solution)/shard_map/wall_part/pallas_call | solution.py:77
  305.0 1.1 copy-done
  306.1 1.1 copy-done.3
  307.2 1.1 copy-done.4
  308.3 58.3 %collective-permute-start.16 = (f32[5,8,64,128]{3,2,1,0:T(8,128)}, f32[5,8,64,128]{3,2,1,0:T(8,128)}, u32[]{:S(2)}, u32[]{:S(2)}) collective-permute-start(f32[5,8,64,128]{3,2,1,0:T(8,128)} %get-tuple-element.69), channel_id=1, source_target_pairs={{0,8},{8,16},{16,24},{24,0},{1,9},{9,17},{17,25},{25,1},{2,10},{10... | collective-permute-start | bytes 3932168 | tf_op jit(solution)/shard_map/ppermute | solution.py:20
  366.8 1.1 reshape.397
  368.2 1.4 collective-permute-start.18
  369.7 0.9 convolution_bitcast_fusion.edge_ref
  370.6 36.3 %local_part.1 = (f32[5,64,64,128]{3,2,1,0:T(8,128)}, f32[5,64,64,128]{3,2,1,0:T(8,128)}) custom-call(f32[5,64,64,128]{3,2,1,0:T(8,128)} %own_ref.3, f32[5,32,64,128]{3,2,1,0:T(8,128)} %collective-permute-done.3.before_ref, f32[5,32,64,128]{3,2,1,0:T(8,128)} %collective-permute-done.4.after_ref, f32[5,64,64,128]{3,2,1,0:T(8,128)} %reg_ref.1, ...), custom_call_target="tpu_custom_call" | custom-call | flops 8053063680 | bytes 52428800 | tf_op jit(solution)/shard_map/local_part/pallas_call | solution.py:217
  406.9 3.0 close_part.8
  409.9 3.0 close_part.9
  412.9 3.4 close_part.10
  416.2 3.4 close_part.11
  419.7 3.0 close_part.12
  422.6 1.5 collective-permute-done.16.term_ref
  424.2 3.3 close_part.13
  427.5 3.0 close_part.14
  430.4 76.9 %collective-permute-done.18.term_ref = f32[5,8,64,128]{3,2,1,0:T(8,128)S(1)} collective-permute-done((f32[5,8,64,128]{3,2,1,0:T(8,128)}, f32[5,8,64,128]{3,2,1,0:T(8,128)S(1)}, u32[]{:S(2)}, u32[]{:S(2)}) %collective-permute-start.18) | collective-permute-done | bytes 1310752 | tf_op jit(solution)/shard_map/ppermute | solution.py:20
  507.4 2.9 close_part.15
  (60 shorter events, 6.2 us)
Async XLA Ops:
  7.2 203.9 %all-gather.3.cloned.1.call-start = ((), (), s32[]{:S(2)}) async-start(), calls=%async_computation.1 | async-start | bytes 2949120 | tf_op jit(solution)/shard_map/all_gather | solution.py:335
  20.4 8.0 %collective-permute-start = (f32[160,128]{1,0:T(8,128)S(1)}, f32[160,128]{1,0:T(8,128)S(1)}, u32[]{:S(2)}, u32[]{:S(2)}) collective-permute-start(f32[160,128]{1,0:T(8,128)S(1)} %reshape_squeeze.3), channel_id=1, source_target_pairs={{0,24},{8,0},{16,8},{24,16},{1,25},{9,1},{17,9},{25,17},{2,26},{10... | collective-permute-start | bytes 245768 | tf_op jit(solution)/shard_map/ppermute | solution.py:20
  25.5 7.5 %collective-permute-start.1 = (f32[160,128]{1,0:T(8,128)S(1)}, f32[160,128]{1,0:T(8,128)S(1)}, u32[]{:S(2)}, u32[]{:S(2)}) collective-permute-start(f32[160,128]{1,0:T(8,128)S(1)} %reshape_squeeze.3), channel_id=1, source_target_pairs={{0,16},{8,24},{16,0},{24,8},{1,17},{9,25},{17,1},{25,9},{2,18},{10... | collective-permute-start | bytes 245768 | tf_op jit(solution)/shard_map/ppermute | solution.py:20
  25.5 7.5 %collective-permute-start.2 = (f32[160,128]{1,0:T(8,128)S(1)}, f32[160,128]{1,0:T(8,128)S(1)}, u32[]{:S(2)}, u32[]{:S(2)}) collective-permute-start(f32[160,128]{1,0:T(8,128)S(1)} %reshape_squeeze.3), channel_id=1, source_target_pairs={{0,8},{8,16},{16,24},{24,0},{1,9},{9,17},{17,25},{25,1},{2,10},{10... | collective-permute-start | bytes 245768 | tf_op jit(solution)/shard_map/ppermute | solution.py:20
  33.8 32.0 %collective-permute-start.7 = (f32[5,8,64,128]{3,2,1,0:T(8,128)}, f32[5,8,64,128]{3,2,1,0:T(8,128)S(1)}, u32[]{:S(2)}, u32[]{:S(2)}) collective-permute-start(f32[5,8,64,128]{3,2,1,0:T(8,128)} %get-tuple-element.87), channel_id=1, source_target_pairs={{0,24},{8,0},{16,8},{24,16},{1,25},{9,1},{17,9},{25,17},{2,26},{10... | collective-permute-start | bytes 3932168 | tf_op jit(solution)/shard_map/ppermute | solution.py:20
  36.0 59.6 %collective-permute-start.9 = (f32[5,8,64,128]{3,2,1,0:T(8,128)S(1)}, f32[5,8,64,128]{3,2,1,0:T(8,128)}, u32[]{:S(2)}, u32[]{:S(2)}) collective-permute-start(f32[5,8,64,128]{3,2,1,0:T(8,128)S(1)} %get-tuple-element.86), channel_id=1, source_target_pairs={{0,8},{8,16},{16,24},{24,0},{1,9},{9,17},{17,25},{25,1},{2,10},{10... | collective-permute-start | bytes 3932168 | tf_op jit(solution)/shard_map/ppermute | solution.py:20
  65.8 1.1 copy-start.8
  66.8 82.9 %collective-permute-start.8 = (f32[5,8,64,128]{3,2,1,0:T(8,128)S(1)}, f32[5,8,64,128]{3,2,1,0:T(8,128)}, u32[]{:S(2)}, u32[]{:S(2)}) collective-permute-start(f32[5,8,64,128]{3,2,1,0:T(8,128)S(1)} %get-tuple-element.46), channel_id=1, source_target_pairs={{0,16},{8,24},{16,0},{24,8},{1,17},{9,25},{17,1},{25,9},{2,18},{10... | collective-permute-start | bytes 3932168 | tf_op jit(solution)/shard_map/ppermute | solution.py:20
  79.3 288.9 %collective-permute-start.3 = (f32[5,32,64,128]{3,2,1,0:T(8,128)}, f32[5,32,64,128]{3,2,1,0:T(8,128)}, u32[]{:S(2)}, u32[]{:S(2)}) collective-permute-start(f32[5,32,64,128]{3,2,1,0:T(8,128)} %get-tuple-element.42), channel_id=1, source_target_pairs={{0,1},{1,2},{2,3},{3,4},{4,5},{5,6},{6,7},{7,0},{8,9},{9,10},{10,1... | collective-permute-start | bytes 15728648 | tf_op jit(solution)/shard_map/ppermute | solution.py:20
  79.3 291.3 %collective-permute-start.4 = (f32[5,32,64,128]{3,2,1,0:T(8,128)}, f32[5,32,64,128]{3,2,1,0:T(8,128)}, u32[]{:S(2)}, u32[]{:S(2)}) collective-permute-start(f32[5,32,64,128]{3,2,1,0:T(8,128)} %get-tuple-element.43), channel_id=1, source_target_pairs={{0,7},{1,0},{2,1},{3,2},{4,3},{5,4},{6,5},{7,6},{8,15},{9,8},{10,9... | collective-permute-start | bytes 15728648 | tf_op jit(solution)/shard_map/ppermute | solution.py:20
  81.9 94.2 %copy-start.7 = (f32[256,256]{1,0:T(8,128)S(1)}, f32[256,256]{1,0:T(8,128)}, u32[]{:S(2)}) copy-start(f32[256,256]{1,0:T(8,128)} %param.11) | copy-start | bytes 786436
  81.9 95.0 %slice-start = ((f32[1,3,128,128]{3,2,1,0:T(8,128)}), f32[1,1,128,128]{3,2,1,0:T(8,128)S(1)}, s32[]{:S(2)}) async-start(f32[1,3,128,128]{3,2,1,0:T(8,128)} %param.10), calls=%async_computation.2 | async-start | bytes 131072 | tf_op jit(solution)/shard_map/slice | solution.py:278
  95.6 98.3 %collective-permute-start.10 = (f32[5,8,64,128]{3,2,1,0:T(8,128)}, f32[5,8,64,128]{3,2,1,0:T(8,128)}, u32[]{:S(2)}, u32[]{:S(2)}) collective-permute-start(f32[5,8,64,128]{3,2,1,0:T(8,128)} %get-tuple-element.51), channel_id=1, source_target_pairs={{0,24},{8,0},{16,8},{24,16},{1,25},{9,1},{17,9},{25,17},{2,26},{10... | collective-permute-start | bytes 3932168 | tf_op jit(solution)/shard_map/ppermute | solution.py:20
  149.7 59.3 %collective-permute-start.12 = (f32[5,8,64,128]{3,2,1,0:T(8,128)}, f32[5,8,64,128]{3,2,1,0:T(8,128)}, u32[]{:S(2)}, u32[]{:S(2)}) collective-permute-start(f32[5,8,64,128]{3,2,1,0:T(8,128)} %get-tuple-element.56), channel_id=1, source_target_pairs={{0,8},{8,16},{16,24},{24,0},{1,9},{9,17},{17,25},{25,1},{2,10},{10... | collective-permute-start | bytes 3932168 | tf_op jit(solution)/shard_map/ppermute | solution.py:20
  183.6 27.4 %copy-start.5 = (f32[5]{0:T(128)S(1)}, f32[5]{0:T(128)}, u32[]{:S(2)}) copy-start(f32[5]{0:T(128)} %gain_ref.1) | copy-start | bytes 64
  193.9 44.1 %collective-permute-start.11 = (f32[5,8,64,128]{3,2,1,0:T(8,128)}, f32[5,8,64,128]{3,2,1,0:T(8,128)S(1)}, u32[]{:S(2)}, u32[]{:S(2)}) collective-permute-start(f32[5,8,64,128]{3,2,1,0:T(8,128)} %get-tuple-element.52), channel_id=1, source_target_pairs={{0,8},{8,16},{16,24},{24,0},{1,9},{9,17},{17,25},{25,1},{2,10},{10... | collective-permute-start | bytes 3932168 | tf_op jit(solution)/shard_map/ppermute | solution.py:20
  193.9 99.5 %collective-permute-start.15 = (f32[5,8,64,128]{3,2,1,0:T(8,128)}, f32[5,8,64,128]{3,2,1,0:T(8,128)}, u32[]{:S(2)}, u32[]{:S(2)}) collective-permute-start(f32[5,8,64,128]{3,2,1,0:T(8,128)} %get-tuple-element.64), channel_id=1, source_target_pairs={{0,16},{8,24},{16,0},{24,8},{1,17},{9,25},{17,1},{25,9},{2,18},{10... | collective-permute-start | bytes 3932168 | tf_op jit(solution)/shard_map/ppermute | solution.py:20
  209.1 159.0 %collective-permute-start.13 = (f32[5,8,64,128]{3,2,1,0:T(8,128)}, f32[5,8,64,128]{3,2,1,0:T(8,128)}, u32[]{:S(2)}, u32[]{:S(2)}) collective-permute-start(f32[5,8,64,128]{3,2,1,0:T(8,128)} %get-tuple-element.57), channel_id=1, source_target_pairs={{0,24},{8,0},{16,8},{24,16},{1,25},{9,1},{17,9},{25,17},{2,26},{10... | collective-permute-start | bytes 3932168 | tf_op jit(solution)/shard_map/ppermute | solution.py:20
  211.0 1.7 copy-start.2
  233.6 133.1 %all-to-all-start = ((f32[4,160,128]{2,1,0:T(8,128)}), f32[4,160,128]{2,1,0:T(8,128)}, u32[]{:S(2)}, u32[]{:S(2)}) async-start(f32[4,160,128]{2,1,0:T(8,128)} %broadcast_in_dim.4), calls=%async_computation | async-start | bytes 655360 | tf_op jit(solution)/shard_map/all_to_all | solution.py:360
  238.0 70.3 %collective-permute-start.5 = (f32[5,32,64]{1,2,0:T(8,128)S(1)}, f32[5,32,64]{1,2,0:T(8,128)S(1)}, u32[]{:S(2)}, u32[]{:S(2)}) collective-permute-start(f32[5,32,64]{1,2,0:T(8,128)S(1)} %get-tuple-element.96), channel_id=1, source_target_pairs={{0,1},{1,2},{2,3},{3,4},{4,5},{5,6},{6,7},{7,0},{8,9},{9,10},{10,1... | collective-permute-start | bytes 122888 | tf_op jit(solution)/shard_map/ppermute | solution.py:20
  293.4 14.9 %collective-permute-start.6 = (f32[5,32,64]{1,2,0:T(8,128)S(1)}, f32[5,32,64]{1,2,0:T(8,128)S(1)}, u32[]{:S(2)}, u32[]{:S(2)}) collective-permute-start(f32[5,32,64]{1,2,0:T(8,128)S(1)} %get-tuple-element.97), channel_id=1, source_target_pairs={{0,7},{1,0},{2,1},{3,2},{4,3},{5,4},{6,5},{7,6},{8,15},{9,8},{10,9... | collective-permute-start | bytes 122888 | tf_op jit(solution)/shard_map/ppermute | solution.py:20
  305.0 1.1 copy-start
  306.0 1.1 copy-start.3
  307.2 1.1 copy-start.4
  308.3 107.9 %collective-permute-start.14 = (f32[5,8,64,128]{3,2,1,0:T(8,128)}, f32[5,8,64,128]{3,2,1,0:T(8,128)}, u32[]{:S(2)}, u32[]{:S(2)}) collective-permute-start(f32[5,8,64,128]{3,2,1,0:T(8,128)} %get-tuple-element.61), channel_id=1, source_target_pairs={{0,16},{8,24},{16,0},{24,8},{1,17},{9,25},{17,1},{25,9},{2,18},{10... | collective-permute-start | bytes 3932168 | tf_op jit(solution)/shard_map/ppermute | solution.py:20
  308.3 115.9 %collective-permute-start.16 = (f32[5,8,64,128]{3,2,1,0:T(8,128)}, f32[5,8,64,128]{3,2,1,0:T(8,128)}, u32[]{:S(2)}, u32[]{:S(2)}) collective-permute-start(f32[5,8,64,128]{3,2,1,0:T(8,128)} %get-tuple-element.69), channel_id=1, source_target_pairs={{0,8},{8,16},{16,24},{24,0},{1,9},{9,17},{17,25},{25,1},{2,10},{10... | collective-permute-start | bytes 3932168 | tf_op jit(solution)/shard_map/ppermute | solution.py:20
  367.9 1.7 copy-start.6
  368.1 59.4 %collective-permute-start.17 = (f32[5,8,64,128]{3,2,1,0:T(8,128)}, f32[5,8,64,128]{3,2,1,0:T(8,128)S(1)}, u32[]{:S(2)}, u32[]{:S(2)}) collective-permute-start(f32[5,8,64,128]{3,2,1,0:T(8,128)} %copy-done.4), channel_id=1, source_target_pairs={{0,24},{8,0},{16,8},{24,16},{1,25},{9,1},{17,9},{25,17},{2,26},{10... | collective-permute-start | bytes 3932168 | tf_op jit(solution)/shard_map/ppermute | solution.py:20
  368.2 139.2 %collective-permute-start.18 = (f32[5,8,64,128]{3,2,1,0:T(8,128)}, f32[5,8,64,128]{3,2,1,0:T(8,128)S(1)}, u32[]{:S(2)}, u32[]{:S(2)}) collective-permute-start(f32[5,8,64,128]{3,2,1,0:T(8,128)} %copy-done.3), channel_id=1, source_target_pairs={{0,16},{8,24},{16,0},{24,8},{1,17},{9,25},{17,1},{25,9},{2,18},{10... | collective-permute-start | bytes 3932168 | tf_op jit(solution)/shard_map/ppermute | solution.py:20
  416.2 3.4 copy-start.1
Sparse Core Ops, SparseCore 0:
  33.9 29.8 all-gather.2

commit v3 on v2

--- a/solution.py
+++ b/solution.py
@@ -13,6 +13,7 @@
 section_gain = 15.0 / 16.0
 time_step = 0.1
 vmem_limit = 48 * 1024 * 1024
+small_cost = pl.CostEstimate(flops=1, bytes_accessed=1, transcendentals=0)
 
 
 def shift(values, axis, step):
@@ -74,6 +75,7 @@
     group = span // count
     block = (fields, 1, rows, cells)
     piece = pl.BlockSpec(block, lambda i, place: (0, i, 0, 0))
+    within = pl.BlockSpec(block, lambda i, place: (0, offset + i, 0, 0))
     return pl.pallas_call(
         functools.partial(wall_kernel, count, fields),
         out_shape=[jax.ShapeDtypeStruct((fields, part, rows, cells), jnp.float32)] * count,
@@ -81,16 +83,12 @@
             num_scalar_prefetch=1,
             grid=(part,),
             in_specs=[pl.BlockSpec(block, lambda i, place: (0, place[0] * group + offset + i, 0, 0))]
-            + [piece] * (count - 1)
+            + [piece if a.shape[1] == part else within for a in received]
             + [pl.BlockSpec(matrix.shape, lambda i, place: (0, 0))],
             out_specs=[piece] * count,
         ),
         compiler_params=pltpu.CompilerParams(vmem_limit_bytes=vmem_limit),
-        cost_estimate=pl.CostEstimate(
-            flops=12 * part * fields * cells * matrix.shape[0] ** 2,
-            bytes_accessed=8 * count * fields * part * rows * cells,
-            transcendentals=0,
-        ),
+        cost_estimate=small_cost,
         name="wall_part",
     )(place, conserved, *received, matrix)
 
@@ -142,11 +140,7 @@
         out_specs=pl.BlockSpec((fields, width), lambda i: (0, i)),
         scratch_shapes=[pltpu.VMEM((3 * fields, lanes, height), jnp.bfloat16)],
         compiler_params=pltpu.CompilerParams(vmem_limit_bytes=vmem_limit),
-        cost_estimate=pl.CostEstimate(
-            flops=6 * fields * lanes * height * columns,
-            bytes_accessed=4 * table.size,
-            transcendentals=0,
-        ),
+        cost_estimate=small_cost,
         name="inlet_part",
     )(table, slot, column, gain)
 
@@ -226,11 +220,7 @@
             pltpu.VMEM((cells // 128, fields * span * tile, 128), jnp.float32),
         ],
         compiler_params=pltpu.CompilerParams(vmem_limit_bytes=vmem_limit),
-        cost_estimate=pl.CostEstimate(
-            flops=12 * conserved.size * (cells + wide),
-            bytes_accessed=20 * conserved.size,
-            transcendentals=0,
-        ),
+        cost_estimate=small_cost,
         name="local_part",
     )(conserved, before, after, register, inlet, edge, band, weights)
 
@@ -261,9 +251,7 @@
         ),
         input_output_aliases={1: 0, 2: 1},
         compiler_params=pltpu.CompilerParams(vmem_limit_bytes=vmem_limit),
-        cost_estimate=pl.CostEstimate(
-            flops=4 * term.size, bytes_accessed=20 * term.size, transcendentals=0
-        ),
+        cost_estimate=small_cost,
         name="close_part",
     )(place, current, partial, term)
 
@@ -310,81 +298,101 @@
     steps = order_of_steps(count)
     place = lambda s: jnp.reshape((row + s) % count, (1,)).astype(jnp.int32)
 
-    def outgoing(source, c, s):
-        start = ((row - s) % count) * group + c * part
-        return lax.dynamic_slice_in_dim(source, start, part, 1)
-
-    first = {s: outgoing(conserved, 0, s) for s in steps}
-    early, late = steps[:2], steps[2:]
-    received = [{s: shift(first[s], "py", -s) for s in early}, {}]
-
-    behind = after(conserved, *[first[s] for s in early])
-    recycle = behind[:, :, :, 3 * cells // 4].reshape(-1, 128)
-    along = [recycle] + [shift(recycle, "py", -s) for s in range(1, count)]
-    rest = after(conserved, recycle)
-    second = {s: outgoing(rest, parts - 1, s) for s in steps}
-    head, tail = after((rest[:, :width], rest[:, span - width :]), *along)
-    for s in late:
-        received[0][s] = shift(after(first[s], received[0][early[0]]), "py", -s)
-    waits = [received[0][s] for s in steps[1:]]
-    for s, wait in zip(steps, waits + [waits[-1]] * count):
-        received[1][s] = shift(after(second[s], wait), "py", -s)
+    def outgoing(source, s, offset, length):
+        start = ((row - s) % count) * group + offset
+        return lax.dynamic_slice_in_dim(source, start, length, 1)
+
+    piece = outgoing(conserved, steps[0], 0, group)
+    received = {steps[0]: shift(piece, "py", -steps[0])}
+    behind = after(conserved, piece)
+    for s in steps[1:-1]:
+        received[s] = shift(outgoing(behind, s, 0, group), "py", -s)
+    pieces = [outgoing(behind, steps[-1], c * part, part) for c in range(parts)]
+    ahead = [received[steps[0]]]
+    last = [shift(pieces[0], "py", -steps[-1])]
+    for c in range(1, parts):
+        last.append(shift(after(pieces[c], ahead[-1]), "py", -steps[-1]))
+    head, tail = after((conserved[:, :width], conserved[:, span - width :]), *pieces)
     halo_after = shift(head, "pz", -1)
     halo_before = shift(tail, "pz", 1)
 
-    table = lax.all_gather(jnp.stack(along), "pz", axis=0).reshape(across * count, fields, -1, 128)
-    myself = lax.axis_index(("py", "pz"))
-    own_block = lax.dynamic_slice_in_dim(source_block[:, :, 0], myself, 1, 0)
-    own_column = lax.dynamic_slice_in_dim(source_column, myself, 1, 0)
-    slot = (own_block % across) * count + (own_block // across - row) % count
+    recycle = after(conserved, received[steps[0]])
+    recycle = recycle[:, :, :, 3 * cells // 4].reshape(-1, 128)
+    along = lax.all_to_all(
+        jnp.broadcast_to(recycle, (count,) + recycle.shape), "py", split_axis=0, concat_axis=0
+    )
+    table = lax.all_gather(along, "pz", axis=0).reshape(across * count, fields, -1, 128)
+
+    place_of = lambda a: lax.dynamic_index_in_dim(
+        a.reshape(count, across, columns), lax.axis_index("pz"), 1, keepdims=False
+    )
+    beside = lambda a, step: lax.dynamic_index_in_dim(
+        lax.dynamic_index_in_dim(a.reshape(count, across, columns), row, 0, keepdims=False),
+        (lax.axis_index("pz") + step) % across,
+        0,
+        keepdims=False,
+    )
+    edge_columns = width * rows
+
+    def sources(a):
+        lines = place_of(a)
+        lines = lax.dynamic_slice_in_dim(jnp.concatenate([lines, lines]), row, count, 0)
+        near = jnp.concatenate(
+            [beside(a, -1)[columns - edge_columns :], lines[0], beside(a, 1)[:edge_columns]]
+        )
+        return near.reshape(1, -1), lines[1:].reshape(1, -1)
+
+    near_block, far_block = sources(source_block)
+    near_column, far_column = sources(source_column)
+    slot = lambda block: (block % across) * count + block // across
 
     twice = jnp.concatenate([wall_matrix, wall_matrix], axis=0)
     twice = lax.dynamic_slice_in_dim(twice, row * rows, count * rows, 0)
     twice = jnp.concatenate([twice, twice], axis=1)
     matrix = lax.dynamic_slice_in_dim(twice, row * rows, count * rows, 1)
 
-    returned = [{}, {}]
-    pieces = wall_part(
-        place(0), conserved, [received[0][s] for s in range(1, count)], matrix, 0, part
-    )
-    returned[0][0] = pieces[0]
-    waits = [received[1][s] for s in steps]
-    for s, wait in zip(steps, waits[:-1] + [waits[-2]] * count):
+    def wall(c, *earlier):
+        parted = {**received, steps[-1]: last[c]}
+        return wall_part(
+            place(0),
+            conserved,
+            [parted[s] for s in range(1, count)],
+            after(matrix, *earlier),
+            c * part,
+            part,
+        )
+
+    pieces = wall(0)
+    returned = [{0: pieces[0]}, {}]
+    waits = [halo_after, halo_before] + [halo_after] * count
+    for s, wait in zip(steps, waits):
         returned[0][s] = shift(after(pieces[s], wait), "py", s)
 
-    inlet = inlet_part(table, slot, own_column, inflow_gain).reshape(fields, span, rows)
-
-    inlet_after = shift(inlet[:, :width], "pz", -1)
-    inlet_before = shift(inlet[:, span - width :], "pz", 1)
-    flat = inlet.reshape(-1, 128)
-    lines = lax.all_to_all(
-        jnp.broadcast_to(flat, (count,) + flat.shape), "py", split_axis=0, concat_axis=0
-    )
-    lines = lines.reshape(count, fields, span, rows)
-    line_flux = jnp.stack(flux_pieces([lines[:, f] for f in range(fields)], 1))
-    own_rows = lax.dynamic_slice_in_dim(wall_matrix, row * rows, rows, 0)
+    near = inlet_part(table, slot(near_block), after(near_column, pieces[0]), inflow_gain)
+    inlet_wide = near.reshape(fields, span + 2 * width, rows).swapaxes(1, 2)
+    far = inlet_part(table, slot(far_block), after(far_column, near), inflow_gain)
+
+    pieces = wall(parts - 1, far)
+    returned[1][0] = pieces[0]
+    for k, s in enumerate(steps):
+        piece = pieces[s]
+        if k >= 2:
+            piece = after(piece, returned[0][steps[k - 2]])
+        returned[1][s] = shift(piece, "py", s)
+
+    own = near.reshape(fields, span + 2 * width, rows)[:, width : width + span]
+    lines = jnp.concatenate(
+        [own[:, None], far.reshape(fields, count - 1, span, rows)], axis=1
+    )
+    line_flux = jnp.stack(flux_pieces([lines[f] for f in range(fields)], 1))
     edge = jnp.einsum(
-        "asb,fszb->faz", own_rows.reshape(rows, count, rows), line_flux, precision=highest
-    )
-    inlet_wide = jnp.concatenate([inlet_before, inlet, inlet_after], axis=1).swapaxes(1, 2)
+        "asb,fszb->faz", matrix[:rows].reshape(rows, count, rows), line_flux, precision=highest
+    )
 
     local_blocks = span // width
     own_blocks = lax.dynamic_slice_in_dim(
         span_blocks, lax.axis_index("pz") * local_blocks, local_blocks, 0
     )
-
-    pieces = wall_part(
-        place(0),
-        conserved,
-        [received[1][s] for s in range(1, count)],
-        matrix,
-        (parts - 1) * part,
-        part,
-    )
-    returned[1][0] = pieces[0]
-    waits = [returned[0][s] for s in steps]
-    for s, wait in zip(steps, waits[:-1] + [waits[-2]] * count):
-        returned[1][s] = shift(after(pieces[s], wait), "py", s)
 
     current, partial = local_part(
         conserved,

time: 518 us -> 493 us (0.952)
  waiting for transfers between devices: 245 us -> 126 us
  Pallas kernels: 101 us -> 176 us
  local copies, waits for them, and re-layouts: 42.2 us -> 58.9 us
    ppermute x19 -> x12, waiting for transfers between devices: 245 us -> 104 us  [shift(): lax.ppermute(values, axis, [(i, (i + step) % count) for i in range(count)])]
    ppermute x19 -> x12, starting transfers between devices: 107 us -> 22 us  [shift(): lax.ppermute(values, axis, [(i, (i + step) % count) for i in range(count)])]
    all_to_all x1, starting transfers between devices: 4.09 us -> 86.5 us  [local(): lax.all_to_all(jnp.broadcast_to(recycle, (count,) + recycle.shape), 'py',...]
    pallas_call x1 -> x2, Pallas kernels: 20 us -> 94.9 us  [inlet_part(): pl.pallas_call(inlet_kernel, out_shape=jax.ShapeDtypeStruct((fields, colu...]
    all_to_all x1, waiting for transfers between devices: 0.01 us -> 20.1 us  [local(): lax.all_to_all(jnp.broadcast_to(recycle, (count,) + recycle.shape), 'py',...]
    unnamed x20 -> x44, local copies, waits for them, and re-layouts: 6.22 us -> 13.8 us
    dynamic_slice x3 -> x5, local copies, waits for them, and re-layouts: 7.87 us -> 11.8 us  [the longest x3 10.7 us: outgoing(): return lax.dynamic_slice_in_dim(source, start, length, 1)]
    slice x3 -> x6, local copies, waits for them, and re-layouts: 19.9 us -> 21.7 us  [the longest x1 10.4 us: local(): recycle = recycle[:, :, :, 3 * cells // 4].reshape(-1, 128)]
  transfers between devices with their start and end apart: 21 -> 14, of which waited for: 9 -> 5; matrix products, arithmetic and copies ran while one was open for 5% -> 11% of each run, Pallas kernels for 19% -> 35%
where the time goes in v3:
time: 493 us; the launch traced here: 492 us
  Pallas kernels  176 us (36%)
  waiting for transfers between devices  126 us (26%)
  starting transfers between devices  108 us (22%)
  local copies, waits for them, and re-layouts  58.9 us (12%)
  between operations  14.4 us (3%)
  other arithmetic  6.57 us (1%)
    ppermute x12, waiting for transfers between devices, shift(): lax.ppermute(values, axis, [(i, (i + step) % count) for i in range(count)])  104 us
    pallas_call x2, Pallas kernels, inlet_part(): pl.pallas_call(inlet_kernel, out_shape=jax.ShapeDtypeStruct((fields, colu...  94.9 us
    all_to_all x1, starting transfers between devices, local(): lax.all_to_all(jnp.broadcast_to(recycle, (count,) + recycle.shape), 'py',...  86.5 us
    pallas_call x1, Pallas kernels, local_part(): pl.pallas_call(functools.partial(local_kernel, halo), out_shape=[shape, s...  36.3 us
    pallas_call x8, Pallas kernels, close_part(): pl.pallas_call(close_kernel, out_shape=[shape, shape], grid_spec=pltpu.Pr...  25.7 us
    ppermute x12, starting transfers between devices, shift(): lax.ppermute(values, axis, [(i, (i + step) % count) for i in range(count)])  22 us
    all_to_all x1, waiting for transfers between devices, local(): lax.all_to_all(jnp.broadcast_to(recycle, (count,) + recycle.shape), 'py',...  20.1 us
    pallas_call x2, Pallas kernels, wall_part(): pl.pallas_call(functools.partial(wall_kernel, count, fields), out_shape=[...  18.8 us
  transfers between devices with their start and end apart: 14, of which 5 were waited for; matrix products, arithmetic and copies ran while one was open for 11% of the time, Pallas kernels for 35%

profile of v3, /device:TPU:0, one launch (start us, length us, event | category | flops | bytes accessed | tf_op | source)
XLA Modules:
  0.0 491.8 jit_solution(11976145303024843240)
XLA Ops:
  7.2 3.6 constant_dynamic-slice_fusion.6
  10.8 5.0 %collective-permute-start.2 = (f32[5,16,64,128]{3,2,1,0:T(8,128)}, f32[5,16,64,128]{3,2,1,0:T(8,128)S(1)}, u32[]{:S(2)}, u32[]{:S(2)}) collective-permute-start(f32[5,16,64,128]{3,2,1,0:T(8,128)} %constant_dynamic-slice_fusion.6), channel_id=1, source_target_pairs={{0,24},{8,0},{16,8},{24,16},{1,25},{9,1},{17,9},{25,17},{2,26},{10... | collective-permute-start | bytes 7864328 | tf_op jit(solution)/shard_map/ppermute | solution.py:21
  15.8 3.5 constant_dynamic-slice_fusion.4
  19.3 3.6 constant_dynamic-slice_fusion
  22.9 1.0 collective-permute-start.4
  23.9 10.3 %fusion.22 = (f32[5,32,64,128]{3,2,1,0:T(8,128)}, f32[5,32,64,128]{3,2,1,0:T(8,128)}) fusion(f32[5,64,64,128]{3,2,1,0:T(8,128)} %own_ref.3), kind=kLoop, calls=%fused_computation.79 | loop fusion | bytes 20971520 | tf_op jit(solution)/shard_map/slice | solution.py:315
  34.3 2.6 collective-permute-start.1
  36.9 1.1 constant_dynamic-slice_fusion.2
  39.4 34.1 %collective-permute-done.2.refs_0_ = f32[5,16,64,128]{3,2,1,0:T(8,128)S(1)} collective-permute-done((f32[5,16,64,128]{3,2,1,0:T(8,128)}, f32[5,16,64,128]{3,2,1,0:T(8,128)S(1)}, u32[]{:S(2)}, u32[]{:S(2)}) %collective-permute-start.2) | collective-permute-done | bytes 2621472 | tf_op jit(solution)/shard_map/ppermute | solution.py:21
  73.5 10.4 %slice_reduce_fusion = f32[5,64,64]{2,1,0:T(8,128)S(1)} fusion(f32[5,64,64,128]{3,2,1,0:T(8,128)} %own_ref.3), kind=kLoop, calls=%fused_computation | loop fusion | bytes 163840 | tf_op jit(solution)/shard_map/slice | solution.py:320
  84.8 86.5 %all-to-all-start = ((f32[4,160,128]{2,1,0:T(8,128)}), f32[4,160,128]{2,1,0:T(8,128)S(1)}, u32[]{:S(2)}, u32[]{:S(2)}) async-start(f32[4,160,128]{2,1,0:T(8,128)} %broadcast_in_dim.7), calls=%async_computation | async-start | bytes 655360 | tf_op jit(solution)/shard_map/all_to_all | solution.py:321
  171.4 20.1 %all-to-all-done = f32[4,160,128]{2,1,0:T(8,128)S(1)} async-done(((f32[4,160,128]{2,1,0:T(8,128)}), f32[4,160,128]{2,1,0:T(8,128)S(1)}, u32[]{:S(2)}, u32[]{:S(2)}) %all-to-all-start) | async-done | bytes 327712 | tf_op jit(solution)/shard_map/all_to_all | solution.py:321
  192.2 1.0 fusion.17.slot_ref
  193.2 1.0 fusion.1
  197.7 1.9 collective-permute-start.8
  199.6 9.7 %wall_part.2 = (f32[5,8,64,128]{3,2,1,0:T(8,128)S(1)}, f32[5,8,64,128]{3,2,1,0:T(8,128)}, f32[5,8,64,128]{3,2,1,0:T(8,128)S(1)}, f32[5,8,64,128]{3,2,1,0:T(8,128)S(1)}) custom-call(s32[1]{0:T(128)} %bitcast.3.place_ref, f32[5,64,64,128]{3,2,1,0:T(8,128)} %own_ref.3, f32[5,16,64,128]{3,2,1,0:T(8,128)} %copy-done.14, ...), custom_call_target="tpu_custom_call" | custom-call | flops 1 | bytes 1 | tf_op jit(solution)/shard_map/wall_part/pallas_call | solution.py:79
  209.3 1.1 copy-done.9
  210.4 1.1 copy-done.10
  211.5 3.1 collective-permute-start.5
  223.1 1.5 all-gather.3.cloned.1.call-done
  224.6 1.7 copy-done
  226.3 38.3 %inlet_part.2 = f32[5,8192]{1,0:T(8,128)S(1)} custom-call(f32[32,5,32,128]{3,2,1,0:T(8,128)S(1)} %bitcast.57, s32[1,8192]{1,0:T(1,128)S(1)} %fusion.19.slot_ref, s32[1,8192]{1,0:T(1,128)S(1)} %bitcast.62, f32[5]{0:T(128)S(1)} %copy-done.8), custom_call_target="tpu_custom_call" | custom-call | flops 1 | bytes 1 | tf_op jit(solution)/shard_map/inlet_part/pallas_call | solution.py:130
  266.2 56.6 %inlet_part.3 = f32[5,12288]{1,0:T(8,128)S(1)} custom-call(f32[32,5,32,128]{3,2,1,0:T(8,128)S(1)} %bitcast.58, s32[1,12288]{1,0:T(1,128)S(1)} %copy-done.5, s32[1,12288]{1,0:T(1,128)S(1)} %bitcast.61, f32[5]{0:T(128)S(1)} %copy-done.8), custom_call_target="tpu_custom_call" | custom-call | flops 1 | bytes 1 | tf_op jit(solution)/shard_map/inlet_part/pallas_call | solution.py:130
  322.8 9.1 %wall_part.3 = (f32[5,8,64,128]{3,2,1,0:T(8,128)S(1)}, f32[5,8,64,128]{3,2,1,0:T(8,128)S(1)}, f32[5,8,64,128]{3,2,1,0:T(8,128)S(1)}, f32[5,8,64,128]{3,2,1,0:T(8,128)S(1)}) custom-call(s32[1]{0:T(128)} %bitcast.3.place_ref, f32[5,64,64,128]{3,2,1,0:T(8,128)} %own_ref.3, f32[5,16,64,128]{3,2,1,0:T(8,128)} %copy-done.14, ...), custom_call_target="tpu_custom_call" | custom-call | flops 1 | bytes 1 | tf_op jit(solution)/shard_map/wall_part/pallas_call | solution.py:79
  332.0 1.1 copy-done.1
  333.0 1.1 copy-done.11
  334.1 1.1 copy-done.12
  335.2 1.0 copy-done.13
  337.1 1.5 collective-permute-start.9
  338.6 2.3 collective-permute-start.10
  341.0 2.8 collective-permute-start.11
  344.7 1.1 copy.37
  345.8 1.0 reshape.487
  347.8 1.0 multiply_dynamic-update-slice_fusion.2
  348.7 1.1 add_dynamic-update-slice_fusion
  349.8 1.0 multiply_dynamic-update-slice_fusion
  350.8 1.8 convolution_bitcast_fusion.edge_ref
  352.7 36.3 %local_part.1 = (f32[5,64,64,128]{3,2,1,0:T(8,128)}, f32[5,64,64,128]{3,2,1,0:T(8,128)}) custom-call(f32[5,64,64,128]{3,2,1,0:T(8,128)} %own_ref.3, f32[5,32,64,128]{3,2,1,0:T(8,128)} %collective-permute-done.before_ref, f32[5,32,64,128]{3,2,1,0:T(8,128)} %collective-permute-done.1.after_ref, f32[5,64,64,128]{3,2,1,0:T(8,128)} %reg_ref.1, ...), custom_call_target="tpu_custom_call" | custom-call | flops 1 | bytes 1 | tf_op jit(solution)/shard_map/local_part/pallas_call | solution.py:211
  389.0 3.0 close_part.8
  392.0 3.0 close_part.9
  395.0 3.4 close_part.10
  398.3 29.0 %collective-permute-done.7.term_ref = f32[5,8,64,128]{3,2,1,0:T(8,128)} collective-permute-done((f32[5,8,64,128]{3,2,1,0:T(8,128)}, f32[5,8,64,128]{3,2,1,0:T(8,128)}, u32[]{:S(2)}, u32[]{:S(2)}) %collective-permute-start.7) | collective-permute-done | bytes 1310752 | tf_op jit(solution)/shard_map/ppermute | solution.py:21
  427.3 3.4 close_part.11
  430.7 3.0 close_part.12
  433.7 3.4 close_part.13
  437.0 3.4 close_part.14
  440.4 41.2 %collective-permute-done.11.term_ref = f32[5,8,64,128]{3,2,1,0:T(8,128)} collective-permute-done((f32[5,8,64,128]{3,2,1,0:T(8,128)}, f32[5,8,64,128]{3,2,1,0:T(8,128)}, u32[]{:S(2)}, u32[]{:S(2)}) %collective-permute-start.11) | collective-permute-done | bytes 1310752 | tf_op jit(solution)/shard_map/ppermute | solution.py:21
  481.6 3.3 close_part.15
  (78 shorter events, 19.2 us)
Async XLA Ops:
  10.8 62.7 %collective-permute-start.2 = (f32[5,16,64,128]{3,2,1,0:T(8,128)}, f32[5,16,64,128]{3,2,1,0:T(8,128)S(1)}, u32[]{:S(2)}, u32[]{:S(2)}) collective-permute-start(f32[5,16,64,128]{3,2,1,0:T(8,128)} %constant_dynamic-slice_fusion.6), channel_id=1, source_target_pairs={{0,24},{8,0},{16,8},{24,16},{1,25},{9,1},{17,9},{25,17},{2,26},{10... | collective-permute-start | bytes 7864328 | tf_op jit(solution)/shard_map/ppermute | solution.py:21
  19.3 180.3 %collective-permute-start.3 = (f32[5,8,64,128]{3,2,1,0:T(8,128)}, f32[5,8,64,128]{3,2,1,0:T(8,128)}, u32[]{:S(2)}, u32[]{:S(2)}) collective-permute-start(f32[5,8,64,128]{3,2,1,0:T(8,128)} %get-tuple-element.81), channel_id=1, source_target_pairs={{0,16},{8,24},{16,0},{24,8},{1,17},{9,25},{17,1},{25,9},{2,18},{10... | collective-permute-start | bytes 3932168 | tf_op jit(solution)/shard_map/ppermute | solution.py:21
  22.9 15.1 %copy-start.17 = (s32[32,4096,1]{1,2,0:T(1,128)S(1)}, s32[32,4096,1]{1,2,0:T(1,128)}, u32[]{:S(2)}) copy-start(s32[32,4096,1]{1,2,0:T(1,128)} %param.14) | copy-start | bytes 1572868
  22.9 176.7 %collective-permute-start.4 = (f32[5,16,64,128]{3,2,1,0:T(8,128)}, f32[5,16,64,128]{3,2,1,0:T(8,128)}, u32[]{:S(2)}, u32[]{:S(2)}) collective-permute-start(f32[5,16,64,128]{3,2,1,0:T(8,128)} %constant_dynamic-slice_fusion), channel_id=1, source_target_pairs={{0,8},{8,16},{16,24},{24,0},{1,9},{9,17},{17,25},{25,1},{2,10},{10... | collective-permute-start | bytes 7864328 | tf_op jit(solution)/shard_map/ppermute | solution.py:21
  34.3 187.3 %collective-permute-start = (f32[5,32,64,128]{3,2,1,0:T(8,128)}, f32[5,32,64,128]{3,2,1,0:T(8,128)}, u32[]{:S(2)}, u32[]{:S(2)}) collective-permute-start(f32[5,32,64,128]{3,2,1,0:T(8,128)} %get-tuple-element.39), channel_id=1, source_target_pairs={{0,1},{1,2},{2,3},{3,4},{4,5},{5,6},{6,7},{7,0},{8,9},{9,10},{10,1... | collective-permute-start | bytes 15728648 | tf_op jit(solution)/shard_map/ppermute | solution.py:21
  34.3 177.2 %collective-permute-start.1 = (f32[5,32,64,128]{3,2,1,0:T(8,128)}, f32[5,32,64,128]{3,2,1,0:T(8,128)}, u32[]{:S(2)}, u32[]{:S(2)}) collective-permute-start(f32[5,32,64,128]{3,2,1,0:T(8,128)} %get-tuple-element.40), channel_id=1, source_target_pairs={{0,7},{1,0},{2,1},{3,2},{4,3},{5,4},{6,5},{7,6},{8,15},{9,8},{10,9... | collective-permute-start | bytes 15728648 | tf_op jit(solution)/shard_map/ppermute | solution.py:21
  38.4 0.8 copy-start.16
  39.4 155.1 %slice-start = ((f32[1,3,128,128]{3,2,1,0:T(8,128)}), f32[1,1,128,128]{3,2,1,0:T(8,128)S(1)}, s32[]{:S(2)}) async-start(f32[1,3,128,128]{3,2,1,0:T(8,128)} %param.10), calls=%async_computation.2 | async-start | bytes 131072 | tf_op jit(solution)/shard_map/slice | solution.py:266
  73.5 10.4 %copy-start.14 = (f32[5,16,64,128]{3,2,1,0:T(8,128)}, f32[5,16,64,128]{3,2,1,0:T(8,128)S(1)}, u32[]{:S(2)}) copy-start(f32[5,16,64,128]{3,2,1,0:T(8,128)S(1)} %collective-permute-done.2.refs_0_) | copy-start | bytes 7864324
  84.8 106.7 %all-to-all-start = ((f32[4,160,128]{2,1,0:T(8,128)}), f32[4,160,128]{2,1,0:T(8,128)S(1)}, u32[]{:S(2)}, u32[]{:S(2)}) async-start(f32[4,160,128]{2,1,0:T(8,128)} %broadcast_in_dim.7), calls=%async_computation | async-start | bytes 655360 | tf_op jit(solution)/shard_map/all_to_all | solution.py:321
  171.3 53.3 %all-gather.3.cloned.1.call-start = ((), (), s32[]{:S(2)}) async-start(), calls=%async_computation.1 | async-start | bytes 2949120 | tf_op jit(solution)/shard_map/all_gather | solution.py:324
  191.5 0.7 copy-start.15
  197.7 125.1 %collective-permute-start.8 = (f32[5,8,64,128]{3,2,1,0:T(8,128)}, f32[5,8,64,128]{3,2,1,0:T(8,128)}, u32[]{:S(2)}, u32[]{:S(2)}) collective-permute-start(f32[5,8,64,128]{3,2,1,0:T(8,128)} %get-tuple-element.61), channel_id=1, source_target_pairs={{0,16},{8,24},{16,0},{24,8},{1,17},{9,25},{17,1},{25,9},{2,18},{10... | collective-permute-start | bytes 3932168 | tf_op jit(solution)/shard_map/ppermute | solution.py:21
  199.6 25.0 %copy-start.8 = (f32[5]{0:T(128)S(1)}, f32[5]{0:T(128)}, u32[]{:S(2)}) copy-start(f32[5]{0:T(128)} %gain_ref.3) | copy-start | bytes 64
  209.3 1.1 copy-start.9
  210.4 1.1 copy-start.10
  211.5 129.5 %collective-permute-start.5 = (f32[5,8,64,128]{3,2,1,0:T(8,128)}, f32[5,8,64,128]{3,2,1,0:T(8,128)S(1)}, u32[]{:S(2)}, u32[]{:S(2)}) collective-permute-start(f32[5,8,64,128]{3,2,1,0:T(8,128)} %get-tuple-element.50), channel_id=1, source_target_pairs={{0,8},{8,16},{16,24},{24,0},{1,9},{9,17},{17,25},{25,1},{2,10},{10... | collective-permute-start | bytes 3932168 | tf_op jit(solution)/shard_map/ppermute | solution.py:21
  219.7 0.6 copy-start.6
  221.6 173.4 %collective-permute-start.6 = (f32[5,8,64,128]{3,2,1,0:T(8,128)}, f32[5,8,64,128]{3,2,1,0:T(8,128)}, u32[]{:S(2)}, u32[]{:S(2)}) collective-permute-start(f32[5,8,64,128]{3,2,1,0:T(8,128)} %copy-done.10), channel_id=1, source_target_pairs={{0,24},{8,0},{16,8},{24,16},{1,25},{9,1},{17,9},{25,17},{2,26},{10... | collective-permute-start | bytes 3932168 | tf_op jit(solution)/shard_map/ppermute | solution.py:21
  222.3 205.0 %collective-permute-start.7 = (f32[5,8,64,128]{3,2,1,0:T(8,128)}, f32[5,8,64,128]{3,2,1,0:T(8,128)}, u32[]{:S(2)}, u32[]{:S(2)}) collective-permute-start(f32[5,8,64,128]{3,2,1,0:T(8,128)} %copy-done.9), channel_id=1, source_target_pairs={{0,16},{8,24},{16,0},{24,8},{1,17},{9,25},{17,1},{25,9},{2,18},{10... | collective-permute-start | bytes 3932168 | tf_op jit(solution)/shard_map/ppermute | solution.py:21
  224.6 1.7 copy-start
  264.6 0.8 copy-start.4
  265.4 0.8 copy-start.5
  331.9 1.1 copy-start.1
  333.0 1.1 copy-start.11
  334.1 1.1 copy-start.12
  335.2 1.0 copy-start.13
  336.3 16.4 %copy-start.3 = (f32[1,1,128,128]{2,3,1,0:T(8,128)S(1)}, f32[1,1,128,128]{2,3,1,0:T(8,128)}, u32[]{:S(2)}) copy-start(f32[1,1,128,128]{2,3,1,0:T(8,128)} %copy.46) | copy-start | bytes 196612
  336.3 16.4 %copy-start.7 = (f32[64,128]{1,0:T(8,128)S(1)}, f32[64,128]{1,0:T(8,128)}, u32[]{:S(2)}) copy-start(f32[64,128]{1,0:T(8,128)} %copy-done.6) | copy-start | bytes 98308
  337.1 96.6 %collective-permute-start.9 = (f32[5,8,64,128]{3,2,1,0:T(8,128)}, f32[5,8,64,128]{3,2,1,0:T(8,128)}, u32[]{:S(2)}, u32[]{:S(2)}) collective-permute-start(f32[5,8,64,128]{3,2,1,0:T(8,128)} %copy-done.13), channel_id=1, source_target_pairs={{0,8},{8,16},{16,24},{24,0},{1,9},{9,17},{17,25},{25,1},{2,10},{10... | collective-permute-start | bytes 3932168 | tf_op jit(solution)/shard_map/ppermute | solution.py:21
  338.6 98.4 %collective-permute-start.10 = (f32[5,8,64,128]{3,2,1,0:T(8,128)}, f32[5,8,64,128]{3,2,1,0:T(8,128)}, u32[]{:S(2)}, u32[]{:S(2)}) collective-permute-start(f32[5,8,64,128]{3,2,1,0:T(8,128)} %copy-done.12), channel_id=1, source_target_pairs={{0,24},{8,0},{16,8},{24,16},{1,25},{9,1},{17,9},{25,17},{2,26},{10... | collective-permute-start | bytes 3932168 | tf_op jit(solution)/shard_map/ppermute | solution.py:21
  341.0 140.7 %collective-permute-start.11 = (f32[5,8,64,128]{3,2,1,0:T(8,128)}, f32[5,8,64,128]{3,2,1,0:T(8,128)}, u32[]{:S(2)}, u32[]{:S(2)}) collective-permute-start(f32[5,8,64,128]{3,2,1,0:T(8,128)} %copy-done.11), channel_id=1, source_target_pairs={{0,16},{8,24},{16,0},{24,8},{1,17},{9,25},{17,1},{25,9},{2,18},{10... | collective-permute-start | bytes 3932168 | tf_op jit(solution)/shard_map/ppermute | solution.py:21
  427.3 3.4 copy-start.2
Sparse Core Ops, SparseCore 0:
  192.3 32.1 all-gather.2

commit v4 on v3

--- a/solution.py
+++ b/solution.py
@@ -75,7 +75,8 @@
     group = span // count
     block = (fields, 1, rows, cells)
     piece = pl.BlockSpec(block, lambda i, place: (0, i, 0, 0))
-    within = pl.BlockSpec(block, lambda i, place: (0, offset + i, 0, 0))
+    within = lambda a: piece if a.shape[1] == part else whole
+    whole = pl.BlockSpec(block, lambda i, place: (0, offset + i, 0, 0))
     return pl.pallas_call(
         functools.partial(wall_kernel, count, fields),
         out_shape=[jax.ShapeDtypeStruct((fields, part, rows, cells), jnp.float32)] * count,
@@ -83,7 +84,7 @@
             num_scalar_prefetch=1,
             grid=(part,),
             in_specs=[pl.BlockSpec(block, lambda i, place: (0, place[0] * group + offset + i, 0, 0))]
-            + [piece if a.shape[1] == part else within for a in received]
+            + [within(a) for a in received]
             + [pl.BlockSpec(matrix.shape, lambda i, place: (0, 0))],
             out_specs=[piece] * count,
         ),
@@ -93,7 +94,7 @@
     )(place, conserved, *received, matrix)
 
 
-def inlet_kernel(table_ref, slot_ref, column_ref, gain_ref, out_ref, split):
+def inlet_kernel(table_ref, source_ref, gain_ref, out_ref, split):
     slots, fields, lines, lanes = table_ref.shape
     height = slots * lines
 
@@ -103,46 +104,47 @@
             rest = table_ref[:, f].reshape(height, lanes)
             for k in range(3):
                 piece = rest.astype(jnp.bfloat16)
-                split[k * fields + f] = piece.T
+                split[pl.ds((k * fields + f) * lanes, lanes), :] = piece.T
                 rest = rest - piece.astype(jnp.float32)
 
-    width = slot_ref.shape[1]
-    column = column_ref[...]
-    line = slot_ref[...] * lines + column // lanes
+    width = source_ref.shape[1]
+    source = source_ref[...]
+    line = source // lanes
     choice = jnp.where(
         lax.broadcasted_iota(jnp.int32, (height, width), 0) == line, 1.0, 0.0
     ).astype(jnp.bfloat16)
-    lane = lax.broadcasted_iota(jnp.int32, (lanes, width), 0) == column % lanes
+    lane = lax.broadcasted_iota(jnp.int32, (lanes, width), 0) == source % lanes
+    found = jnp.dot(split[...], choice, preferred_element_type=jnp.float32)
+    found = found.reshape(3, fields, lanes, width)
     for f in range(fields):
-        total = jnp.zeros((lanes, width), jnp.float32)
-        for k in (2, 1, 0):
-            total += jnp.dot(split[k * fields + f], choice, preferred_element_type=jnp.float32)
+        total = found[2, f] + found[1, f] + found[0, f]
         picked = jnp.sum(jnp.where(lane, total, 0.0), axis=0, keepdims=True)
-        out_ref[f : f + 1, :] = picked * gain_ref[f]
-
-
-def inlet_part(table, slot, column, gain):
+        picked = picked * gain_ref[f]
+        for k in range(width // lanes):
+            out_ref[f, k : k + 1, :] = picked[:, k * lanes : (k + 1) * lanes]
+
+
+def inlet_part(table, source, gain):
     slots, fields, lines, lanes = table.shape
     height = slots * lines
-    columns = column.shape[1]
-    width = math.gcd(columns, 512)
+    columns = source.shape[1]
+    width = 8 * lanes
     row = pl.BlockSpec((1, width), lambda i: (0, i))
     return pl.pallas_call(
         inlet_kernel,
-        out_shape=jax.ShapeDtypeStruct((fields, columns), jnp.float32),
+        out_shape=jax.ShapeDtypeStruct((fields, columns // lanes, lanes), jnp.float32),
         grid=(columns // width,),
         in_specs=[
             pl.BlockSpec(table.shape, lambda i: (0, 0, 0, 0)),
             row,
-            row,
             pl.BlockSpec(memory_space=pltpu.SMEM),
         ],
-        out_specs=pl.BlockSpec((fields, width), lambda i: (0, i)),
-        scratch_shapes=[pltpu.VMEM((3 * fields, lanes, height), jnp.bfloat16)],
+        out_specs=pl.BlockSpec((fields, 8, lanes), lambda i: (0, i, 0)),
+        scratch_shapes=[pltpu.VMEM((3 * fields * lanes, height), jnp.bfloat16)],
         compiler_params=pltpu.CompilerParams(vmem_limit_bytes=vmem_limit),
         cost_estimate=small_cost,
         name="inlet_part",
-    )(table, slot, column, gain)
+    )(table, source, gain)
 
 
 def local_kernel(
@@ -152,7 +154,9 @@
     after_ref,
     reg_ref,
     inlet_ref,
-    edge_ref,
+    near_ref,
+    far_ref,
+    matrix_ref,
     band_ref,
     stream_ref,
     current_ref,
@@ -187,6 +191,19 @@
             for t in range(cells // 128):
                 lines = span_flux[t, pl.ds(f * wide * tile + y, wide, stride=tile), :]
                 span_out[t, pl.ds(f * span * tile + y, span, stride=tile), :] = matmul(band, lines)
+    lines = near_ref.shape[1]
+    near = flux_pieces([near_ref[f] for f in range(fields)], 1)
+    far = flux_pieces([far_ref[f] for f in range(fields)], 1)
+    folds = 128 // span
+    height = far_ref.shape[1]
+    edges = []
+    for f in range(fields):
+        edge = matmul(matrix_ref[:, :lines], near[f])[:, halo : halo + span]
+        for h in range(folds):
+            low = lines + h * height
+            part = matmul(matrix_ref[:, low : low + height], far[f])
+            edge = edge + part[:, h * span : (h + 1) * span]
+        edges.append(edge)
     weights = stream_ref[...]
     for f in range(fields):
         rows = pl.ds(f * span * tile, span * tile)
@@ -194,11 +211,11 @@
         total = matmul(stream_flux[rows, :], weights) + beside
         total = total.reshape(span, tile, cells)
         for z in range(span):
-            term = total[z] + jnp.where(lane == 0, edge_ref[f, :, z : z + 1], 0.0)
+            term = total[z] + jnp.where(lane == 0, edges[f][:, z : z + 1], 0.0)
             partial_ref[f, z] = section_decay * reg_ref[f, z] - time_step * term
 
 
-def local_part(conserved, before, after, register, inlet, edge, band, weights):
+def local_part(conserved, before, after, register, near, far, matrix, band, weights):
     fields, span, rows, cells = conserved.shape
     halo = before.shape[1]
     wide = span + 2 * halo
@@ -206,13 +223,24 @@
     main = pl.BlockSpec((fields, span, tile, cells), lambda i: (0, 0, i, 0))
     side = pl.BlockSpec((fields, halo, tile, cells), lambda i: (0, 0, i, 0))
     whole = lambda a: pl.BlockSpec(a.shape, lambda i: (0, 0))
-    column = lambda a: pl.BlockSpec((fields, tile, a.shape[2]), lambda i: (0, i, 0))
+    whole3 = lambda a: pl.BlockSpec(a.shape, lambda i: (0, 0, 0))
     shape = jax.ShapeDtypeStruct(conserved.shape, jnp.float32)
     return pl.pallas_call(
         functools.partial(local_kernel, halo),
         out_shape=[shape, shape],
         grid=(rows // tile,),
-        in_specs=[main, side, side, main, column(inlet), column(edge), whole(band), whole(weights)],
+        in_specs=[
+            main,
+            side,
+            side,
+            main,
+            pl.BlockSpec((fields, tile, near.shape[2]), lambda i: (0, i, 0)),
+            whole3(near),
+            whole3(far),
+            pl.BlockSpec((tile, matrix.shape[1]), lambda i: (i, 0)),
+            whole(band),
+            whole(weights),
+        ],
         out_specs=[main, main],
         scratch_shapes=[
             pltpu.VMEM((cells // 128, fields * wide * tile, 128), jnp.float32),
@@ -222,7 +250,7 @@
         compiler_params=pltpu.CompilerParams(vmem_limit_bytes=vmem_limit),
         cost_estimate=small_cost,
         name="local_part",
-    )(conserved, before, after, register, inlet, edge, band, weights)
+    )(conserved, before, after, register, near, near, far, matrix, band, weights)
 
 
 def close_kernel(place_ref, current_ref, partial_ref, term_ref, cons_out, reg_out):
@@ -234,7 +262,7 @@
 
 def close_part(place, current, partial, term, group, offset):
     fields, part, rows, cells = term.shape
-    step = math.gcd(part, 4)
+    step = math.gcd(math.gcd(part, 4), math.gcd(group, offset))
     block = (fields, step, rows, cells)
     there = pl.BlockSpec(
         block, lambda i, place: (0, (place[0] * group + offset) // step + i, 0, 0)
@@ -258,22 +286,23 @@
 
 def stream_weights(blocks):
     count, _, width, _ = blocks.shape
-    size = count * width
-    full = jnp.zeros((size, size), jnp.float32)
+    lines = []
     for k in range(count):
-        for j in range(3):
-            if 0 <= k + j - 1 < count:
-                full = lax.dynamic_update_slice(full, blocks[k, j], (k * width, (k + j - 1) * width))
-    return full.T
+        empty = jnp.zeros((width, width), jnp.float32)
+        near = [blocks[i, 1 + k - i].T if abs(k - i) <= 1 else empty for i in range(count)]
+        lines.append(jnp.concatenate(near, axis=1))
+    return jnp.concatenate(lines, axis=0)
 
 
 def span_band(blocks):
     count, _, width, _ = blocks.shape
-    full = jnp.zeros((count * width, (count + 2) * width), jnp.float32)
+    lines = []
     for k in range(count):
-        for j in range(3):
-            full = lax.dynamic_update_slice(full, blocks[k, j], (k * width, (k + j) * width))
-    return full
+        line = [jnp.zeros((width, k * width), jnp.float32)] if k else []
+        line += [blocks[k, j] for j in range(3)]
+        line += [jnp.zeros((width, (count - 1 - k) * width), jnp.float32)] if k < count - 1 else []
+        lines.append(jnp.concatenate(line, axis=1))
+    return jnp.concatenate(lines, axis=0)
 
 
 def local(
@@ -292,8 +321,8 @@
     across = lax.axis_size("pz")
     row = lax.axis_index("py")
     group = span // count
-    parts = min(2, group)
-    part = group // parts
+    sizes = [group - group // 2, group // 2] if group >= 2 else [group]
+    offsets = [sum(sizes[:c]) for c in range(len(sizes))]
     width = span_blocks.shape[2]
     steps = order_of_steps(count)
     place = lambda s: jnp.reshape((row + s) % count, (1,)).astype(jnp.int32)
@@ -302,26 +331,20 @@
         start = ((row - s) % count) * group + offset
         return lax.dynamic_slice_in_dim(source, start, length, 1)
 
-    piece = outgoing(conserved, steps[0], 0, group)
-    received = {steps[0]: shift(piece, "py", -steps[0])}
-    behind = after(conserved, piece)
-    for s in steps[1:-1]:
-        received[s] = shift(outgoing(behind, s, 0, group), "py", -s)
-    pieces = [outgoing(behind, steps[-1], c * part, part) for c in range(parts)]
-    ahead = [received[steps[0]]]
-    last = [shift(pieces[0], "py", -steps[-1])]
-    for c in range(1, parts):
-        last.append(shift(after(pieces[c], ahead[-1]), "py", -steps[-1]))
-    head, tail = after((conserved[:, :width], conserved[:, span - width :]), *pieces)
+    received = [{} for _ in sizes]
+    sent = []
+    for s in steps[:-1]:
+        sent.append(outgoing(after(conserved, *sent) if sent else conserved, s, 0, group))
+        arrived = shift(sent[-1], "py", -s)
+        for part in received:
+            part[s] = arrived
+    for c in range(len(sizes)):
+        sent.append(outgoing(after(conserved, *sent), steps[-1], offsets[c], sizes[c]))
+        piece = after(sent[-1], received[0][steps[0]]) if c else sent[-1]
+        received[c][steps[-1]] = shift(piece, "py", -steps[-1])
+    head, tail = after((conserved[:, :width], conserved[:, span - width :]), *sent)
     halo_after = shift(head, "pz", -1)
     halo_before = shift(tail, "pz", 1)
-
-    recycle = after(conserved, received[steps[0]])
-    recycle = recycle[:, :, :, 3 * cells // 4].reshape(-1, 128)
-    along = lax.all_to_all(
-        jnp.broadcast_to(recycle, (count,) + recycle.shape), "py", split_axis=0, concat_axis=0
-    )
-    table = lax.all_gather(along, "pz", axis=0).reshape(across * count, fields, -1, 128)
 
     place_of = lambda a: lax.dynamic_index_in_dim(
         a.reshape(count, across, columns), lax.axis_index("pz"), 1, keepdims=False
@@ -340,74 +363,79 @@
         near = jnp.concatenate(
             [beside(a, -1)[columns - edge_columns :], lines[0], beside(a, 1)[:edge_columns]]
         )
-        return near.reshape(1, -1), lines[1:].reshape(1, -1)
-
-    near_block, far_block = sources(source_block)
-    near_column, far_column = sources(source_column)
-    slot = lambda block: (block % across) * count + block // across
+        near = near.reshape(-1, rows).T
+        near = jnp.pad(near, ((0, 0), (0, 128 - near.shape[1])))
+        far = lines[1:].reshape(count - 1, span, rows).swapaxes(1, 2)
+        far = far.reshape(128 // span, -1, span).swapaxes(0, 1)
+        return near.reshape(1, -1), far.reshape(1, -1)
+
+    block = source_block[:, :, 0]
+    near_source, far_source = sources(
+        ((block % across) * count + block // across) * columns + source_column
+    )
 
     twice = jnp.concatenate([wall_matrix, wall_matrix], axis=0)
     twice = lax.dynamic_slice_in_dim(twice, row * rows, count * rows, 0)
     twice = jnp.concatenate([twice, twice], axis=1)
     matrix = lax.dynamic_slice_in_dim(twice, row * rows, count * rows, 1)
 
+    local_blocks = span // width
+    own_blocks = lax.dynamic_slice_in_dim(
+        span_blocks, lax.axis_index("pz") * local_blocks, local_blocks, 0
+    )
+    band = span_band(own_blocks)
+    weights = stream_weights(stream_blocks)
+    small = [matrix, band, weights, near_source, far_source]
+
+    recycle = after(conserved, head, tail, *small)[:, :, :, 3 * cells // 4].reshape(-1, 128)
+    along = lax.all_to_all(
+        jnp.broadcast_to(recycle, (count,) + recycle.shape), "py", split_axis=0, concat_axis=0
+    )
+
+    along = after(along, *received[0].values())
+    prepared = [band, weights, near_source, far_source, halo_after, halo_before]
+
     def wall(c, *earlier):
-        parted = {**received, steps[-1]: last[c]}
         return wall_part(
             place(0),
             conserved,
-            [parted[s] for s in range(1, count)],
+            [received[c][s] for s in range(1, count)],
             after(matrix, *earlier),
-            c * part,
-            part,
+            offsets[c],
+            sizes[c],
         )
 
-    pieces = wall(0)
-    returned = [{0: pieces[0]}, {}]
-    waits = [halo_after, halo_before] + [halo_after] * count
-    for s, wait in zip(steps, waits):
-        returned[0][s] = shift(after(pieces[s], wait), "py", s)
-
-    near = inlet_part(table, slot(near_block), after(near_column, pieces[0]), inflow_gain)
-    inlet_wide = near.reshape(fields, span + 2 * width, rows).swapaxes(1, 2)
-    far = inlet_part(table, slot(far_block), after(far_column, near), inflow_gain)
-
-    pieces = wall(parts - 1, far)
-    returned[1][0] = pieces[0]
-    for k, s in enumerate(steps):
-        piece = pieces[s]
-        if k >= 2:
-            piece = after(piece, returned[0][steps[k - 2]])
-        returned[1][s] = shift(piece, "py", s)
-
-    own = near.reshape(fields, span + 2 * width, rows)[:, width : width + span]
-    lines = jnp.concatenate(
-        [own[:, None], far.reshape(fields, count - 1, span, rows)], axis=1
-    )
-    line_flux = jnp.stack(flux_pieces([lines[f] for f in range(fields)], 1))
-    edge = jnp.einsum(
-        "asb,fszb->faz", matrix[:rows].reshape(rows, count, rows), line_flux, precision=highest
-    )
-
-    local_blocks = span // width
-    own_blocks = lax.dynamic_slice_in_dim(
-        span_blocks, lax.axis_index("pz") * local_blocks, local_blocks, 0
-    )
-
+    returned = [{} for _ in sizes]
+
+    def give(c, pieces, *earlier):
+        returned[c][0] = pieces[0]
+        for s in steps:
+            returned[c][s] = shift(after(pieces[s], *earlier), "py", s)
+
+    walls = [wall(0, *prepared)]
+    give(0, walls[0])
+
+    table = lax.all_gather(along, "pz", axis=0).reshape(across * count, fields, -1, 128)
+    near = inlet_part(table, after(near_source, walls[0][0]), inflow_gain)
+    far = inlet_part(table, after(far_source, near), inflow_gain)
     current, partial = local_part(
         conserved,
         halo_before,
         halo_after,
         register,
-        inlet_wide,
-        edge,
-        span_band(own_blocks),
-        stream_weights(stream_blocks),
-    )
-    for c in range(parts):
+        near,
+        far,
+        matrix,
+        band,
+        weights,
+    )
+    for c in range(1, len(sizes)):
+        walls.append(wall(c, far))
+        give(c, walls[c])
+    for c in range(len(sizes)):
         for s in [0] + steps:
             current, partial = close_part(
-                place(-s), current, partial, returned[c][s], group, c * part
+                place(-s), current, partial, returned[c][s], group, offsets[c]
             )
     return (current, partial)
 

time: 493 us -> 488 us (0.990)
  blocking collectives: 0 us -> 138 us
  starting transfers between devices: 108 us -> 30.2 us
  waiting for transfers between devices: 126 us -> 89.6 us
  local copies, waits for them, and re-layouts: 58.9 us -> 38.5 us
    all_to_all x0 -> x1, blocking collectives: none -> 138 us  [local(): lax.all_to_all(jnp.broadcast_to(recycle, (count,) + recycle.shape), 'py',...]
    all_to_all x1 -> x0, starting transfers between devices: 86.5 us -> none  [local(): lax.all_to_all(jnp.broadcast_to(recycle, (count,) + recycle.shape), 'py',...]
    ppermute x12, waiting for transfers between devices: 104 us -> 75.8 us  [shift(): lax.ppermute(values, axis, [(i, (i + step) % count) for i in range(count)])]
    all_to_all x1 -> x0, waiting for transfers between devices: 20.1 us -> none  [local(): lax.all_to_all(jnp.broadcast_to(recycle, (count,) + recycle.shape), 'py',...]
    all_gather x1, waiting for transfers between devices: 1.47 us -> 13.8 us  [local(): lax.all_gather(along, 'pz', axis=0).reshape(across * count, fields, -1, 128)]
    unnamed x44 -> x16, local copies, waits for them, and re-layouts: 13.8 us -> 3.87 us
    ppermute x12, starting transfers between devices: 22 us -> 30.2 us  [shift(): lax.ppermute(values, axis, [(i, (i + step) % count) for i in range(count)])]
    pallas_call x2, Pallas kernels: 94.9 us -> 88.9 us  [inlet_part(): pl.pallas_call(inlet_kernel, out_shape=jax.ShapeDtypeStruct((fields, colu...]
  transfers between devices with their start and end apart: 14 -> 13, of which waited for: 5 -> 3; matrix products, arithmetic and copies ran while one was open for 11% -> 7% of each run, Pallas kernels for 35% -> 35%
where the time goes in v4:
time: 488 us; the launch traced here: 487 us
  Pallas kernels  174 us (36%)
  blocking collectives  138 us (28%)
  waiting for transfers between devices  89.6 us (18%)
  local copies, waits for them, and re-layouts  38.5 us (8%)
  starting transfers between devices  30.2 us (6%)
  between operations  14.3 us (3%)
    all_to_all x1, blocking collectives, local(): lax.all_to_all(jnp.broadcast_to(recycle, (count,) + recycle.shape), 'py',...  138 us
    pallas_call x2, Pallas kernels, inlet_part(): pl.pallas_call(inlet_kernel, out_shape=jax.ShapeDtypeStruct((fields, colu...  88.9 us
    ppermute x12, waiting for transfers between devices, shift(): lax.ppermute(values, axis, [(i, (i + step) % count) for i in range(count)])  75.8 us
    pallas_call x1, Pallas kernels, local_part(): pl.pallas_call(functools.partial(local_kernel, halo), out_shape=[shape, s...  40.7 us
    ppermute x12, starting transfers between devices, shift(): lax.ppermute(values, axis, [(i, (i + step) % count) for i in range(count)])  30.2 us
    pallas_call x8, Pallas kernels, close_part(): pl.pallas_call(close_kernel, out_shape=[shape, shape], grid_spec=pltpu.Pr...  24.1 us
    pallas_call x2, Pallas kernels, wall_part(): pl.pallas_call(functools.partial(wall_kernel, count, fields), out_shape=[...  20.5 us
    all_gather x1, waiting for transfers between devices, local(): lax.all_gather(along, 'pz', axis=0).reshape(across * count, fields, -1, 128)  13.8 us
  transfers between devices with their start and end apart: 13, of which 3 were waited for; matrix products, arithmetic and copies ran while one was open for 7% of the time, Pallas kernels for 35%

profile of v4, /device:TPU:0, one launch (start us, length us, event | category | flops | bytes accessed | tf_op | source)
XLA Modules:
  0.0 486.6 jit_solution(7678359873505125178)
XLA Ops:
  7.2 3.6 constant_dynamic-slice_fusion.5
  10.8 5.0 %collective-permute-start.2 = (f32[5,16,64,128]{3,2,1,0:T(8,128)}, f32[5,16,64,128]{3,2,1,0:T(8,128)S(1)}, u32[]{:S(2)}, u32[]{:S(2)}) collective-permute-start(f32[5,16,64,128]{3,2,1,0:T(8,128)} %constant_dynamic-slice_fusion.5), channel_id=1, source_target_pairs={{0,24},{8,0},{16,8},{24,16},{1,25},{9,1},{17,9},{25,17},{2,26},{10... | collective-permute-start | bytes 7864328 | tf_op jit(solution)/shard_map/ppermute | solution.py:21
  15.8 3.6 constant_dynamic-slice_fusion.4
  19.4 2.5 constant_dynamic-slice_fusion.3
  21.9 1.0 collective-permute-start.4
  22.9 10.3 %fusion.13 = (f32[5,32,64,128]{3,2,1,0:T(8,128)}, f32[5,32,64,128]{3,2,1,0:T(8,128)}) fusion(f32[5,64,64,128]{3,2,1,0:T(8,128)} %own_ref.3), kind=kLoop, calls=%fused_computation.42 | loop fusion | bytes 20971520 | tf_op jit(solution)/shard_map/slice | solution.py:345
  33.3 2.6 constant_dynamic-slice_fusion.2
  35.9 2.6 collective-permute-start.1
  38.5 1.8 fusion.4
  40.4 0.8 copy-done.5
  41.5 0.1 copy.40
  41.6 1.0 fusion.14
  42.5 0.1 reshape.56
  42.7 0.1 reshape.58
  42.8 0.1 copy.36
  42.9 0.1 copy.37
  43.0 0.1 reshape.60.source_ref
  43.1 0.8 dynamic-slice_bitcast_fusion.5
  44.0 0.1 maximum_maximum_fusion.band_ref
  44.1 0.1 fusion.11
  44.2 0.2 fusion.10.refs_3_.matrix_ref
  44.4 9.5 %slice_reduce_fusion = f32[5,64,64]{2,1,0:T(8,128)S(1)} fusion(f32[5,64,64,128]{3,2,1,0:T(8,128)} %own_ref.3), kind=kLoop, calls=%fused_computation | loop fusion | bytes 163840 | tf_op jit(solution)/shard_map/slice | solution.py:390
  53.9 0.1 reshape_squeeze.3
  54.0 137.5 %all_to_all.5 = f32[4,160,128]{2,1,0:T(8,128)} all-to-all(f32[4,160,128]{2,1,0:T(8,128)S(1)} %broadcast_in_dim.3), channel_id=1, replica_groups=mesh['py'=4,'pz'=8] {'py'}, dimensions={0} | all-to-all | bytes 655360 | tf_op jit(solution)/shard_map/all_to_all | solution.py:391
  191.6 3.3 collective-permute-start.8
  194.9 10.2 %wall_part.2 = (f32[5,8,64,128]{3,2,1,0:T(8,128)S(1)}, f32[5,8,64,128]{3,2,1,0:T(8,128)}, f32[5,8,64,128]{3,2,1,0:T(8,128)}, f32[5,8,64,128]{3,2,1,0:T(8,128)}) custom-call(s32[1]{0:T(128)} %bitcast.3.place_ref, f32[5,64,64,128]{3,2,1,0:T(8,128)} %own_ref.3, f32[5,16,64,128]{3,2,1,0:T(8,128)} %copy-done.4, f32[5,8,64,128]{3,2,1,0:T(8,128)} %collective-permute-done.4.refs_1_, ...), custom_call_target="tpu_custom_call" | custom-call | flops 1 | bytes 1 | tf_op jit(solution)/shard_map/wall_part/pallas_call | solution.py:80
  205.2 1.2 copy-done.1
  206.3 1.8 collective-permute-start.5
  208.1 2.1 collective-permute-start.6
  210.1 13.8 %all-gather.3.cloned.1.call-done = f32[32,160,128]{2,1,0:T(8,128)} async-done(((f32[4,160,128]{2,1,0:T(8,128)}), f32[32,160,128]{2,1,0:T(8,128)}) %all-gather.3.cloned.1.call-update) | async-done | bytes 2621456 | tf_op jit(solution)/shard_map/all_gather | solution.py:418
  223.9 1.7 copy-done
  225.6 35.9 %inlet_part.2.inlet_ref.near_ref = f32[5,64,128]{2,1,0:T(8,128)S(1)} custom-call(f32[32,5,32,128]{3,2,1,0:T(8,128)S(1)} %bitcast.54, s32[1,8192]{1,0:T(1,128)S(1)} %bitcast.57, f32[5]{0:T(128)S(1)} %copy-done.3), custom_call_target="tpu_custom_call" | custom-call | flops 1 | bytes 1 | tf_op jit(solution)/shard_map/inlet_part/pallas_call | solution.py:133
  261.5 53.0 %inlet_part.3.far_ref = f32[5,96,128]{2,1,0:T(8,128)S(1)} custom-call(f32[32,5,32,128]{3,2,1,0:T(8,128)S(1)} %bitcast.55, s32[1,12288]{1,0:T(1,128)S(1)} %reshape.60.source_ref, f32[5]{0:T(128)S(1)} %copy-done.3), custom_call_target="tpu_custom_call" | custom-call | flops 1 | bytes 1 | tf_op jit(solution)/shard_map/inlet_part/pallas_call | solution.py:133
  314.6 10.2 %wall_part.3 = (f32[5,8,64,128]{3,2,1,0:T(8,128)S(1)}, f32[5,8,64,128]{3,2,1,0:T(8,128)}, f32[5,8,64,128]{3,2,1,0:T(8,128)}, f32[5,8,64,128]{3,2,1,0:T(8,128)}) custom-call(s32[1]{0:T(128)} %bitcast.3.place_ref, f32[5,64,64,128]{3,2,1,0:T(8,128)} %own_ref.3, f32[5,16,64,128]{3,2,1,0:T(8,128)} %copy-done.4, f32[5,8,64,128]{3,2,1,0:T(8,128)} %collective-permute-done.8.refs_1_, ...), custom_call_target="tpu_custom_call" | custom-call | flops 1 | bytes 1 | tf_op jit(solution)/shard_map/wall_part/pallas_call | solution.py:80
  324.8 1.5 collective-permute-start.9
  326.3 2.3 collective-permute-start.10
  328.7 10.5 %collective-permute-start.11 = (f32[5,8,64,128]{3,2,1,0:T(8,128)}, f32[5,8,64,128]{3,2,1,0:T(8,128)S(1)}, u32[]{:S(2)}, u32[]{:S(2)}) collective-permute-start(f32[5,8,64,128]{3,2,1,0:T(8,128)} %get-tuple-element.73), channel_id=1, source_target_pairs={{0,16},{8,24},{16,0},{24,8},{1,17},{9,25},{17,1},{25,9},{2,18},{10... | collective-permute-start | bytes 3932168 | tf_op jit(solution)/shard_map/ppermute | solution.py:21
  339.2 40.7 %local_part.1 = (f32[5,64,64,128]{3,2,1,0:T(8,128)}, f32[5,64,64,128]{3,2,1,0:T(8,128)}) custom-call(f32[5,64,64,128]{3,2,1,0:T(8,128)} %own_ref.3, f32[5,32,64,128]{3,2,1,0:T(8,128)} %collective-permute-done.before_ref, f32[5,32,64,128]{3,2,1,0:T(8,128)} %collective-permute-done.1.after_ref, f32[5,64,64,128]{3,2,1,0:T(8,128)} %reg_ref.1, ...), custom_call_target="tpu_custom_call" | custom-call | flops 1 | bytes 1 | tf_op jit(solution)/shard_map/local_part/pallas_call | solution.py:228
  379.9 3.0 close_part.8
  382.9 3.4 close_part.9
  386.2 3.0 close_part.10
  389.2 32.2 %collective-permute-done.7.term_ref = f32[5,8,64,128]{3,2,1,0:T(8,128)S(1)} collective-permute-done((f32[5,8,64,128]{3,2,1,0:T(8,128)}, f32[5,8,64,128]{3,2,1,0:T(8,128)S(1)}, u32[]{:S(2)}, u32[]{:S(2)}) %collective-permute-start.7) | collective-permute-done | bytes 1310752 | tf_op jit(solution)/shard_map/ppermute | solution.py:21
  421.4 2.9 close_part.11
  424.3 3.0 close_part.12
  427.3 3.0 close_part.13
  430.3 3.0 close_part.14
  433.3 43.6 %collective-permute-done.11.term_ref = f32[5,8,64,128]{3,2,1,0:T(8,128)S(1)} collective-permute-done((f32[5,8,64,128]{3,2,1,0:T(8,128)}, f32[5,8,64,128]{3,2,1,0:T(8,128)S(1)}, u32[]{:S(2)}, u32[]{:S(2)}) %collective-permute-start.11) | collective-permute-done | bytes 1310752 | tf_op jit(solution)/shard_map/ppermute | solution.py:21
  476.9 2.9 close_part.15
  (37 shorter events, 0.4 us)
Async XLA Ops:
  7.2 216.7 %all-gather.3.cloned.1.call-start = ((), (), s32[]{:S(2)}) async-start(), calls=%async_computation.1 | async-start | bytes 2949120 | tf_op jit(solution)/shard_map/all_gather | solution.py:418
  10.8 180.8 %collective-permute-start.2 = (f32[5,16,64,128]{3,2,1,0:T(8,128)}, f32[5,16,64,128]{3,2,1,0:T(8,128)S(1)}, u32[]{:S(2)}, u32[]{:S(2)}) collective-permute-start(f32[5,16,64,128]{3,2,1,0:T(8,128)} %constant_dynamic-slice_fusion.5), channel_id=1, source_target_pairs={{0,24},{8,0},{16,8},{24,16},{1,25},{9,1},{17,9},{25,17},{2,26},{10... | collective-permute-start | bytes 7864328 | tf_op jit(solution)/shard_map/ppermute | solution.py:21
  19.4 172.2 %collective-permute-start.3 = (f32[5,16,64,128]{3,2,1,0:T(8,128)}, f32[5,16,64,128]{3,2,1,0:T(8,128)}, u32[]{:S(2)}, u32[]{:S(2)}) collective-permute-start(f32[5,16,64,128]{3,2,1,0:T(8,128)} %constant_dynamic-slice_fusion.4), channel_id=1, source_target_pairs={{0,8},{8,16},{16,24},{24,0},{1,9},{9,17},{17,25},{25,1},{2,10},{10... | collective-permute-start | bytes 7864328 | tf_op jit(solution)/shard_map/ppermute | solution.py:21
  21.9 19.5 %slice-start = ((f32[1,3,128,128]{3,2,1,0:T(8,128)}), f32[1,1,128,128]{3,2,1,0:T(8,128)S(1)}, s32[]{:S(2)}) async-start(f32[1,3,128,128]{3,2,1,0:T(8,128)} %param.10), calls=%async_computation.2 | async-start | bytes 131072 | tf_op jit(solution)/shard_map/slice | solution.py:292
  21.9 169.6 %collective-permute-start.4 = (f32[5,8,64,128]{3,2,1,0:T(8,128)}, f32[5,8,64,128]{3,2,1,0:T(8,128)}, u32[]{:S(2)}, u32[]{:S(2)}) collective-permute-start(f32[5,8,64,128]{3,2,1,0:T(8,128)} %constant_dynamic-slice_fusion.3), channel_id=1, source_target_pairs={{0,16},{8,24},{16,0},{24,8},{1,17},{9,25},{17,1},{25,9},{2,18},{10... | collective-permute-start | bytes 3932168 | tf_op jit(solution)/shard_map/ppermute | solution.py:21
  33.3 10.8 %copy-start.6 = (f32[256,256]{1,0:T(8,128)S(1)}, f32[256,256]{1,0:T(8,128)}, u32[]{:S(2)}) copy-start(f32[256,256]{1,0:T(8,128)} %param.11) | copy-start | bytes 786436
  35.9 159.0 %collective-permute-start = (f32[5,32,64,128]{3,2,1,0:T(8,128)}, f32[5,32,64,128]{3,2,1,0:T(8,128)}, u32[]{:S(2)}, u32[]{:S(2)}) collective-permute-start(f32[5,32,64,128]{3,2,1,0:T(8,128)} %get-tuple-element.41), channel_id=1, source_target_pairs={{0,1},{1,2},{2,3},{3,4},{4,5},{5,6},{6,7},{7,0},{8,9},{9,10},{10,1... | collective-permute-start | bytes 15728648 | tf_op jit(solution)/shard_map/ppermute | solution.py:21
  35.9 159.0 %collective-permute-start.1 = (f32[5,32,64,128]{3,2,1,0:T(8,128)}, f32[5,32,64,128]{3,2,1,0:T(8,128)}, u32[]{:S(2)}, u32[]{:S(2)}) collective-permute-start(f32[5,32,64,128]{3,2,1,0:T(8,128)} %get-tuple-element.42), channel_id=1, source_target_pairs={{0,7},{1,0},{2,1},{3,2},{4,3},{5,4},{6,5},{7,6},{8,15},{9,8},{10,9... | collective-permute-start | bytes 15728648 | tf_op jit(solution)/shard_map/ppermute | solution.py:21
  40.4 0.8 copy-start.5
  191.6 3.3 copy-start.4
  191.6 123.0 %collective-permute-start.8 = (f32[5,8,64,128]{3,2,1,0:T(8,128)}, f32[5,8,64,128]{3,2,1,0:T(8,128)}, u32[]{:S(2)}, u32[]{:S(2)}) collective-permute-start(f32[5,8,64,128]{3,2,1,0:T(8,128)} %constant_dynamic-slice_fusion.2), channel_id=1, source_target_pairs={{0,16},{8,24},{16,0},{24,8},{1,17},{9,25},{17,1},{25,9},{2,18},{10... | collective-permute-start | bytes 3932168 | tf_op jit(solution)/shard_map/ppermute | solution.py:21
  194.9 29.0 %copy-start.3 = (f32[5]{0:T(128)S(1)}, f32[5]{0:T(128)}, u32[]{:S(2)}) copy-start(f32[5]{0:T(128)} %gain_ref.3) | copy-start | bytes 64
  205.2 1.2 copy-start.1
  206.3 122.4 %collective-permute-start.5 = (f32[5,8,64,128]{3,2,1,0:T(8,128)}, f32[5,8,64,128]{3,2,1,0:T(8,128)}, u32[]{:S(2)}, u32[]{:S(2)}) collective-permute-start(f32[5,8,64,128]{3,2,1,0:T(8,128)} %get-tuple-element.53), channel_id=1, source_target_pairs={{0,8},{8,16},{16,24},{24,0},{1,9},{9,17},{17,25},{25,1},{2,10},{10... | collective-permute-start | bytes 3932168 | tf_op jit(solution)/shard_map/ppermute | solution.py:21
  208.1 178.2 %collective-permute-start.6 = (f32[5,8,64,128]{3,2,1,0:T(8,128)}, f32[5,8,64,128]{3,2,1,0:T(8,128)S(1)}, u32[]{:S(2)}, u32[]{:S(2)}) collective-permute-start(f32[5,8,64,128]{3,2,1,0:T(8,128)} %get-tuple-element.56), channel_id=1, source_target_pairs={{0,24},{8,0},{16,8},{24,16},{1,25},{9,1},{17,9},{25,17},{2,26},{10... | collective-permute-start | bytes 3932168 | tf_op jit(solution)/shard_map/ppermute | solution.py:21
  210.1 211.3 %collective-permute-start.7 = (f32[5,8,64,128]{3,2,1,0:T(8,128)}, f32[5,8,64,128]{3,2,1,0:T(8,128)S(1)}, u32[]{:S(2)}, u32[]{:S(2)}) collective-permute-start(f32[5,8,64,128]{3,2,1,0:T(8,128)} %get-tuple-element.59), channel_id=1, source_target_pairs={{0,16},{8,24},{16,0},{24,8},{1,17},{9,25},{17,1},{25,9},{2,18},{10... | collective-permute-start | bytes 3932168 | tf_op jit(solution)/shard_map/ppermute | solution.py:21
  223.9 1.7 copy-start
  324.8 102.5 %collective-permute-start.9 = (f32[5,8,64,128]{3,2,1,0:T(8,128)}, f32[5,8,64,128]{3,2,1,0:T(8,128)S(1)}, u32[]{:S(2)}, u32[]{:S(2)}) collective-permute-start(f32[5,8,64,128]{3,2,1,0:T(8,128)} %get-tuple-element.67), channel_id=1, source_target_pairs={{0,8},{8,16},{16,24},{24,0},{1,9},{9,17},{17,25},{25,1},{2,10},{10... | collective-permute-start | bytes 3932168 | tf_op jit(solution)/shard_map/ppermute | solution.py:21
  326.3 104.0 %collective-permute-start.10 = (f32[5,8,64,128]{3,2,1,0:T(8,128)}, f32[5,8,64,128]{3,2,1,0:T(8,128)S(1)}, u32[]{:S(2)}, u32[]{:S(2)}) collective-permute-start(f32[5,8,64,128]{3,2,1,0:T(8,128)} %get-tuple-element.70), channel_id=1, source_target_pairs={{0,24},{8,0},{16,8},{24,16},{1,25},{9,1},{17,9},{25,17},{2,26},{10... | collective-permute-start | bytes 3932168 | tf_op jit(solution)/shard_map/ppermute | solution.py:21
  328.7 51.2 %copy-start.2 = (f32[5,8,64,128]{3,2,1,0:T(8,128)S(1)}, f32[5,8,64,128]{3,2,1,0:T(8,128)}, u32[]{:S(2)}) copy-start(f32[5,8,64,128]{3,2,1,0:T(8,128)} %copy-done.1) | copy-start | bytes 3932164
  328.7 148.2 %collective-permute-start.11 = (f32[5,8,64,128]{3,2,1,0:T(8,128)}, f32[5,8,64,128]{3,2,1,0:T(8,128)S(1)}, u32[]{:S(2)}, u32[]{:S(2)}) collective-permute-start(f32[5,8,64,128]{3,2,1,0:T(8,128)} %get-tuple-element.73), channel_id=1, source_target_pairs={{0,16},{8,24},{16,0},{24,8},{1,17},{9,25},{17,1},{25,9},{2,18},{10... | collective-permute-start | bytes 3932168 | tf_op jit(solution)/shard_map/ppermute | solution.py:21
Sparse Core Ops, SparseCore 0:
  191.7 32.1 all-gather.2

commit v5 on v4

--- a/solution.py
+++ b/solution.py
@@ -332,15 +332,16 @@
         return lax.dynamic_slice_in_dim(source, start, length, 1)
 
     received = [{} for _ in sizes]
-    sent = []
+    sent = [outgoing(conserved, steps[-1], 0, sizes[0])]
+    received[0][steps[-1]] = shift(sent[0], "py", -steps[-1])
     for s in steps[:-1]:
-        sent.append(outgoing(after(conserved, *sent) if sent else conserved, s, 0, group))
+        sent.append(outgoing(after(conserved, *sent), s, 0, group))
         arrived = shift(sent[-1], "py", -s)
         for part in received:
             part[s] = arrived
-    for c in range(len(sizes)):
+    for c in range(1, len(sizes)):
         sent.append(outgoing(after(conserved, *sent), steps[-1], offsets[c], sizes[c]))
-        piece = after(sent[-1], received[0][steps[0]]) if c else sent[-1]
+        piece = after(sent[-1], received[0][steps[0]])
         received[c][steps[-1]] = shift(piece, "py", -steps[-1])
     head, tail = after((conserved[:, :width], conserved[:, span - width :]), *sent)
     halo_after = shift(head, "pz", -1)

time: 488 us -> 486 us (level)
  no operation moved by 1% of the time
where the time goes in v5:
time: 486 us; the launch traced here: 485 us
  Pallas kernels  174 us (36%)
  blocking collectives  136 us (28%)
  waiting for transfers between devices  89.7 us (18%)
  local copies, waits for them, and re-layouts  38.4 us (8%)
  starting transfers between devices  29.4 us (6%)
  between operations  14.3 us (3%)
    all_to_all x1, blocking collectives, local(): lax.all_to_all(jnp.broadcast_to(recycle, (count,) + recycle.shape), 'py',...  136 us
    pallas_call x2, Pallas kernels, inlet_part(): pl.pallas_call(inlet_kernel, out_shape=jax.ShapeDtypeStruct((fields, colu...  88.9 us
    ppermute x12, waiting for transfers between devices, shift(): lax.ppermute(values, axis, [(i, (i + step) % count) for i in range(count)])  75.8 us
    pallas_call x1, Pallas kernels, local_part(): pl.pallas_call(functools.partial(local_kernel, halo), out_shape=[shape, s...  40.7 us
    ppermute x12, starting transfers between devices, shift(): lax.ppermute(values, axis, [(i, (i + step) % count) for i in range(count)])  29.4 us
    pallas_call x8, Pallas kernels, close_part(): pl.pallas_call(close_kernel, out_shape=[shape, shape], grid_spec=pltpu.Pr...  24.1 us
    pallas_call x2, Pallas kernels, wall_part(): pl.pallas_call(functools.partial(wall_kernel, count, fields), out_shape=[...  20.4 us
    all_gather x1, waiting for transfers between devices, local(): lax.all_gather(along, 'pz', axis=0).reshape(across * count, fields, -1, 128)  13.9 us
  transfers between devices with their start and end apart: 13, of which 3 were waited for; matrix products, arithmetic and copies ran while one was open for 7% of the time, Pallas kernels for 35%

profile of v5, /device:TPU:0, one launch (start us, length us, event | category | flops | bytes accessed | tf_op | source)
XLA Modules:
  0.0 484.7 jit_solution(10328720523222452841)
XLA Ops:
  7.2 2.6 constant_dynamic-slice_fusion.5
  9.8 4.0 collective-permute-start.2
  13.9 3.5 constant_dynamic-slice_fusion.4
  17.4 1.3 collective-permute-start.3
  18.8 3.6 constant_dynamic-slice_fusion.3
  22.3 0.7 collective-permute-start.4
  23.0 10.3 %fusion.13 = (f32[5,32,64,128]{3,2,1,0:T(8,128)}, f32[5,32,64,128]{3,2,1,0:T(8,128)}) fusion(f32[5,64,64,128]{3,2,1,0:T(8,128)} %own_ref.3), kind=kLoop, calls=%fused_computation.42 | loop fusion | bytes 20971520 | tf_op jit(solution)/shard_map/slice | solution.py:346
  33.3 2.6 constant_dynamic-slice_fusion.2
  35.9 2.6 collective-permute-start.1
  38.6 1.8 fusion.4
  40.4 0.8 copy-done.5
  41.5 0.1 copy.40
  41.6 1.0 fusion.14
  42.7 0.1 reshape.58
  42.9 0.1 copy.36
  43.0 0.1 copy.37
  43.1 0.1 reshape.60.source_ref
  43.2 0.8 dynamic-slice_bitcast_fusion.5
  44.0 0.1 maximum_maximum_fusion.band_ref
  44.1 0.1 fusion.11
  44.2 0.2 fusion.10.refs_3_.matrix_ref
  44.5 9.5 %slice_reduce_fusion = f32[5,64,64]{2,1,0:T(8,128)S(1)} fusion(f32[5,64,64,128]{3,2,1,0:T(8,128)} %own_ref.3), kind=kLoop, calls=%fused_computation | loop fusion | bytes 163840 | tf_op jit(solution)/shard_map/slice | solution.py:391
  53.9 0.1 reshape_squeeze.3
  54.0 136.4 %all_to_all.5 = f32[4,160,128]{2,1,0:T(8,128)} all-to-all(f32[4,160,128]{2,1,0:T(8,128)S(1)} %broadcast_in_dim.3), channel_id=1, replica_groups=mesh['py'=4,'pz'=8] {'py'}, dimensions={0} | all-to-all | bytes 655360 | tf_op jit(solution)/shard_map/all_to_all | solution.py:392
  190.5 2.5 collective-permute-start.8
  193.0 10.2 %wall_part.2 = (f32[5,8,64,128]{3,2,1,0:T(8,128)S(1)}, f32[5,8,64,128]{3,2,1,0:T(8,128)}, f32[5,8,64,128]{3,2,1,0:T(8,128)}, f32[5,8,64,128]{3,2,1,0:T(8,128)}) custom-call(s32[1]{0:T(128)} %bitcast.3.place_ref, f32[5,64,64,128]{3,2,1,0:T(8,128)} %own_ref.3, f32[5,16,64,128]{3,2,1,0:T(8,128)} %copy-done.4, f32[5,8,64,128]{3,2,1,0:T(8,128)} %collective-permute-done.2.refs_1_, ...), custom_call_target="tpu_custom_call" | custom-call | flops 1 | bytes 1 | tf_op jit(solution)/shard_map/wall_part/pallas_call | solution.py:80
  203.2 1.1 copy-done.1
  204.3 1.8 collective-permute-start.5
  206.0 2.1 collective-permute-start.6
  208.1 13.9 %all-gather.3.cloned.1.call-done = f32[32,160,128]{2,1,0:T(8,128)} async-done(((f32[4,160,128]{2,1,0:T(8,128)}), f32[32,160,128]{2,1,0:T(8,128)}) %all-gather.3.cloned.1.call-update) | async-done | bytes 2621456 | tf_op jit(solution)/shard_map/all_gather | solution.py:419
  222.0 1.7 copy-done
  223.7 35.9 %inlet_part.2.inlet_ref.near_ref = f32[5,64,128]{2,1,0:T(8,128)S(1)} custom-call(f32[32,5,32,128]{3,2,1,0:T(8,128)S(1)} %bitcast.54, s32[1,8192]{1,0:T(1,128)S(1)} %bitcast.57, f32[5]{0:T(128)S(1)} %copy-done.3), custom_call_target="tpu_custom_call" | custom-call | flops 1 | bytes 1 | tf_op jit(solution)/shard_map/inlet_part/pallas_call | solution.py:133
  259.6 53.0 %inlet_part.3.far_ref = f32[5,96,128]{2,1,0:T(8,128)S(1)} custom-call(f32[32,5,32,128]{3,2,1,0:T(8,128)S(1)} %bitcast.55, s32[1,12288]{1,0:T(1,128)S(1)} %reshape.60.source_ref, f32[5]{0:T(128)S(1)} %copy-done.3), custom_call_target="tpu_custom_call" | custom-call | flops 1 | bytes 1 | tf_op jit(solution)/shard_map/inlet_part/pallas_call | solution.py:133
  312.7 10.2 %wall_part.3 = (f32[5,8,64,128]{3,2,1,0:T(8,128)S(1)}, f32[5,8,64,128]{3,2,1,0:T(8,128)}, f32[5,8,64,128]{3,2,1,0:T(8,128)}, f32[5,8,64,128]{3,2,1,0:T(8,128)}) custom-call(s32[1]{0:T(128)} %bitcast.3.place_ref, f32[5,64,64,128]{3,2,1,0:T(8,128)} %own_ref.3, f32[5,16,64,128]{3,2,1,0:T(8,128)} %copy-done.4, f32[5,8,64,128]{3,2,1,0:T(8,128)} %collective-permute-done.8.refs_1_, ...), custom_call_target="tpu_custom_call" | custom-call | flops 1 | bytes 1 | tf_op jit(solution)/shard_map/wall_part/pallas_call | solution.py:80
  322.9 1.5 collective-permute-start.9
  324.4 2.3 collective-permute-start.10
  326.7 10.5 %collective-permute-start.11 = (f32[5,8,64,128]{3,2,1,0:T(8,128)}, f32[5,8,64,128]{3,2,1,0:T(8,128)S(1)}, u32[]{:S(2)}, u32[]{:S(2)}) collective-permute-start(f32[5,8,64,128]{3,2,1,0:T(8,128)} %get-tuple-element.73), channel_id=1, source_target_pairs={{0,16},{8,24},{16,0},{24,8},{1,17},{9,25},{17,1},{25,9},{2,18},{10... | collective-permute-start | bytes 3932168 | tf_op jit(solution)/shard_map/ppermute | solution.py:21
  337.3 40.7 %local_part.1 = (f32[5,64,64,128]{3,2,1,0:T(8,128)}, f32[5,64,64,128]{3,2,1,0:T(8,128)}) custom-call(f32[5,64,64,128]{3,2,1,0:T(8,128)} %own_ref.3, f32[5,32,64,128]{3,2,1,0:T(8,128)} %collective-permute-done.before_ref, f32[5,32,64,128]{3,2,1,0:T(8,128)} %collective-permute-done.1.after_ref, f32[5,64,64,128]{3,2,1,0:T(8,128)} %reg_ref.1, ...), custom_call_target="tpu_custom_call" | custom-call | flops 1 | bytes 1 | tf_op jit(solution)/shard_map/local_part/pallas_call | solution.py:228
  378.0 3.0 close_part.8
  380.9 3.4 close_part.9
  384.3 3.0 close_part.10
  387.3 32.8 %collective-permute-done.7.term_ref = f32[5,8,64,128]{3,2,1,0:T(8,128)S(1)} collective-permute-done((f32[5,8,64,128]{3,2,1,0:T(8,128)}, f32[5,8,64,128]{3,2,1,0:T(8,128)S(1)}, u32[]{:S(2)}, u32[]{:S(2)}) %collective-permute-start.7) | collective-permute-done | bytes 1310752 | tf_op jit(solution)/shard_map/ppermute | solution.py:21
  420.1 2.9 close_part.11
  423.0 3.0 close_part.12
  426.0 3.0 close_part.13
  429.0 3.0 close_part.14
  431.9 43.0 %collective-permute-done.11.term_ref = f32[5,8,64,128]{3,2,1,0:T(8,128)S(1)} collective-permute-done((f32[5,8,64,128]{3,2,1,0:T(8,128)}, f32[5,8,64,128]{3,2,1,0:T(8,128)S(1)}, u32[]{:S(2)}, u32[]{:S(2)}) %collective-permute-start.11) | collective-permute-done | bytes 1310752 | tf_op jit(solution)/shard_map/ppermute | solution.py:21
  474.9 2.9 close_part.15
  (37 shorter events, 0.5 us)
Async XLA Ops:
  7.2 214.8 %all-gather.3.cloned.1.call-start = ((), (), s32[]{:S(2)}) async-start(), calls=%async_computation.1 | async-start | bytes 2949120 | tf_op jit(solution)/shard_map/all_gather | solution.py:419
  9.8 180.6 %collective-permute-start.2 = (f32[5,8,64,128]{3,2,1,0:T(8,128)}, f32[5,8,64,128]{3,2,1,0:T(8,128)}, u32[]{:S(2)}, u32[]{:S(2)}) collective-permute-start(f32[5,8,64,128]{3,2,1,0:T(8,128)} %constant_dynamic-slice_fusion.5), channel_id=1, source_target_pairs={{0,16},{8,24},{16,0},{24,8},{1,17},{9,25},{17,1},{25,9},{2,18},{10... | collective-permute-start | bytes 3932168 | tf_op jit(solution)/shard_map/ppermute | solution.py:21
  17.4 173.1 %collective-permute-start.3 = (f32[5,16,64,128]{3,2,1,0:T(8,128)}, f32[5,16,64,128]{3,2,1,0:T(8,128)S(1)}, u32[]{:S(2)}, u32[]{:S(2)}) collective-permute-start(f32[5,16,64,128]{3,2,1,0:T(8,128)} %constant_dynamic-slice_fusion.4), channel_id=1, source_target_pairs={{0,24},{8,0},{16,8},{24,16},{1,25},{9,1},{17,9},{25,17},{2,26},{10... | collective-permute-start | bytes 7864328 | tf_op jit(solution)/shard_map/ppermute | solution.py:21
  22.3 19.2 %slice-start = ((f32[1,3,128,128]{3,2,1,0:T(8,128)}), f32[1,1,128,128]{3,2,1,0:T(8,128)S(1)}, s32[]{:S(2)}) async-start(f32[1,3,128,128]{3,2,1,0:T(8,128)} %param.10), calls=%async_computation.2 | async-start | bytes 131072 | tf_op jit(solution)/shard_map/slice | solution.py:292
  22.3 168.1 %collective-permute-start.4 = (f32[5,16,64,128]{3,2,1,0:T(8,128)}, f32[5,16,64,128]{3,2,1,0:T(8,128)}, u32[]{:S(2)}, u32[]{:S(2)}) collective-permute-start(f32[5,16,64,128]{3,2,1,0:T(8,128)} %constant_dynamic-slice_fusion.3), channel_id=1, source_target_pairs={{0,8},{8,16},{16,24},{24,0},{1,9},{9,17},{17,25},{25,1},{2,10},{10... | collective-permute-start | bytes 7864328 | tf_op jit(solution)/shard_map/ppermute | solution.py:21
  33.3 10.8 %copy-start.6 = (f32[256,256]{1,0:T(8,128)S(1)}, f32[256,256]{1,0:T(8,128)}, u32[]{:S(2)}) copy-start(f32[256,256]{1,0:T(8,128)} %param.11) | copy-start | bytes 786436
  35.9 157.1 %collective-permute-start = (f32[5,32,64,128]{3,2,1,0:T(8,128)}, f32[5,32,64,128]{3,2,1,0:T(8,128)}, u32[]{:S(2)}, u32[]{:S(2)}) collective-permute-start(f32[5,32,64,128]{3,2,1,0:T(8,128)} %get-tuple-element.41), channel_id=1, source_target_pairs={{0,1},{1,2},{2,3},{3,4},{4,5},{5,6},{6,7},{7,0},{8,9},{9,10},{10,1... | collective-permute-start | bytes 15728648 | tf_op jit(solution)/shard_map/ppermute | solution.py:21
  35.9 157.1 %collective-permute-start.1 = (f32[5,32,64,128]{3,2,1,0:T(8,128)}, f32[5,32,64,128]{3,2,1,0:T(8,128)}, u32[]{:S(2)}, u32[]{:S(2)}) collective-permute-start(f32[5,32,64,128]{3,2,1,0:T(8,128)} %get-tuple-element.42), channel_id=1, source_target_pairs={{0,7},{1,0},{2,1},{3,2},{4,3},{5,4},{6,5},{7,6},{8,15},{9,8},{10,9... | collective-permute-start | bytes 15728648 | tf_op jit(solution)/shard_map/ppermute | solution.py:21
  40.4 0.8 copy-start.5
  190.5 2.5 copy-start.4
  190.5 122.2 %collective-permute-start.8 = (f32[5,8,64,128]{3,2,1,0:T(8,128)}, f32[5,8,64,128]{3,2,1,0:T(8,128)}, u32[]{:S(2)}, u32[]{:S(2)}) collective-permute-start(f32[5,8,64,128]{3,2,1,0:T(8,128)} %constant_dynamic-slice_fusion.2), channel_id=1, source_target_pairs={{0,16},{8,24},{16,0},{24,8},{1,17},{9,25},{17,1},{25,9},{2,18},{10... | collective-permute-start | bytes 3932168 | tf_op jit(solution)/shard_map/ppermute | solution.py:21
  193.0 29.0 %copy-start.3 = (f32[5]{0:T(128)S(1)}, f32[5]{0:T(128)}, u32[]{:S(2)}) copy-start(f32[5]{0:T(128)} %gain_ref.3) | copy-start | bytes 64
  203.2 1.1 copy-start.1
  204.3 122.5 %collective-permute-start.5 = (f32[5,8,64,128]{3,2,1,0:T(8,128)}, f32[5,8,64,128]{3,2,1,0:T(8,128)}, u32[]{:S(2)}, u32[]{:S(2)}) collective-permute-start(f32[5,8,64,128]{3,2,1,0:T(8,128)} %get-tuple-element.53), channel_id=1, source_target_pairs={{0,8},{8,16},{16,24},{24,0},{1,9},{9,17},{17,25},{25,1},{2,10},{10... | collective-permute-start | bytes 3932168 | tf_op jit(solution)/shard_map/ppermute | solution.py:21
  206.0 178.3 %collective-permute-start.6 = (f32[5,8,64,128]{3,2,1,0:T(8,128)}, f32[5,8,64,128]{3,2,1,0:T(8,128)S(1)}, u32[]{:S(2)}, u32[]{:S(2)}) collective-permute-start(f32[5,8,64,128]{3,2,1,0:T(8,128)} %get-tuple-element.56), channel_id=1, source_target_pairs={{0,24},{8,0},{16,8},{24,16},{1,25},{9,1},{17,9},{25,17},{2,26},{10... | collective-permute-start | bytes 3932168 | tf_op jit(solution)/shard_map/ppermute | solution.py:21
  208.1 212.0 %collective-permute-start.7 = (f32[5,8,64,128]{3,2,1,0:T(8,128)}, f32[5,8,64,128]{3,2,1,0:T(8,128)S(1)}, u32[]{:S(2)}, u32[]{:S(2)}) collective-permute-start(f32[5,8,64,128]{3,2,1,0:T(8,128)} %get-tuple-element.59), channel_id=1, source_target_pairs={{0,16},{8,24},{16,0},{24,8},{1,17},{9,25},{17,1},{25,9},{2,18},{10... | collective-permute-start | bytes 3932168 | tf_op jit(solution)/shard_map/ppermute | solution.py:21
  222.0 1.7 copy-start
  322.9 103.1 %collective-permute-start.9 = (f32[5,8,64,128]{3,2,1,0:T(8,128)}, f32[5,8,64,128]{3,2,1,0:T(8,128)S(1)}, u32[]{:S(2)}, u32[]{:S(2)}) collective-permute-start(f32[5,8,64,128]{3,2,1,0:T(8,128)} %get-tuple-element.67), channel_id=1, source_target_pairs={{0,8},{8,16},{16,24},{24,0},{1,9},{9,17},{17,25},{25,1},{2,10},{10... | collective-permute-start | bytes 3932168 | tf_op jit(solution)/shard_map/ppermute | solution.py:21
  324.4 104.6 %collective-permute-start.10 = (f32[5,8,64,128]{3,2,1,0:T(8,128)}, f32[5,8,64,128]{3,2,1,0:T(8,128)S(1)}, u32[]{:S(2)}, u32[]{:S(2)}) collective-permute-start(f32[5,8,64,128]{3,2,1,0:T(8,128)} %get-tuple-element.70), channel_id=1, source_target_pairs={{0,24},{8,0},{16,8},{24,16},{1,25},{9,1},{17,9},{25,17},{2,26},{10... | collective-permute-start | bytes 3932168 | tf_op jit(solution)/shard_map/ppermute | solution.py:21
  326.7 51.2 %copy-start.2 = (f32[5,8,64,128]{3,2,1,0:T(8,128)S(1)}, f32[5,8,64,128]{3,2,1,0:T(8,128)}, u32[]{:S(2)}) copy-start(f32[5,8,64,128]{3,2,1,0:T(8,128)} %copy-done.1) | copy-start | bytes 3932164
  326.7 148.2 %collective-permute-start.11 = (f32[5,8,64,128]{3,2,1,0:T(8,128)}, f32[5,8,64,128]{3,2,1,0:T(8,128)S(1)}, u32[]{:S(2)}, u32[]{:S(2)}) collective-permute-start(f32[5,8,64,128]{3,2,1,0:T(8,128)} %get-tuple-element.73), channel_id=1, source_target_pairs={{0,16},{8,24},{16,0},{24,8},{1,17},{9,25},{17,1},{25,9},{2,18},{10... | collective-permute-start | bytes 3932168 | tf_op jit(solution)/shard_map/ppermute | solution.py:21
Sparse Core Ops, SparseCore 0:
  190.6 31.2 all-gather.2

commit v6 on v5

--- a/solution.py
+++ b/solution.py
@@ -243,9 +243,9 @@
         ],
         out_specs=[main, main],
         scratch_shapes=[
-            pltpu.VMEM((cells // 128, fields * wide * tile, 128), jnp.float32),
+            pltpu.VMEM((cells // 128, fields * wide * tile + tile, 128), jnp.float32),
             pltpu.VMEM((fields * span * tile, cells), jnp.float32),
-            pltpu.VMEM((cells // 128, fields * span * tile, 128), jnp.float32),
+            pltpu.VMEM((cells // 128, fields * span * tile + tile, 128), jnp.float32),
         ],
         compiler_params=pltpu.CompilerParams(vmem_limit_bytes=vmem_limit),
         cost_estimate=small_cost,

time: 486 us -> 486 us (level)
  no operation moved by 1% of the time
where the time goes in v6:
time: 486 us; the launch traced here: 485 us
  Pallas kernels  174 us (36%)
  blocking collectives  136 us (28%)
  waiting for transfers between devices  89.7 us (18%)
  local copies, waits for them, and re-layouts  38.4 us (8%)
  starting transfers between devices  29.4 us (6%)
  between operations  14.3 us (3%)
    all_to_all x1, blocking collectives, local(): lax.all_to_all(jnp.broadcast_to(recycle, (count,) + recycle.shape), 'py',...  136 us
    pallas_call x2, Pallas kernels, inlet_part(): pl.pallas_call(inlet_kernel, out_shape=jax.ShapeDtypeStruct((fields, colu...  88.9 us
    ppermute x12, waiting for transfers between devices, shift(): lax.ppermute(values, axis, [(i, (i + step) % count) for i in range(count)])  75.8 us
    pallas_call x1, Pallas kernels, local_part(): pl.pallas_call(functools.partial(local_kernel, halo), out_shape=[shape, s...  40.7 us
    ppermute x12, starting transfers between devices, shift(): lax.ppermute(values, axis, [(i, (i + step) % count) for i in range(count)])  29.4 us
    pallas_call x8, Pallas kernels, close_part(): pl.pallas_call(close_kernel, out_shape=[shape, shape], grid_spec=pltpu.Pr...  24.1 us
    pallas_call x2, Pallas kernels, wall_part(): pl.pallas_call(functools.partial(wall_kernel, count, fields), out_shape=[...  20.4 us
    all_gather x1, waiting for transfers between devices, local(): lax.all_gather(along, 'pz', axis=0).reshape(across * count, fields, -1, 128)  13.9 us
  transfers between devices with their start and end apart: 13, of which 3 were waited for; matrix products, arithmetic and copies ran while one was open for 7% of the time, Pallas kernels for 35%

profile of v6, /device:TPU:0, one launch (start us, length us, event | category | flops | bytes accessed | tf_op | source)
XLA Modules:
  0.0 484.7 jit_solution(17458032251058287062)
XLA Ops:
  7.2 2.6 constant_dynamic-slice_fusion.5
  9.8 4.0 collective-permute-start.2
  13.9 3.5 constant_dynamic-slice_fusion.4
  17.4 1.3 collective-permute-start.3
  18.8 3.6 constant_dynamic-slice_fusion.3
  22.3 0.7 collective-permute-start.4
  23.0 10.3 %fusion.13 = (f32[5,32,64,128]{3,2,1,0:T(8,128)}, f32[5,32,64,128]{3,2,1,0:T(8,128)}) fusion(f32[5,64,64,128]{3,2,1,0:T(8,128)} %own_ref.3), kind=kLoop, calls=%fused_computation.42 | loop fusion | bytes 20971520 | tf_op jit(solution)/shard_map/slice | solution.py:346
  33.3 2.6 constant_dynamic-slice_fusion.2
  35.9 2.6 collective-permute-start.1
  38.6 1.8 fusion.4
  40.4 0.8 copy-done.5
  41.5 0.1 copy.40
  41.6 1.0 fusion.14
  42.7 0.1 reshape.58
  42.9 0.1 copy.36
  43.0 0.1 copy.37
  43.1 0.1 reshape.60.source_ref
  43.2 0.8 dynamic-slice_bitcast_fusion.5
  44.0 0.1 maximum_maximum_fusion.band_ref
  44.1 0.1 fusion.11
  44.2 0.2 fusion.10.refs_3_.matrix_ref
  44.5 9.5 %slice_reduce_fusion = f32[5,64,64]{2,1,0:T(8,128)S(1)} fusion(f32[5,64,64,128]{3,2,1,0:T(8,128)} %own_ref.3), kind=kLoop, calls=%fused_computation | loop fusion | bytes 163840 | tf_op jit(solution)/shard_map/slice | solution.py:391
  53.9 0.1 reshape_squeeze.3
  54.0 136.4 %all_to_all.5 = f32[4,160,128]{2,1,0:T(8,128)} all-to-all(f32[4,160,128]{2,1,0:T(8,128)S(1)} %broadcast_in_dim.3), channel_id=1, replica_groups=mesh['py'=4,'pz'=8] {'py'}, dimensions={0} | all-to-all | bytes 655360 | tf_op jit(solution)/shard_map/all_to_all | solution.py:392
  190.5 2.5 collective-permute-start.8
  193.0 10.2 %wall_part.2 = (f32[5,8,64,128]{3,2,1,0:T(8,128)S(1)}, f32[5,8,64,128]{3,2,1,0:T(8,128)}, f32[5,8,64,128]{3,2,1,0:T(8,128)}, f32[5,8,64,128]{3,2,1,0:T(8,128)}) custom-call(s32[1]{0:T(128)} %bitcast.3.place_ref, f32[5,64,64,128]{3,2,1,0:T(8,128)} %own_ref.3, f32[5,16,64,128]{3,2,1,0:T(8,128)} %copy-done.4, f32[5,8,64,128]{3,2,1,0:T(8,128)} %collective-permute-done.2.refs_1_, ...), custom_call_target="tpu_custom_call" | custom-call | flops 1 | bytes 1 | tf_op jit(solution)/shard_map/wall_part/pallas_call | solution.py:80
  203.2 1.1 copy-done.1
  204.3 1.8 collective-permute-start.5
  206.0 2.1 collective-permute-start.6
  208.1 13.9 %all-gather.3.cloned.1.call-done = f32[32,160,128]{2,1,0:T(8,128)} async-done(((f32[4,160,128]{2,1,0:T(8,128)}), f32[32,160,128]{2,1,0:T(8,128)}) %all-gather.3.cloned.1.call-update) | async-done | bytes 2621456 | tf_op jit(solution)/shard_map/all_gather | solution.py:419
  222.0 1.7 copy-done
  223.7 35.9 %inlet_part.2.inlet_ref.near_ref = f32[5,64,128]{2,1,0:T(8,128)S(1)} custom-call(f32[32,5,32,128]{3,2,1,0:T(8,128)S(1)} %bitcast.54, s32[1,8192]{1,0:T(1,128)S(1)} %bitcast.57, f32[5]{0:T(128)S(1)} %copy-done.3), custom_call_target="tpu_custom_call" | custom-call | flops 1 | bytes 1 | tf_op jit(solution)/shard_map/inlet_part/pallas_call | solution.py:133
  259.6 53.0 %inlet_part.3.far_ref = f32[5,96,128]{2,1,0:T(8,128)S(1)} custom-call(f32[32,5,32,128]{3,2,1,0:T(8,128)S(1)} %bitcast.55, s32[1,12288]{1,0:T(1,128)S(1)} %reshape.60.source_ref, f32[5]{0:T(128)S(1)} %copy-done.3), custom_call_target="tpu_custom_call" | custom-call | flops 1 | bytes 1 | tf_op jit(solution)/shard_map/inlet_part/pallas_call | solution.py:133
  312.7 10.2 %wall_part.3 = (f32[5,8,64,128]{3,2,1,0:T(8,128)S(1)}, f32[5,8,64,128]{3,2,1,0:T(8,128)}, f32[5,8,64,128]{3,2,1,0:T(8,128)}, f32[5,8,64,128]{3,2,1,0:T(8,128)}) custom-call(s32[1]{0:T(128)} %bitcast.3.place_ref, f32[5,64,64,128]{3,2,1,0:T(8,128)} %own_ref.3, f32[5,16,64,128]{3,2,1,0:T(8,128)} %copy-done.4, f32[5,8,64,128]{3,2,1,0:T(8,128)} %collective-permute-done.8.refs_1_, ...), custom_call_target="tpu_custom_call" | custom-call | flops 1 | bytes 1 | tf_op jit(solution)/shard_map/wall_part/pallas_call | solution.py:80
  322.9 1.5 collective-permute-start.9
  324.4 2.3 collective-permute-start.10
  326.7 10.5 %collective-permute-start.11 = (f32[5,8,64,128]{3,2,1,0:T(8,128)}, f32[5,8,64,128]{3,2,1,0:T(8,128)S(1)}, u32[]{:S(2)}, u32[]{:S(2)}) collective-permute-start(f32[5,8,64,128]{3,2,1,0:T(8,128)} %get-tuple-element.73), channel_id=1, source_target_pairs={{0,16},{8,24},{16,0},{24,8},{1,17},{9,25},{17,1},{25,9},{2,18},{10... | collective-permute-start | bytes 3932168 | tf_op jit(solution)/shard_map/ppermute | solution.py:21
  337.3 40.7 %local_part.1 = (f32[5,64,64,128]{3,2,1,0:T(8,128)}, f32[5,64,64,128]{3,2,1,0:T(8,128)}) custom-call(f32[5,64,64,128]{3,2,1,0:T(8,128)} %own_ref.3, f32[5,32,64,128]{3,2,1,0:T(8,128)} %collective-permute-done.before_ref, f32[5,32,64,128]{3,2,1,0:T(8,128)} %collective-permute-done.1.after_ref, f32[5,64,64,128]{3,2,1,0:T(8,128)} %reg_ref.1, ...), custom_call_target="tpu_custom_call" | custom-call | flops 1 | bytes 1 | tf_op jit(solution)/shard_map/local_part/pallas_call | solution.py:228
  378.0 3.0 close_part.8
  380.9 3.4 close_part.9
  384.3 3.0 close_part.10
  387.3 32.8 %collective-permute-done.7.term_ref = f32[5,8,64,128]{3,2,1,0:T(8,128)S(1)} collective-permute-done((f32[5,8,64,128]{3,2,1,0:T(8,128)}, f32[5,8,64,128]{3,2,1,0:T(8,128)S(1)}, u32[]{:S(2)}, u32[]{:S(2)}) %collective-permute-start.7) | collective-permute-done | bytes 1310752 | tf_op jit(solution)/shard_map/ppermute | solution.py:21
  420.1 2.9 close_part.11
  423.0 3.0 close_part.12
  426.0 3.0 close_part.13
  429.0 3.0 close_part.14
  431.9 43.0 %collective-permute-done.11.term_ref = f32[5,8,64,128]{3,2,1,0:T(8,128)S(1)} collective-permute-done((f32[5,8,64,128]{3,2,1,0:T(8,128)}, f32[5,8,64,128]{3,2,1,0:T(8,128)S(1)}, u32[]{:S(2)}, u32[]{:S(2)}) %collective-permute-start.11) | collective-permute-done | bytes 1310752 | tf_op jit(solution)/shard_map/ppermute | solution.py:21
  474.9 2.9 close_part.15
  (37 shorter events, 0.5 us)
Async XLA Ops:
  7.2 214.8 %all-gather.3.cloned.1.call-start = ((), (), s32[]{:S(2)}) async-start(), calls=%async_computation.1 | async-start | bytes 2949120 | tf_op jit(solution)/shard_map/all_gather | solution.py:419
  9.8 180.6 %collective-permute-start.2 = (f32[5,8,64,128]{3,2,1,0:T(8,128)}, f32[5,8,64,128]{3,2,1,0:T(8,128)}, u32[]{:S(2)}, u32[]{:S(2)}) collective-permute-start(f32[5,8,64,128]{3,2,1,0:T(8,128)} %constant_dynamic-slice_fusion.5), channel_id=1, source_target_pairs={{0,16},{8,24},{16,0},{24,8},{1,17},{9,25},{17,1},{25,9},{2,18},{10... | collective-permute-start | bytes 3932168 | tf_op jit(solution)/shard_map/ppermute | solution.py:21
  17.4 173.1 %collective-permute-start.3 = (f32[5,16,64,128]{3,2,1,0:T(8,128)}, f32[5,16,64,128]{3,2,1,0:T(8,128)S(1)}, u32[]{:S(2)}, u32[]{:S(2)}) collective-permute-start(f32[5,16,64,128]{3,2,1,0:T(8,128)} %constant_dynamic-slice_fusion.4), channel_id=1, source_target_pairs={{0,24},{8,0},{16,8},{24,16},{1,25},{9,1},{17,9},{25,17},{2,26},{10... | collective-permute-start | bytes 7864328 | tf_op jit(solution)/shard_map/ppermute | solution.py:21
  22.3 19.2 %slice-start = ((f32[1,3,128,128]{3,2,1,0:T(8,128)}), f32[1,1,128,128]{3,2,1,0:T(8,128)S(1)}, s32[]{:S(2)}) async-start(f32[1,3,128,128]{3,2,1,0:T(8,128)} %param.10), calls=%async_computation.2 | async-start | bytes 131072 | tf_op jit(solution)/shard_map/slice | solution.py:292
  22.3 168.1 %collective-permute-start.4 = (f32[5,16,64,128]{3,2,1,0:T(8,128)}, f32[5,16,64,128]{3,2,1,0:T(8,128)}, u32[]{:S(2)}, u32[]{:S(2)}) collective-permute-start(f32[5,16,64,128]{3,2,1,0:T(8,128)} %constant_dynamic-slice_fusion.3), channel_id=1, source_target_pairs={{0,8},{8,16},{16,24},{24,0},{1,9},{9,17},{17,25},{25,1},{2,10},{10... | collective-permute-start | bytes 7864328 | tf_op jit(solution)/shard_map/ppermute | solution.py:21
  33.3 10.8 %copy-start.6 = (f32[256,256]{1,0:T(8,128)S(1)}, f32[256,256]{1,0:T(8,128)}, u32[]{:S(2)}) copy-start(f32[256,256]{1,0:T(8,128)} %param.11) | copy-start | bytes 786436
  35.9 157.1 %collective-permute-start = (f32[5,32,64,128]{3,2,1,0:T(8,128)}, f32[5,32,64,128]{3,2,1,0:T(8,128)}, u32[]{:S(2)}, u32[]{:S(2)}) collective-permute-start(f32[5,32,64,128]{3,2,1,0:T(8,128)} %get-tuple-element.41), channel_id=1, source_target_pairs={{0,1},{1,2},{2,3},{3,4},{4,5},{5,6},{6,7},{7,0},{8,9},{9,10},{10,1... | collective-permute-start | bytes 15728648 | tf_op jit(solution)/shard_map/ppermute | solution.py:21
  35.9 157.1 %collective-permute-start.1 = (f32[5,32,64,128]{3,2,1,0:T(8,128)}, f32[5,32,64,128]{3,2,1,0:T(8,128)}, u32[]{:S(2)}, u32[]{:S(2)}) collective-permute-start(f32[5,32,64,128]{3,2,1,0:T(8,128)} %get-tuple-element.42), channel_id=1, source_target_pairs={{0,7},{1,0},{2,1},{3,2},{4,3},{5,4},{6,5},{7,6},{8,15},{9,8},{10,9... | collective-permute-start | bytes 15728648 | tf_op jit(solution)/shard_map/ppermute | solution.py:21
  40.4 0.8 copy-start.5
  190.5 2.5 copy-start.4
  190.5 122.2 %collective-permute-start.8 = (f32[5,8,64,128]{3,2,1,0:T(8,128)}, f32[5,8,64,128]{3,2,1,0:T(8,128)}, u32[]{:S(2)}, u32[]{:S(2)}) collective-permute-start(f32[5,8,64,128]{3,2,1,0:T(8,128)} %constant_dynamic-slice_fusion.2), channel_id=1, source_target_pairs={{0,16},{8,24},{16,0},{24,8},{1,17},{9,25},{17,1},{25,9},{2,18},{10... | collective-permute-start | bytes 3932168 | tf_op jit(solution)/shard_map/ppermute | solution.py:21
  193.0 29.0 %copy-start.3 = (f32[5]{0:T(128)S(1)}, f32[5]{0:T(128)}, u32[]{:S(2)}) copy-start(f32[5]{0:T(128)} %gain_ref.3) | copy-start | bytes 64
  203.2 1.1 copy-start.1
  204.3 122.5 %collective-permute-start.5 = (f32[5,8,64,128]{3,2,1,0:T(8,128)}, f32[5,8,64,128]{3,2,1,0:T(8,128)}, u32[]{:S(2)}, u32[]{:S(2)}) collective-permute-start(f32[5,8,64,128]{3,2,1,0:T(8,128)} %get-tuple-element.53), channel_id=1, source_target_pairs={{0,8},{8,16},{16,24},{24,0},{1,9},{9,17},{17,25},{25,1},{2,10},{10... | collective-permute-start | bytes 3932168 | tf_op jit(solution)/shard_map/ppermute | solution.py:21
  206.0 178.3 %collective-permute-start.6 = (f32[5,8,64,128]{3,2,1,0:T(8,128)}, f32[5,8,64,128]{3,2,1,0:T(8,128)S(1)}, u32[]{:S(2)}, u32[]{:S(2)}) collective-permute-start(f32[5,8,64,128]{3,2,1,0:T(8,128)} %get-tuple-element.56), channel_id=1, source_target_pairs={{0,24},{8,0},{16,8},{24,16},{1,25},{9,1},{17,9},{25,17},{2,26},{10... | collective-permute-start | bytes 3932168 | tf_op jit(solution)/shard_map/ppermute | solution.py:21
  208.1 212.0 %collective-permute-start.7 = (f32[5,8,64,128]{3,2,1,0:T(8,128)}, f32[5,8,64,128]{3,2,1,0:T(8,128)S(1)}, u32[]{:S(2)}, u32[]{:S(2)}) collective-permute-start(f32[5,8,64,128]{3,2,1,0:T(8,128)} %get-tuple-element.59), channel_id=1, source_target_pairs={{0,16},{8,24},{16,0},{24,8},{1,17},{9,25},{17,1},{25,9},{2,18},{10... | collective-permute-start | bytes 3932168 | tf_op jit(solution)/shard_map/ppermute | solution.py:21
  222.0 1.7 copy-start
  322.9 103.1 %collective-permute-start.9 = (f32[5,8,64,128]{3,2,1,0:T(8,128)}, f32[5,8,64,128]{3,2,1,0:T(8,128)S(1)}, u32[]{:S(2)}, u32[]{:S(2)}) collective-permute-start(f32[5,8,64,128]{3,2,1,0:T(8,128)} %get-tuple-element.67), channel_id=1, source_target_pairs={{0,8},{8,16},{16,24},{24,0},{1,9},{9,17},{17,25},{25,1},{2,10},{10... | collective-permute-start | bytes 3932168 | tf_op jit(solution)/shard_map/ppermute | solution.py:21
  324.4 104.6 %collective-permute-start.10 = (f32[5,8,64,128]{3,2,1,0:T(8,128)}, f32[5,8,64,128]{3,2,1,0:T(8,128)S(1)}, u32[]{:S(2)}, u32[]{:S(2)}) collective-permute-start(f32[5,8,64,128]{3,2,1,0:T(8,128)} %get-tuple-element.70), channel_id=1, source_target_pairs={{0,24},{8,0},{16,8},{24,16},{1,25},{9,1},{17,9},{25,17},{2,26},{10... | collective-permute-start | bytes 3932168 | tf_op jit(solution)/shard_map/ppermute | solution.py:21
  326.7 51.2 %copy-start.2 = (f32[5,8,64,128]{3,2,1,0:T(8,128)S(1)}, f32[5,8,64,128]{3,2,1,0:T(8,128)}, u32[]{:S(2)}) copy-start(f32[5,8,64,128]{3,2,1,0:T(8,128)} %copy-done.1) | copy-start | bytes 3932164
  326.7 148.2 %collective-permute-start.11 = (f32[5,8,64,128]{3,2,1,0:T(8,128)}, f32[5,8,64,128]{3,2,1,0:T(8,128)S(1)}, u32[]{:S(2)}, u32[]{:S(2)}) collective-permute-start(f32[5,8,64,128]{3,2,1,0:T(8,128)} %get-tuple-element.73), channel_id=1, source_target_pairs={{0,16},{8,24},{16,0},{24,8},{1,17},{9,25},{17,1},{25,9},{2,18},{10... | collective-permute-start | bytes 3932168 | tf_op jit(solution)/shard_map/ppermute | solution.py:21
Sparse Core Ops, SparseCore 0:
  190.6 31.2 all-gather.2

commit v7 on v6

--- a/solution.py
+++ b/solution.py
@@ -262,7 +262,7 @@
 
 def close_part(place, current, partial, term, group, offset):
     fields, part, rows, cells = term.shape
-    step = math.gcd(math.gcd(part, 4), math.gcd(group, offset))
+    step = math.gcd(math.gcd(part, 2), math.gcd(group, offset))
     block = (fields, step, rows, cells)
     there = pl.BlockSpec(
         block, lambda i, place: (0, (place[0] * group + offset) // step + i, 0, 0)

time: 486 us -> 487 us (level)
  Pallas kernels: 174 us -> 183 us
  waiting for transfers between devices: 89.7 us -> 82.2 us
    pallas_call x8, Pallas kernels: 24.1 us -> 32.6 us  [close_part(): pl.pallas_call(close_kernel, out_shape=[shape, shape], grid_spec=pltpu.Pr...]
    ppermute x12, waiting for transfers between devices: 75.8 us -> 68.4 us  [shift(): lax.ppermute(values, axis, [(i, (i + step) % count) for i in range(count)])]
  transfers between devices with their start and end apart: 13 -> 13, of which waited for: 3 -> 3; matrix products, arithmetic and copies ran while one was open for 7% -> 7% of each run, Pallas kernels for 35% -> 37%
where the time goes in v7:
time: 487 us; the launch traced here: 486 us
  Pallas kernels  183 us (38%)
  blocking collectives  136 us (28%)
  waiting for transfers between devices  82.2 us (17%)
  local copies, waits for them, and re-layouts  38.4 us (8%)
  starting transfers between devices  29.4 us (6%)
  between operations  14.3 us (3%)
    all_to_all x1, blocking collectives, local(): lax.all_to_all(jnp.broadcast_to(recycle, (count,) + recycle.shape), 'py',...  136 us
    pallas_call x2, Pallas kernels, inlet_part(): pl.pallas_call(inlet_kernel, out_shape=jax.ShapeDtypeStruct((fields, colu...  88.9 us
    ppermute x12, waiting for transfers between devices, shift(): lax.ppermute(values, axis, [(i, (i + step) % count) for i in range(count)])  68.4 us
    pallas_call x1, Pallas kernels, local_part(): pl.pallas_call(functools.partial(local_kernel, halo), out_shape=[shape, s...  40.7 us
    pallas_call x8, Pallas kernels, close_part(): pl.pallas_call(close_kernel, out_shape=[shape, shape], grid_spec=pltpu.Pr...  32.6 us
    ppermute x12, starting transfers between devices, shift(): lax.ppermute(values, axis, [(i, (i + step) % count) for i in range(count)])  29.4 us
    pallas_call x2, Pallas kernels, wall_part(): pl.pallas_call(functools.partial(wall_kernel, count, fields), out_shape=[...  20.4 us
    all_gather x1, waiting for transfers between devices, local(): lax.all_gather(along, 'pz', axis=0).reshape(across * count, fields, -1, 128)  13.9 us
  transfers between devices with their start and end apart: 13, of which 3 were waited for; matrix products, arithmetic and copies ran while one was open for 7% of the time, Pallas kernels for 37%

profile of v7, /device:TPU:0, one launch (start us, length us, event | category | flops | bytes accessed | tf_op | source)
XLA Modules:
  0.0 485.8 jit_solution(9267464883856699778)
XLA Ops:
  7.2 2.6 constant_dynamic-slice_fusion.5
  9.8 4.0 collective-permute-start.2
  13.9 3.5 constant_dynamic-slice_fusion.4
  17.4 1.3 collective-permute-start.3
  18.8 3.6 constant_dynamic-slice_fusion.3
  22.3 0.7 collective-permute-start.4
  23.0 10.3 %fusion.13 = (f32[5,32,64,128]{3,2,1,0:T(8,128)}, f32[5,32,64,128]{3,2,1,0:T(8,128)}) fusion(f32[5,64,64,128]{3,2,1,0:T(8,128)} %own_ref.3), kind=kLoop, calls=%fused_computation.42 | loop fusion | bytes 20971520 | tf_op jit(solution)/shard_map/slice | solution.py:346
  33.3 2.6 constant_dynamic-slice_fusion.2
  35.9 2.6 collective-permute-start.1
  38.6 1.8 fusion.4
  40.4 0.8 copy-done.5
  41.5 0.1 copy.40
  41.6 1.0 fusion.14
  42.7 0.1 reshape.58
  42.9 0.1 copy.36
  43.0 0.1 copy.37
  43.1 0.1 reshape.60.source_ref
  43.2 0.8 dynamic-slice_bitcast_fusion.5
  44.0 0.1 maximum_maximum_fusion.band_ref
  44.1 0.1 fusion.11
  44.2 0.2 fusion.10.refs_3_.matrix_ref
  44.5 9.5 %slice_reduce_fusion = f32[5,64,64]{2,1,0:T(8,128)S(1)} fusion(f32[5,64,64,128]{3,2,1,0:T(8,128)} %own_ref.3), kind=kLoop, calls=%fused_computation | loop fusion | bytes 163840 | tf_op jit(solution)/shard_map/slice | solution.py:391
  53.9 0.1 reshape_squeeze.3
  54.0 136.4 %all_to_all.5 = f32[4,160,128]{2,1,0:T(8,128)} all-to-all(f32[4,160,128]{2,1,0:T(8,128)S(1)} %broadcast_in_dim.3), channel_id=1, replica_groups=mesh['py'=4,'pz'=8] {'py'}, dimensions={0} | all-to-all | bytes 655360 | tf_op jit(solution)/shard_map/all_to_all | solution.py:392
  190.5 2.5 collective-permute-start.8
  193.0 10.2 %wall_part.2 = (f32[5,8,64,128]{3,2,1,0:T(8,128)S(1)}, f32[5,8,64,128]{3,2,1,0:T(8,128)}, f32[5,8,64,128]{3,2,1,0:T(8,128)}, f32[5,8,64,128]{3,2,1,0:T(8,128)}) custom-call(s32[1]{0:T(128)} %bitcast.3.place_ref, f32[5,64,64,128]{3,2,1,0:T(8,128)} %own_ref.3, f32[5,16,64,128]{3,2,1,0:T(8,128)} %copy-done.4, f32[5,8,64,128]{3,2,1,0:T(8,128)} %collective-permute-done.2.refs_1_, ...), custom_call_target="tpu_custom_call" | custom-call | flops 1 | bytes 1 | tf_op jit(solution)/shard_map/wall_part/pallas_call | solution.py:80
  203.2 1.1 copy-done.1
  204.3 1.8 collective-permute-start.5
  206.0 2.1 collective-permute-start.6
  208.1 13.9 %all-gather.3.cloned.1.call-done = f32[32,160,128]{2,1,0:T(8,128)} async-done(((f32[4,160,128]{2,1,0:T(8,128)}), f32[32,160,128]{2,1,0:T(8,128)}) %all-gather.3.cloned.1.call-update) | async-done | bytes 2621456 | tf_op jit(solution)/shard_map/all_gather | solution.py:419
  222.0 1.7 copy-done
  223.7 35.9 %inlet_part.2.inlet_ref.near_ref = f32[5,64,128]{2,1,0:T(8,128)S(1)} custom-call(f32[32,5,32,128]{3,2,1,0:T(8,128)S(1)} %bitcast.54, s32[1,8192]{1,0:T(1,128)S(1)} %bitcast.57, f32[5]{0:T(128)S(1)} %copy-done.3), custom_call_target="tpu_custom_call" | custom-call | flops 1 | bytes 1 | tf_op jit(solution)/shard_map/inlet_part/pallas_call | solution.py:133
  259.6 53.0 %inlet_part.3.far_ref = f32[5,96,128]{2,1,0:T(8,128)S(1)} custom-call(f32[32,5,32,128]{3,2,1,0:T(8,128)S(1)} %bitcast.55, s32[1,12288]{1,0:T(1,128)S(1)} %reshape.60.source_ref, f32[5]{0:T(128)S(1)} %copy-done.3), custom_call_target="tpu_custom_call" | custom-call | flops 1 | bytes 1 | tf_op jit(solution)/shard_map/inlet_part/pallas_call | solution.py:133
  312.7 10.2 %wall_part.3 = (f32[5,8,64,128]{3,2,1,0:T(8,128)S(1)}, f32[5,8,64,128]{3,2,1,0:T(8,128)}, f32[5,8,64,128]{3,2,1,0:T(8,128)}, f32[5,8,64,128]{3,2,1,0:T(8,128)}) custom-call(s32[1]{0:T(128)} %bitcast.3.place_ref, f32[5,64,64,128]{3,2,1,0:T(8,128)} %own_ref.3, f32[5,16,64,128]{3,2,1,0:T(8,128)} %copy-done.4, f32[5,8,64,128]{3,2,1,0:T(8,128)} %collective-permute-done.8.refs_1_, ...), custom_call_target="tpu_custom_call" | custom-call | flops 1 | bytes 1 | tf_op jit(solution)/shard_map/wall_part/pallas_call | solution.py:80
  322.9 1.5 collective-permute-start.9
  324.4 2.3 collective-permute-start.10
  326.7 10.5 %collective-permute-start.11 = (f32[5,8,64,128]{3,2,1,0:T(8,128)}, f32[5,8,64,128]{3,2,1,0:T(8,128)S(1)}, u32[]{:S(2)}, u32[]{:S(2)}) collective-permute-start(f32[5,8,64,128]{3,2,1,0:T(8,128)} %get-tuple-element.73), channel_id=1, source_target_pairs={{0,16},{8,24},{16,0},{24,8},{1,17},{9,25},{17,1},{25,9},{2,18},{10... | collective-permute-start | bytes 3932168 | tf_op jit(solution)/shard_map/ppermute | solution.py:21
  337.3 40.7 %local_part.1 = (f32[5,64,64,128]{3,2,1,0:T(8,128)}, f32[5,64,64,128]{3,2,1,0:T(8,128)}) custom-call(f32[5,64,64,128]{3,2,1,0:T(8,128)} %own_ref.3, f32[5,32,64,128]{3,2,1,0:T(8,128)} %collective-permute-done.before_ref, f32[5,32,64,128]{3,2,1,0:T(8,128)} %collective-permute-done.1.after_ref, f32[5,64,64,128]{3,2,1,0:T(8,128)} %reg_ref.1, ...), custom_call_target="tpu_custom_call" | custom-call | flops 1 | bytes 1 | tf_op jit(solution)/shard_map/local_part/pallas_call | solution.py:228
  378.0 4.1 close_part.8
  382.0 4.3 close_part.9
  386.3 4.1 close_part.10
  390.4 29.7 %collective-permute-done.7.term_ref = f32[5,8,64,128]{3,2,1,0:T(8,128)S(1)} collective-permute-done((f32[5,8,64,128]{3,2,1,0:T(8,128)}, f32[5,8,64,128]{3,2,1,0:T(8,128)S(1)}, u32[]{:S(2)}, u32[]{:S(2)}) %collective-permute-start.7) | collective-permute-done | bytes 1310752 | tf_op jit(solution)/shard_map/ppermute | solution.py:21
  420.1 4.0 close_part.11
  424.1 4.1 close_part.12
  428.2 4.1 close_part.13
  432.2 4.1 close_part.14
  436.3 38.6 %collective-permute-done.11.term_ref = f32[5,8,64,128]{3,2,1,0:T(8,128)S(1)} collective-permute-done((f32[5,8,64,128]{3,2,1,0:T(8,128)}, f32[5,8,64,128]{3,2,1,0:T(8,128)S(1)}, u32[]{:S(2)}, u32[]{:S(2)}) %collective-permute-start.11) | collective-permute-done | bytes 1310752 | tf_op jit(solution)/shard_map/ppermute | solution.py:21
  474.9 4.0 close_part.15
  (37 shorter events, 0.5 us)
Async XLA Ops:
  7.2 214.8 %all-gather.3.cloned.1.call-start = ((), (), s32[]{:S(2)}) async-start(), calls=%async_computation.1 | async-start | bytes 2949120 | tf_op jit(solution)/shard_map/all_gather | solution.py:419
  9.8 180.6 %collective-permute-start.2 = (f32[5,8,64,128]{3,2,1,0:T(8,128)}, f32[5,8,64,128]{3,2,1,0:T(8,128)}, u32[]{:S(2)}, u32[]{:S(2)}) collective-permute-start(f32[5,8,64,128]{3,2,1,0:T(8,128)} %constant_dynamic-slice_fusion.5), channel_id=1, source_target_pairs={{0,16},{8,24},{16,0},{24,8},{1,17},{9,25},{17,1},{25,9},{2,18},{10... | collective-permute-start | bytes 3932168 | tf_op jit(solution)/shard_map/ppermute | solution.py:21
  17.4 173.1 %collective-permute-start.3 = (f32[5,16,64,128]{3,2,1,0:T(8,128)}, f32[5,16,64,128]{3,2,1,0:T(8,128)S(1)}, u32[]{:S(2)}, u32[]{:S(2)}) collective-permute-start(f32[5,16,64,128]{3,2,1,0:T(8,128)} %constant_dynamic-slice_fusion.4), channel_id=1, source_target_pairs={{0,24},{8,0},{16,8},{24,16},{1,25},{9,1},{17,9},{25,17},{2,26},{10... | collective-permute-start | bytes 7864328 | tf_op jit(solution)/shard_map/ppermute | solution.py:21
  22.3 19.2 %slice-start = ((f32[1,3,128,128]{3,2,1,0:T(8,128)}), f32[1,1,128,128]{3,2,1,0:T(8,128)S(1)}, s32[]{:S(2)}) async-start(f32[1,3,128,128]{3,2,1,0:T(8,128)} %param.10), calls=%async_computation.2 | async-start | bytes 131072 | tf_op jit(solution)/shard_map/slice | solution.py:292
  22.3 168.1 %collective-permute-start.4 = (f32[5,16,64,128]{3,2,1,0:T(8,128)}, f32[5,16,64,128]{3,2,1,0:T(8,128)}, u32[]{:S(2)}, u32[]{:S(2)}) collective-permute-start(f32[5,16,64,128]{3,2,1,0:T(8,128)} %constant_dynamic-slice_fusion.3), channel_id=1, source_target_pairs={{0,8},{8,16},{16,24},{24,0},{1,9},{9,17},{17,25},{25,1},{2,10},{10... | collective-permute-start | bytes 7864328 | tf_op jit(solution)/shard_map/ppermute | solution.py:21
  33.3 10.8 %copy-start.6 = (f32[256,256]{1,0:T(8,128)S(1)}, f32[256,256]{1,0:T(8,128)}, u32[]{:S(2)}) copy-start(f32[256,256]{1,0:T(8,128)} %param.11) | copy-start | bytes 786436
  35.9 157.1 %collective-permute-start = (f32[5,32,64,128]{3,2,1,0:T(8,128)}, f32[5,32,64,128]{3,2,1,0:T(8,128)}, u32[]{:S(2)}, u32[]{:S(2)}) collective-permute-start(f32[5,32,64,128]{3,2,1,0:T(8,128)} %get-tuple-element.41), channel_id=1, source_target_pairs={{0,1},{1,2},{2,3},{3,4},{4,5},{5,6},{6,7},{7,0},{8,9},{9,10},{10,1... | collective-permute-start | bytes 15728648 | tf_op jit(solution)/shard_map/ppermute | solution.py:21
  35.9 157.1 %collective-permute-start.1 = (f32[5,32,64,128]{3,2,1,0:T(8,128)}, f32[5,32,64,128]{3,2,1,0:T(8,128)}, u32[]{:S(2)}, u32[]{:S(2)}) collective-permute-start(f32[5,32,64,128]{3,2,1,0:T(8,128)} %get-tuple-element.42), channel_id=1, source_target_pairs={{0,7},{1,0},{2,1},{3,2},{4,3},{5,4},{6,5},{7,6},{8,15},{9,8},{10,9... | collective-permute-start | bytes 15728648 | tf_op jit(solution)/shard_map/ppermute | solution.py:21
  40.4 0.8 copy-start.5
  190.5 2.5 copy-start.4
  190.5 122.2 %collective-permute-start.8 = (f32[5,8,64,128]{3,2,1,0:T(8,128)}, f32[5,8,64,128]{3,2,1,0:T(8,128)}, u32[]{:S(2)}, u32[]{:S(2)}) collective-permute-start(f32[5,8,64,128]{3,2,1,0:T(8,128)} %constant_dynamic-slice_fusion.2), channel_id=1, source_target_pairs={{0,16},{8,24},{16,0},{24,8},{1,17},{9,25},{17,1},{25,9},{2,18},{10... | collective-permute-start | bytes 3932168 | tf_op jit(solution)/shard_map/ppermute | solution.py:21
  193.0 29.0 %copy-start.3 = (f32[5]{0:T(128)S(1)}, f32[5]{0:T(128)}, u32[]{:S(2)}) copy-start(f32[5]{0:T(128)} %gain_ref.3) | copy-start | bytes 64
  203.2 1.1 copy-start.1
  204.3 122.5 %collective-permute-start.5 = (f32[5,8,64,128]{3,2,1,0:T(8,128)}, f32[5,8,64,128]{3,2,1,0:T(8,128)}, u32[]{:S(2)}, u32[]{:S(2)}) collective-permute-start(f32[5,8,64,128]{3,2,1,0:T(8,128)} %get-tuple-element.53), channel_id=1, source_target_pairs={{0,8},{8,16},{16,24},{24,0},{1,9},{9,17},{17,25},{25,1},{2,10},{10... | collective-permute-start | bytes 3932168 | tf_op jit(solution)/shard_map/ppermute | solution.py:21
  206.0 180.3 %collective-permute-start.6 = (f32[5,8,64,128]{3,2,1,0:T(8,128)}, f32[5,8,64,128]{3,2,1,0:T(8,128)S(1)}, u32[]{:S(2)}, u32[]{:S(2)}) collective-permute-start(f32[5,8,64,128]{3,2,1,0:T(8,128)} %get-tuple-element.56), channel_id=1, source_target_pairs={{0,24},{8,0},{16,8},{24,16},{1,25},{9,1},{17,9},{25,17},{2,26},{10... | collective-permute-start | bytes 3932168 | tf_op jit(solution)/shard_map/ppermute | solution.py:21
  208.1 212.0 %collective-permute-start.7 = (f32[5,8,64,128]{3,2,1,0:T(8,128)}, f32[5,8,64,128]{3,2,1,0:T(8,128)S(1)}, u32[]{:S(2)}, u32[]{:S(2)}) collective-permute-start(f32[5,8,64,128]{3,2,1,0:T(8,128)} %get-tuple-element.59), channel_id=1, source_target_pairs={{0,16},{8,24},{16,0},{24,8},{1,17},{9,25},{17,1},{25,9},{2,18},{10... | collective-permute-start | bytes 3932168 | tf_op jit(solution)/shard_map/ppermute | solution.py:21
  222.0 1.7 copy-start
  322.9 105.3 %collective-permute-start.9 = (f32[5,8,64,128]{3,2,1,0:T(8,128)}, f32[5,8,64,128]{3,2,1,0:T(8,128)S(1)}, u32[]{:S(2)}, u32[]{:S(2)}) collective-permute-start(f32[5,8,64,128]{3,2,1,0:T(8,128)} %get-tuple-element.67), channel_id=1, source_target_pairs={{0,8},{8,16},{16,24},{24,0},{1,9},{9,17},{17,25},{25,1},{2,10},{10... | collective-permute-start | bytes 3932168 | tf_op jit(solution)/shard_map/ppermute | solution.py:21
  324.4 107.8 %collective-permute-start.10 = (f32[5,8,64,128]{3,2,1,0:T(8,128)}, f32[5,8,64,128]{3,2,1,0:T(8,128)S(1)}, u32[]{:S(2)}, u32[]{:S(2)}) collective-permute-start(f32[5,8,64,128]{3,2,1,0:T(8,128)} %get-tuple-element.70), channel_id=1, source_target_pairs={{0,24},{8,0},{16,8},{24,16},{1,25},{9,1},{17,9},{25,17},{2,26},{10... | collective-permute-start | bytes 3932168 | tf_op jit(solution)/shard_map/ppermute | solution.py:21
  326.7 51.2 %copy-start.2 = (f32[5,8,64,128]{3,2,1,0:T(8,128)S(1)}, f32[5,8,64,128]{3,2,1,0:T(8,128)}, u32[]{:S(2)}) copy-start(f32[5,8,64,128]{3,2,1,0:T(8,128)} %copy-done.1) | copy-start | bytes 3932164
  326.7 148.2 %collective-permute-start.11 = (f32[5,8,64,128]{3,2,1,0:T(8,128)}, f32[5,8,64,128]{3,2,1,0:T(8,128)S(1)}, u32[]{:S(2)}, u32[]{:S(2)}) collective-permute-start(f32[5,8,64,128]{3,2,1,0:T(8,128)} %get-tuple-element.73), channel_id=1, source_target_pairs={{0,16},{8,24},{16,0},{24,8},{1,17},{9,25},{17,1},{25,9},{2,18},{10... | collective-permute-start | bytes 3932168 | tf_op jit(solution)/shard_map/ppermute | solution.py:21
Sparse Core Ops, SparseCore 0:
  190.6 31.2 all-gather.2
